TPU v7x, 32 devices: a whole 2x2x4 slice. The times are simulated.
32 devices in a mesh: section: 2 (over y), tensor: 4 (over x, core), dp: 4 (over z).
Axes of the slice: x: 2, y: 2, z: 4, core: 2. Of those that a mesh axis runs over, the one named last changes fastest.
Arguments:
- inputs: bfloat16 [2, 2, 4, 729, 1152], P('section', None, 'dp', None, 'tensor'), may hold values from -6 to 6
- norm_gain: float32 [2, 2, 1152], P('section', None, 'tensor'), may hold values from 0.5 to 1.5
- norm_bias: float32 [2, 2, 1152], P('section', None, 'tensor'), may hold values from -1.8 to 1.8
- w_query: bfloat16 [2, 1152, 1152], P('section', None, 'tensor'), may hold values from -0.1875 to 0.1875
- b_query: float32 [2, 1152], P('section', 'tensor'), may hold values from -3 to 3
- w_key: bfloat16 [2, 1152, 1152], P('section', None, 'tensor'), may hold values from -0.1875 to 0.1875
- w_value: bfloat16 [2, 1152, 1152], P('section', None, 'tensor'), may hold values from -0.1875 to 0.1875
- b_value: float32 [2, 1152], P('section', 'tensor'), may hold values from -3 to 3
- w_out: bfloat16 [2, 1152, 1152], P('section', 'tensor'), may hold values from -0.75 to 0.75
- out_bias: float32 [2, 2, 1152], P('section', None, 'tensor'), may hold values from -1.8 to 1.8
- w_up: bfloat16 [2, 1152, 4304], P('section', None, 'tensor'), may hold values from -1 to 1
- b_up: float32 [2, 4304], P('section', 'tensor'), may hold values from -3 to 3
- w_down: bfloat16 [2, 4304, 1152], P('section', 'tensor'), may hold values from -0.09375 to 0.09375
Outputs:
- ends: float32 [2, 2, 4, 729, 1152], P('section', None, 'dp', None, 'tensor')
- grad_norm_gain: float32 [2, 2, 1152], P('section', None, 'tensor')
- grad_norm_bias: float32 [2, 2, 1152], P('section', None, 'tensor')
- grad_query: float32 [2, 1152, 1152], P('section', None, 'tensor')
- grad_b_query: float32 [2, 1152], P('section', 'tensor')
- grad_key: float32 [2, 1152, 1152], P('section', None, 'tensor')
- grad_value: float32 [2, 1152, 1152], P('section', None, 'tensor')
- grad_b_value: float32 [2, 1152], P('section', 'tensor')
- grad_out: float32 [2, 1152, 1152], P('section', 'tensor')
- grad_out_bias: float32 [2, 2, 1152], P('section', None, 'tensor')
- grad_up: float32 [2, 1152, 4304], P('section', None, 'tensor')
- grad_b_up: float32 [2, 4304], P('section', 'tensor')
- grad_down: float32 [2, 4304, 1152], P('section', 'tensor')
All inputs are finite; a program needn't handle non-finite values.
Results may differ from a plain program's by a relative error of at most 0.014.
Values may be sent and summed in bfloat16 or wider, within the bound.
No kernel may reach another device: no remote copies, remote signals or barrier semaphores. Data moves between devices by JAX's collectives and lax.ppermute only.
A program may use at most 256 MiB of HBM per device.

v0:
```python
import jax
import jax.numpy as jnp
from jax import lax
from jax.sharding import PartitionSpec as P

D = 1152
HD = 72


epsilon = 1e-06


def from_behind(block, axis, distance):
    devices = range(lax.axis_size(axis))
    route = [(i - distance, i) for i in devices if i - distance in devices]
    return lax.ppermute(block, axis, route)


def forward_dot(left, right):
    return jnp.dot(left, right, preferred_element_type=jnp.float32)


def right_dot(left, right):
    return lax.dot_general(
        left, right, (((1,), (1,)), ((), ())), preferred_element_type=jnp.float32
    )


def left_dot(left, right):
    return lax.dot_general(
        left, right, (((0,), (0,)), ((), ())), preferred_element_type=jnp.float32
    )


def smooth_gate(values):
    return jax.nn.gelu(values, approximate=True)


def normalize(stream, scale_row, shift_row):
    totals = lax.psum((jnp.sum(stream, 1), jnp.sum(stream * stream, 1)), "tensor")
    center_mean = totals[0] / D
    spread = totals[1] / D - center_mean * center_mean
    inverse = lax.rsqrt(spread + epsilon)
    unit = (stream - center_mean[:, None]) * inverse[:, None]
    return (unit, inverse, (unit * scale_row + shift_row).astype(jnp.bfloat16))


def norm_backward(incoming, unit, inverse, scale_row):
    scale_grad = jnp.sum(incoming * unit, 0)
    shift_grad = jnp.sum(incoming, 0)
    scaled = incoming * scale_row
    totals = lax.psum((jnp.sum(scaled, 1), jnp.sum(scaled * unit, 1)), "tensor")
    result = inverse[:, None] * (scaled - totals[0][:, None] / D - unit * (totals[1][:, None] / D))
    return (result, scale_grad, shift_grad)


def widen(piece):
    return lax.all_gather(piece, "tensor", axis=1, tiled=True)


def collect(partial_value):
    return lax.psum_scatter(partial_value, "tensor", scatter_dimension=1, tiled=True)


def widen_grad(piece):
    return lax.all_gather(piece, "tensor", axis=1, tiled=True)


def collect_grad(partial_value):
    return lax.psum_scatter(partial_value, "tensor", scatter_dimension=1, tiled=True)


def image_forward(triple):
    queries, keys, values = triple
    scores = jnp.einsum("lhe,mhe->hlm", queries, keys, preferred_element_type=jnp.float32) * HD ** (
        -0.5
    )
    highest = jnp.max(scores, -1, keepdims=True)
    weights = jnp.exp(scores - highest)
    total = jnp.sum(weights, -1, keepdims=True)
    probs = (weights / total).astype(jnp.bfloat16)
    mixed = jnp.einsum("hlm,mhe->lhe", probs, values, preferred_element_type=jnp.float32)
    return (mixed.astype(jnp.bfloat16), highest[..., 0] + jnp.log(total[..., 0]))


def image_backward(bundle):
    queries, keys, values, logsum, upstream = bundle
    factor = HD ** (-0.5)
    scores = jnp.einsum("lhe,mhe->hlm", queries, keys, preferred_element_type=jnp.float32) * factor
    probs = jnp.exp(scores - logsum[..., None])
    value_grad = jnp.einsum(
        "hlm,lhe->mhe", probs.astype(jnp.bfloat16), upstream, preferred_element_type=jnp.float32
    )
    prob_grad = jnp.einsum("lhe,mhe->hlm", upstream, values, preferred_element_type=jnp.float32)
    score_grad = probs * (prob_grad - jnp.sum(probs * prob_grad, -1, keepdims=True))
    score_grad = score_grad.astype(jnp.bfloat16)
    query_grad = (
        jnp.einsum("hlm,mhe->lhe", score_grad, keys, preferred_element_type=jnp.float32) * factor
    )
    key_grad = (
        jnp.einsum("hlm,lhe->mhe", score_grad, queries, preferred_element_type=jnp.float32) * factor
    )
    return (
        query_grad.astype(jnp.bfloat16),
        key_grad.astype(jnp.bfloat16),
        value_grad.astype(jnp.bfloat16),
    )


def forward_layer(stream, weights, images, length):
    (
        norm_scale,
        norm_shift,
        query_w,
        query_b,
        key_w,
        value_w,
        value_b,
        out_w,
        out_b,
        up_w,
        up_b,
        down_w,
    ) = weights
    heads = query_w.shape[1] // HD
    split = (images, length, heads, HD)
    unit_one, inverse_one, normed_one = normalize(stream, norm_scale[0], norm_shift[0])
    full_one = widen(normed_one)
    queries = (forward_dot(full_one, query_w) + query_b).astype(jnp.bfloat16)
    keys = forward_dot(full_one, key_w).astype(jnp.bfloat16)
    values = (forward_dot(full_one, value_w) + value_b).astype(jnp.bfloat16)
    mixed, logsum = lax.map(
        image_forward, (queries.reshape(split), keys.reshape(split), values.reshape(split))
    )
    mixed = mixed.reshape(images * length, heads * HD)
    middle = stream + collect(forward_dot(mixed, out_w)) + out_b[0]
    unit_two, inverse_two, normed_two = normalize(middle, norm_scale[1], norm_shift[1])
    full_two = widen(normed_two)
    hidden = forward_dot(full_two, up_w) + up_b
    active = smooth_gate(hidden).astype(jnp.bfloat16)
    result = middle + collect(forward_dot(active, down_w)) + out_b[1]
    saved = (
        unit_one,
        inverse_one,
        full_one,
        queries,
        keys,
        values,
        mixed,
        logsum,
        unit_two,
        inverse_two,
        full_two,
        hidden,
        active,
    )
    return (result, saved)


def backward_layer(upstream, saved, weights, images, length):
    (
        norm_scale,
        norm_shift,
        query_w,
        query_b,
        key_w,
        value_w,
        value_b,
        out_w,
        out_b,
        up_w,
        up_b,
        down_w,
    ) = weights
    (
        unit_one,
        inverse_one,
        full_one,
        queries,
        keys,
        values,
        mixed,
        logsum,
        unit_two,
        inverse_two,
        full_two,
        hidden,
        active,
    ) = saved
    heads = query_w.shape[1] // HD
    split = (images, length, heads, HD)
    upstream_low = upstream.astype(jnp.bfloat16)
    upstream_full = widen_grad(upstream_low)
    active_grad = right_dot(upstream_full, down_w)
    down_grad = left_dot(active, upstream_full)
    down_bias_grad = jnp.sum(upstream_low.astype(jnp.float32), 0)
    _, gate_pull = jax.vjp(smooth_gate, hidden)
    hidden_grad = gate_pull(active_grad)[0].astype(jnp.bfloat16)
    up_grad = left_dot(full_two, hidden_grad)
    up_bias_grad = jnp.sum(hidden_grad.astype(jnp.float32), 0)
    normed_two_grad = collect_grad(right_dot(hidden_grad, up_w))
    middle_part, scale_two, shift_two = norm_backward(
        normed_two_grad, unit_two, inverse_two, norm_scale[1]
    )
    middle_grad = upstream + middle_part
    middle_low = middle_grad.astype(jnp.bfloat16)
    middle_full = widen_grad(middle_low)
    mixed_grad = right_dot(middle_full, out_w).astype(jnp.bfloat16)
    out_grad = left_dot(mixed, middle_full)
    out_bias_grad = jnp.sum(middle_low.astype(jnp.float32), 0)
    query_grad, key_grad, value_grad = lax.map(
        image_backward,
        (
            queries.reshape(split),
            keys.reshape(split),
            values.reshape(split),
            logsum,
            mixed_grad.reshape(split),
        ),
    )
    rows = images * length
    query_grad = query_grad.reshape(rows, heads * HD)
    key_grad = key_grad.reshape(rows, heads * HD)
    value_grad = value_grad.reshape(rows, heads * HD)
    normed_one_grad = collect_grad(
        right_dot(query_grad, query_w) + right_dot(key_grad, key_w) + right_dot(value_grad, value_w)
    )
    stream_part, scale_one, shift_one = norm_backward(
        normed_one_grad, unit_one, inverse_one, norm_scale[0]
    )
    stream_grad = middle_grad + stream_part
    grads = (
        jnp.stack([scale_one, scale_two]),
        jnp.stack([shift_one, shift_two]),
        left_dot(full_one, query_grad),
        jnp.sum(query_grad.astype(jnp.float32), 0),
        left_dot(full_one, key_grad),
        left_dot(full_one, value_grad),
        jnp.sum(value_grad.astype(jnp.float32), 0),
        out_grad,
        jnp.stack([out_bias_grad, down_bias_grad]),
        up_grad,
        up_bias_grad,
        down_grad,
    )
    return (stream_grad, grads)


def place(buffer, slot, flag, value):
    previous = lax.dynamic_index_in_dim(buffer, slot, 0, keepdims=False)
    return lax.dynamic_update_index_in_dim(buffer, jnp.where(flag, value, previous), slot, 0)


def per_device(
    inputs,
    norm_gain,
    norm_bias,
    w_query,
    b_query,
    w_key,
    w_value,
    b_value,
    w_out,
    out_bias,
    w_up,
    b_up,
    w_down,
):
    section_pos = lax.axis_index("section")
    first = section_pos == 0
    micro = inputs.shape[1]
    images = inputs.shape[2]
    length = inputs.shape[3]
    columns = inputs.shape[4]
    rows = images * length
    own = inputs[0].reshape(micro, rows, columns).astype(jnp.float32)
    weights = (
        norm_gain[0],
        norm_bias[0],
        w_query[0],
        b_query[0],
        w_key[0],
        w_value[0],
        b_value[0],
        w_out[0],
        out_bias[0],
        w_up[0],
        b_up[0],
        w_down[0],
    )
    ends_buffer = jnp.zeros((micro, rows, columns), jnp.float32)
    stored_inputs = jnp.zeros((micro, rows, columns), jnp.float32)
    arrived = jnp.zeros((rows, columns), jnp.bfloat16)
    for moment in range(micro + 1):
        batch_pos = moment - section_pos
        usable = (batch_pos >= 0) & (batch_pos < micro)
        slot = jnp.clip(batch_pos, 0, micro - 1)
        stream = jnp.where(first, own[min(moment, micro - 1)], arrived.astype(jnp.float32))
        result, saved = forward_layer(stream, weights, images, length)
        if moment < micro:
            arrived = from_behind(result.astype(jnp.bfloat16), "section", 1)
        ends_buffer = place(ends_buffer, slot, usable & jnp.logical_not(first), result)
        stored_inputs = place(stored_inputs, slot, usable, stream)
    totals = None
    returning = jnp.zeros((rows, columns), jnp.bfloat16)
    for moment in range(micro + 1):
        batch_pos = moment - 1 + section_pos
        usable = (batch_pos >= 0) & (batch_pos < micro)
        slot = jnp.clip(batch_pos, 0, micro - 1)
        upstream = jnp.where(first, returning.astype(jnp.float32), own[min(moment, micro - 1)])
        stream = lax.dynamic_index_in_dim(stored_inputs, slot, 0, keepdims=False)
        _, saved = forward_layer(stream, weights, images, length)
        stream_grad, grads = backward_layer(upstream, saved, weights, images, length)
        masked = tuple((jnp.where(usable, item, jnp.zeros_like(item)) for item in grads))
        if totals is None:
            totals = masked
        else:
            totals = tuple((total + item for total, item in zip(totals, masked)))
        if moment < micro:
            returning = from_behind(stream_grad.astype(jnp.bfloat16), "section", -1)
        ends_buffer = place(ends_buffer, slot, usable & first, stream_grad)
    totals = lax.psum(totals, "dp")
    ends = ends_buffer.reshape(1, micro, images, length, columns)
    return (
        ends,
        totals[0][None],
        totals[1][None],
        totals[2][None],
        totals[3][None],
        totals[4][None],
        totals[5][None],
        totals[6][None],
        totals[7][None],
        totals[8][None],
        totals[9][None],
        totals[10][None],
        totals[11][None],
    )


def solution(mesh):
    in_specs = (
        P("section", None, "dp", None, "tensor"),
        P("section", None, "tensor"),
        P("section", None, "tensor"),
        P("section", None, "tensor"),
        P("section", "tensor"),
        P("section", None, "tensor"),
        P("section", None, "tensor"),
        P("section", "tensor"),
        P("section", "tensor", None),
        P("section", None, "tensor"),
        P("section", None, "tensor"),
        P("section", "tensor"),
        P("section", "tensor", None),
    )
    out_specs = (
        P("section", None, "dp", None, "tensor"),
        P("section", None, "tensor"),
        P("section", None, "tensor"),
        P("section", None, "tensor"),
        P("section", "tensor"),
        P("section", None, "tensor"),
        P("section", None, "tensor"),
        P("section", "tensor"),
        P("section", "tensor", None),
        P("section", None, "tensor"),
        P("section", None, "tensor"),
        P("section", "tensor"),
        P("section", "tensor", None),
    )
    return jax.shard_map(
        per_device, mesh=mesh, in_specs=in_specs, out_specs=out_specs, check_vma=False
    )
```

profile of v0, /device:TPU:0, one launch (start us, length us, event | category | flops | bytes accessed | tf_op | source)
XLA Modules:
  0.0 2051.9 jit_solution(4777992496656342934)
XLA Ops:
  67.2 39.9 %reduce-scatter.16.cloned.1.call-done = f32[729,288]{0,1:T(8,128)} async-done(((f32[729,1152]{0,1:T(8,128)}), f32[729,288]{0,1:T(8,128)}) %reduce-scatter.16.cloned.1.call-update) | async-done | bytes 839824 | tf_op jit(solution)/shard_map/reduce_scatter | solution.py:62
  119.0 21.8 %all-gather.21.cloned.1.call-done = bf16[729,1152]{0,1:T(8,128)(2,1)} async-done(((bf16[729,288]{0,1:T(8,128)(2,1)}), bf16[729,1152]{0,1:T(8,128)(2,1)}) %all-gather.21.cloned.1.call-update) | async-done | bytes 1679632 | tf_op jit(solution)/shard_map/all_gather | solution.py:58
  151.3 40.5 %reduce-scatter.18.cloned.1.call-done = f32[729,288]{0,1:T(8,128)} async-done(((f32[729,1152]{0,1:T(8,128)}), f32[729,288]{0,1:T(8,128)}) %reduce-scatter.18.cloned.1.call-update) | async-done | bytes 839824 | tf_op jit(solution)/shard_map/reduce_scatter | solution.py:62
  218.9 21.7 %all-gather.23.cloned.1.call-done = bf16[729,1152]{0,1:T(8,128)(2,1)} async-done(((bf16[729,288]{0,1:T(8,128)(2,1)}), bf16[729,1152]{0,1:T(8,128)(2,1)}) %all-gather.23.cloned.1.call-update) | async-done | bytes 1679632 | tf_op jit(solution)/shard_map/all_gather | solution.py:58
  262.8 40.5 %reduce-scatter.20.cloned.1.call-done = f32[729,288]{0,1:T(8,128)} async-done(((f32[729,1152]{0,1:T(8,128)}), f32[729,288]{0,1:T(8,128)}) %reduce-scatter.20.cloned.1.call-update) | async-done | bytes 839824 | tf_op jit(solution)/shard_map/reduce_scatter | solution.py:62
  314.2 21.7 %all-gather.25.cloned.1.call-done = bf16[729,1152]{0,1:T(8,128)(2,1)} async-done(((bf16[729,288]{0,1:T(8,128)(2,1)}), bf16[729,1152]{0,1:T(8,128)(2,1)}) %all-gather.25.cloned.1.call-update) | async-done | bytes 1679632 | tf_op jit(solution)/shard_map/all_gather | solution.py:58
  346.4 40.5 %reduce-scatter.22.cloned.1.call-done = f32[729,288]{0,1:T(8,128)} async-done(((f32[729,1152]{0,1:T(8,128)}), f32[729,288]{0,1:T(8,128)}) %reduce-scatter.22.cloned.1.call-update) | async-done | bytes 839824 | tf_op jit(solution)/shard_map/reduce_scatter | solution.py:62
  452.7 40.5 %reduce-scatter.28.cloned.1.call-done = f32[729,288]{0,1:T(8,128)} async-done(((f32[729,1152]{0,1:T(8,128)}), f32[729,288]{0,1:T(8,128)}) %reduce-scatter.28.cloned.1.call-update) | async-done | bytes 839824 | tf_op jit(solution)/shard_map/reduce_scatter | solution.py:62
  562.4 40.5 %reduce-scatter.30.cloned.1.call-done = f32[729,288]{0,1:T(8,128)} async-done(((f32[729,1152]{0,1:T(8,128)}), f32[729,288]{0,1:T(8,128)}) %reduce-scatter.30.cloned.1.call-update) | async-done | bytes 839824 | tf_op jit(solution)/shard_map/reduce_scatter | solution.py:70
  615.2 21.8 %all-gather.37.cloned.1.call-done = bf16[729,1152]{0,1:T(8,128)(2,1)} async-done(((bf16[729,288]{0,1:T(8,128)(2,1)}), bf16[729,1152]{0,1:T(8,128)(2,1)}) %all-gather.37.cloned.1.call-update) | async-done | bytes 1679632 | tf_op jit(solution)/shard_map/all_gather | solution.py:66
  674.1 40.5 %reduce-scatter.32.cloned.1.call-done = f32[729,288]{0,1:T(8,128)} async-done(((f32[729,1152]{0,1:T(8,128)}), f32[729,288]{0,1:T(8,128)}) %reduce-scatter.32.cloned.1.call-update) | async-done | bytes 839824 | tf_op jit(solution)/shard_map/reduce_scatter | solution.py:70
  725.9 21.5 %all-gather.39.cloned.1.call-done = bf16[729,1152]{0,1:T(8,128)(2,1)} async-done(((bf16[729,288]{0,1:T(8,128)(2,1)}), bf16[729,1152]{0,1:T(8,128)(2,1)}) %all-gather.39.cloned.1.call-update) | async-done | bytes 1679632 | tf_op jit(solution)/shard_map/all_gather | solution.py:58
  761.6 40.5 %reduce-scatter.34.cloned.1.call-done = f32[729,288]{0,1:T(8,128)} async-done(((f32[729,1152]{0,1:T(8,128)}), f32[729,288]{0,1:T(8,128)}) %reduce-scatter.34.cloned.1.call-update) | async-done | bytes 839824 | tf_op jit(solution)/shard_map/reduce_scatter | solution.py:62
  875.6 40.5 %reduce-scatter.36.cloned.1.call-done = f32[729,288]{0,1:T(8,128)} async-done(((f32[729,1152]{0,1:T(8,128)}), f32[729,288]{0,1:T(8,128)}) %reduce-scatter.36.cloned.1.call-update) | async-done | bytes 839824 | tf_op jit(solution)/shard_map/reduce_scatter | solution.py:70
  928.5 21.7 %all-gather.45.cloned.1.call-done = bf16[729,1152]{0,1:T(8,128)(2,1)} async-done(((bf16[729,288]{0,1:T(8,128)(2,1)}), bf16[729,1152]{0,1:T(8,128)(2,1)}) %all-gather.45.cloned.1.call-update) | async-done | bytes 1679632 | tf_op jit(solution)/shard_map/all_gather | solution.py:66
  987.4 40.5 %reduce-scatter.38.cloned.1.call-done = f32[729,288]{0,1:T(8,128)} async-done(((f32[729,1152]{0,1:T(8,128)}), f32[729,288]{0,1:T(8,128)}) %reduce-scatter.38.cloned.1.call-update) | async-done | bytes 839824 | tf_op jit(solution)/shard_map/reduce_scatter | solution.py:70
  1039.1 21.6 %all-gather.47.cloned.1.call-done = bf16[729,1152]{0,1:T(8,128)(2,1)} async-done(((bf16[729,288]{0,1:T(8,128)(2,1)}), bf16[729,1152]{0,1:T(8,128)(2,1)}) %all-gather.47.cloned.1.call-update) | async-done | bytes 1679632 | tf_op jit(solution)/shard_map/all_gather | solution.py:58
  1074.9 40.5 %reduce-scatter.40.cloned.1.call-done = f32[729,288]{0,1:T(8,128)} async-done(((f32[729,1152]{0,1:T(8,128)}), f32[729,288]{0,1:T(8,128)}) %reduce-scatter.40.cloned.1.call-update) | async-done | bytes 839824 | tf_op jit(solution)/shard_map/reduce_scatter | solution.py:62
  1189.5 39.2 %reduce-scatter.42.cloned.1.call-done = f32[729,288]{0,1:T(8,128)} async-done(((f32[729,1152]{0,1:T(8,128)}), f32[729,288]{0,1:T(8,128)}) %reduce-scatter.42.cloned.1.call-update) | async-done | bytes 839824 | tf_op jit(solution)/shard_map/reduce_scatter | solution.py:70
  1244.3 21.6 %all-gather.53.cloned.1.call-done = bf16[729,1152]{0,1:T(8,128)(2,1)} async-done(((bf16[729,288]{0,1:T(8,128)(2,1)}), bf16[729,1152]{0,1:T(8,128)(2,1)}) %all-gather.53.cloned.1.call-update) | async-done | bytes 1679632 | tf_op jit(solution)/shard_map/all_gather | solution.py:66
  1302.1 40.5 %reduce-scatter.44.cloned.1.call-done = f32[729,288]{0,1:T(8,128)} async-done(((f32[729,1152]{0,1:T(8,128)}), f32[729,288]{0,1:T(8,128)}) %reduce-scatter.44.cloned.1.call-update) | async-done | bytes 839824 | tf_op jit(solution)/shard_map/reduce_scatter | solution.py:70
  1482.8 22.8 %all-reduce = (f32[1,2,288]{2,1,0:T(2,128)}, f32[1,2,288]{2,1,0:T(2,128)}, f32[1,288]{1,0:T(1,128)}, f32[1,288]{1,0:T(1,128)}, f32[1,2,288]{2,1,0:T(2,128)}, /*index=5*/f32[1,1076]{1,0:T(1,128)}) all-reduce(f32[1,2,288]{2,1,0:T(2,128)S(1)} %fusion.256, ...), channel_id=1, replica_groups=mesh['section'=2,'tensor'=4,'dp'=4] {'dp'}, use_global_device_ids=true, to_apply=%region_108.109 | all-reduce | flops 3380 | bytes 27040 | tf_op jit(solution)/shard_map/psum | solution.py:322
  1505.6 481.6 %all-reduce.18.cloned.1.call-done = (f32[1,1152,288]{1,2,0:T(8,128)}, f32[1,1152,288]{1,2,0:T(8,128)}, f32[1,1152,288]{1,2,0:T(8,128)}, f32[1,288,1152]{2,1,0:T(...) async-done(((f32[1,1152,288]{1,2,0:T(8,128)}, f32[1,1152,288]{1,2,0:T(8,128)}, f32[1,1152,288]{1,2,0:T(8,128)}, f32[1,288,1152]{2,1,0:T(8,128)}, ...) | async-done | bytes 15224848 | tf_op jit(solution)/shard_map/psum | solution.py:322
  1998.6 22.2 %copy.42 = f32[1,1076,1152]{2,0,1:T(1,128)} copy(f32[1,1076,1152]{2,1,0:T(8,128)S(1)} %bitcast.498) | data formatting | bytes 9916416
  (602 shorter events, 809.8 us)
Async XLA Ops:
  23.2 83.9 %reduce-scatter.16.cloned.1.call-start = ((), (), s32[]{:S(2)}) async-start(), calls=%async_computation.16 | async-start | bytes 4423680 | tf_op jit(solution)/shard_map/reduce_scatter | solution.py:62
  66.5 74.2 %all-gather.21.cloned.1.call-start = ((), (), s32[]{:S(2)}) async-start(), calls=%async_computation.17 | async-start | bytes 2211840 | tf_op jit(solution)/shard_map/all_gather | solution.py:58
  151.2 89.4 %all-gather.23.cloned.1.call-start = ((), (), s32[]{:S(2)}) async-start(), calls=%async_computation.19 | async-start | bytes 2211840 | tf_op jit(solution)/shard_map/all_gather | solution.py:58
  218.7 84.7 %reduce-scatter.20.cloned.1.call-start = ((), (), s32[]{:S(2)}) async-start(), calls=%async_computation.20 | async-start | bytes 4423680 | tf_op jit(solution)/shard_map/reduce_scatter | solution.py:62
  346.4 92.0 %all-gather.31.cloned.1.call-start = ((), (), s32[]{:S(2)}) async-start(), calls=%async_computation.27 | async-start | bytes 2211840 | tf_op jit(solution)/shard_map/all_gather | solution.py:58
  416.5 76.7 %reduce-scatter.28.cloned.1.call-start = ((), (), s32[]{:S(2)}) async-start(), calls=%async_computation.28 | async-start | bytes 4423680 | tf_op jit(solution)/shard_map/reduce_scatter | solution.py:62
  504.3 98.6 %reduce-scatter.30.cloned.1.call-start = ((), (), s32[]{:S(2)}) async-start(), calls=%async_computation.31 | async-start | bytes 4423680 | tf_op jit(solution)/shard_map/reduce_scatter | solution.py:70
  562.3 74.6 %all-gather.37.cloned.1.call-start = ((), (), s32[]{:S(2)}) async-start(), calls=%async_computation.32 | async-start | bytes 2211840 | tf_op jit(solution)/shard_map/all_gather | solution.py:66
  614.9 99.7 %reduce-scatter.32.cloned.1.call-start = ((), (), s32[]{:S(2)}) async-start(), calls=%async_computation.33 | async-start | bytes 4423680 | tf_op jit(solution)/shard_map/reduce_scatter | solution.py:70
  725.4 76.7 %reduce-scatter.34.cloned.1.call-start = ((), (), s32[]{:S(2)}) async-start(), calls=%async_computation.35 | async-start | bytes 4423680 | tf_op jit(solution)/shard_map/reduce_scatter | solution.py:62
  761.6 77.3 %all-gather.43.cloned.1.call-start = ((), (), s32[]{:S(2)}) async-start(), calls=%async_computation.37 | async-start | bytes 2211840 | tf_op jit(solution)/shard_map/all_gather | solution.py:58
  836.8 79.3 %reduce-scatter.36.cloned.1.call-start = ((), (), s32[]{:S(2)}) async-start(), calls=%async_computation.38 | async-start | bytes 4423680 | tf_op jit(solution)/shard_map/reduce_scatter | solution.py:70
  875.5 74.8 %all-gather.45.cloned.1.call-start = ((), (), s32[]{:S(2)}) async-start(), calls=%async_computation.39 | async-start | bytes 2211840 | tf_op jit(solution)/shard_map/all_gather | solution.py:66
  928.3 99.7 %reduce-scatter.38.cloned.1.call-start = ((), (), s32[]{:S(2)}) async-start(), calls=%async_computation.40 | async-start | bytes 4423680 | tf_op jit(solution)/shard_map/reduce_scatter | solution.py:70
  987.4 73.3 %all-gather.47.cloned.1.call-start = ((), (), s32[]{:S(2)}) async-start(), calls=%async_computation.41 | async-start | bytes 2211840 | tf_op jit(solution)/shard_map/all_gather | solution.py:58
  1038.7 76.8 %reduce-scatter.40.cloned.1.call-start = ((), (), s32[]{:S(2)}) async-start(), calls=%async_computation.42 | async-start | bytes 4423680 | tf_op jit(solution)/shard_map/reduce_scatter | solution.py:62
  1074.9 77.3 %all-gather.51.cloned.1.call-start = ((), (), s32[]{:S(2)}) async-start(), calls=%async_computation.44 | async-start | bytes 2211840 | tf_op jit(solution)/shard_map/all_gather | solution.py:58
  1149.5 79.2 %reduce-scatter.42.cloned.1.call-start = ((), (), s32[]{:S(2)}) async-start(), calls=%async_computation.45 | async-start | bytes 4423680 | tf_op jit(solution)/shard_map/reduce_scatter | solution.py:70
  1188.1 77.8 %all-gather.53.cloned.1.call-start = ((), (), s32[]{:S(2)}) async-start(), calls=%async_computation.46 | async-start | bytes 2211840 | tf_op jit(solution)/shard_map/all_gather | solution.py:66
  1244.0 98.6 %reduce-scatter.44.cloned.1.call-start = ((), (), s32[]{:S(2)}) async-start(), calls=%async_computation.47 | async-start | bytes 4423680 | tf_op jit(solution)/shard_map/reduce_scatter | solution.py:70
  1345.6 83.7 %reduce-scatter.24.cloned.1.call-start = ((), (), s32[]{:S(2)}) async-start(), calls=%async_computation.24 | async-start | bytes 4423680 | tf_op jit(solution)/shard_map/reduce_scatter | solution.py:62
  1388.7 77.2 %all-gather.29.cloned.1.call-start = ((), (), s32[]{:S(2)}) async-start(), calls=%async_computation.25 | async-start | bytes 2211840 | tf_op jit(solution)/shard_map/all_gather | solution.py:58
  1444.0 543.2 %all-reduce.18.cloned.1.call-start = ((), (), s32[]{:S(2)}) async-start(), calls=%async_computation.48 | async-start | bytes 30523392 | tf_op jit(solution)/shard_map/psum | solution.py:322
  1459.1 569.9 %reduce-scatter.26.cloned.1.call-start = ((), (), s32[]{:S(2)}) async-start(), calls=%async_computation.26 | async-start | bytes 4423680 | tf_op jit(solution)/shard_map/reduce_scatter | solution.py:62
  (155 other events, 1637.0 us)
Sparse Core Ops, SparseCore 0:
  66.7 40.4 reduce-scatter.15
  118.8 21.8 all-gather.20
  151.3 40.4 reduce-scatter.17
  262.9 40.4 reduce-scatter.19
  314.0 21.8 all-gather.24
  346.5 40.4 reduce-scatter.21
  416.6 21.7 all-gather.30
  452.7 40.4 reduce-scatter.27
  503.9 21.8 all-gather.34
  562.5 40.4 reduce-scatter.29
  615.1 21.8 all-gather.36
  674.2 40.4 reduce-scatter.31
  725.6 21.8 all-gather.38
  761.7 40.4 reduce-scatter.33
  875.7 40.3 reduce-scatter.35
  928.4 21.8 all-gather.44
  987.5 40.4 reduce-scatter.37
  1038.8 21.8 all-gather.46
  1075.0 40.4 reduce-scatter.39
  1188.3 40.4 reduce-scatter.41
  1302.2 40.4 reduce-scatter.43
  1388.8 40.4 reduce-scatter.23
  1470.2 516.9 all-reduce.17
  1989.7 39.1 reduce-scatter.25
  (10 shorter events, 212.2 us)
where the time goes:
time: 2060 us; the launch traced here: 2050 us
  waiting for transfers between devices  1380 us (67%)
  matrix products  305 us (15%)
  other arithmetic  141 us (7%)
  blocking collectives  125 us (6%)
  local copies, waits for them, and re-layouts  67.7 us (3%)
    psum x1, waiting for transfers between devices, per_device(): totals = lax.psum(totals, 'dp')  482 us
    reduce_scatter x9, waiting for transfers between devices, collect(): lax.psum_scatter(partial_value, 'tensor', scatter_dimension=1, tiled=True)  299 us
    reduce_scatter x6, waiting for transfers between devices, collect_grad(): lax.psum_scatter(partial_value, 'tensor', scatter_dimension=1, tiled=True)  242 us
    all_gather x12, waiting for transfers between devices, widen(): return lax.all_gather(piece, 'tensor', axis=1, tiled=True)  203 us
    all_gather x6, waiting for transfers between devices, widen_grad(): return lax.all_gather(piece, 'tensor', axis=1, tiled=True)  117 us
    dot_general x30, matrix products, forward_dot(): return jnp.dot(left, right, preferred_element_type=jnp.float32)  99.2 us
    psum x10, blocking collectives, normalize(): lax.psum((jnp.sum(stream, 1), jnp.sum(stream * stream, 1)), 'tensor')  70.3 us
    unnamed x289, local copies, waits for them, and re-layouts  59.9 us
  transfers between devices with their start and end apart: 38, of which 38 were waited for; matrix products, arithmetic and copies ran while one was open for 6% of the time, Pallas kernels for 0%

commit v1 on v0

v1 whole, which is shorter than its diff:
```python
import functools

import jax
import jax.numpy as jnp
from jax import lax
from jax.experimental import pallas as pl
from jax.experimental.pallas import tpu as pltpu
from jax.sharding import PartitionSpec as P

HD = 72
LANES = 128
EPS = 1e-06
SCALE = HD**-0.5
LOG2E = 1.4426950408889634
FAR = -1e30
GELU_A = 0.7978845608028654
GELU_B = 0.044715
F32 = jnp.float32
BF16 = jnp.bfloat16
VMEM = pl.BlockSpec(memory_space=pltpu.VMEM)
SMEM = pl.BlockSpec(memory_space=pltpu.SMEM)


def run(body, outs, args, scalars=0, flops=0, scratch=(), limit=16):
    bytes_accessed = sum(a.size * a.dtype.itemsize for a in args)
    return pl.pallas_call(
        body,
        out_shape=[jax.ShapeDtypeStruct(shape, dtype) for shape, dtype in outs],
        in_specs=[SMEM] * scalars + [VMEM] * (len(args) - scalars),
        out_specs=[VMEM] * len(outs),
        scratch_shapes=list(scratch),
        compiler_params=pltpu.CompilerParams(vmem_limit_bytes=limit * 2**20),
        cost_estimate=pl.CostEstimate(
            flops=int(flops), bytes_accessed=int(bytes_accessed), transcendentals=0
        ),
    )(*args)


def mm(left, right):
    return jnp.dot(left, right, preferred_element_type=F32)


def mm_nt(left, right):
    return lax.dot_general(left, right, (((1,), (1,)), ((), ())), preferred_element_type=F32)


def mm_tn(left, right):
    return lax.dot_general(left, right, (((0,), (0,)), ((), ())), preferred_element_type=F32)


def unit_rows(x):
    center = x - jnp.mean(x, 1, keepdims=True)
    inverse = lax.rsqrt(jnp.mean(center * center, 1, keepdims=True) + EPS)
    return center * inverse, inverse


def assemble(stack, rel, order, rows):
    parts, _, cols = stack.shape
    half = parts // 2

    def body(rel_ref, order_ref, stack_ref, mine_ref, other_ref):
        for place in range(parts):
            start = pl.multiple_of(order_ref[place] * rows, 16)
            block = jnp.concatenate(
                [stack_ref[rel_ref[s], pl.ds(start, rows), :] for s in range(parts)], axis=1
            )
            out = mine_ref if place < half else other_ref
            at = (place % half) * rows
            out[at : at + rows, :] = block

    shape = ((half * rows, parts * cols), BF16)
    return run(body, [shape, shape], (rel, order, stack), scalars=2)


def select_rows(flag, base, blocks):
    def body(flag_ref, base_ref, *refs):
        out = refs[-1]

        @pl.when(flag_ref[0] != 0)
        def _():
            out[...] = base_ref[...]

        @pl.when(flag_ref[0] == 0)
        def _():
            at = 0
            for ref in refs[:-1]:
                out[at : at + ref.shape[0], :] = ref[...]
                at += ref.shape[0]

    return run(body, [(base.shape, BF16)], (flag, base, *blocks), scalars=1)[0]


def project(info, xm, xo, gain, bias, wq, bq, wk, wv, bv):
    half, width = xm.shape
    total = 2 * half
    cols = wq.shape[0]
    heads = cols // HD

    def body(info_ref, xm_ref, xo_ref, g_ref, b_ref, wq_ref, bq_ref, wk_ref, wv_ref, bv_ref,
             n_ref, q_ref, k_ref, v_ref):
        step = half // 2
        for index, ref in enumerate((xm_ref, xo_ref)):
            for at in range(0, half, step):
                unit, _ = unit_rows(ref[at : at + step, :].astype(F32))
                n_ref[index * half + at : index * half + at + step, :] = (
                    unit * g_ref[...] + b_ref[...]
                ).astype(BF16)
        normed = n_ref[...]
        row = lax.broadcasted_iota(jnp.int32, (total, LANES - HD), 0)
        lane = lax.broadcasted_iota(jnp.int32, (total, LANES - HD), 1)
        pad_start = info_ref[0]
        padded = (row >= pad_start) & (row < pad_start + info_ref[1])
        ones = jnp.where(lane == 0, 1.0, 0.0).astype(BF16)
        mask = jnp.where((lane == 0) & padded, FAR, 0.0).astype(BF16)

        def spread(value, out, extra):
            for h in range(heads):
                out[:, h * LANES : (h + 1) * LANES] = jnp.concatenate(
                    [value[:, h * HD : (h + 1) * HD], extra], axis=1
                )

        spread((mm_nt(normed, wq_ref[...]) + bq_ref[...]).astype(BF16), q_ref, ones)
        spread(mm_nt(normed, wk_ref[...]).astype(BF16), k_ref, mask)
        spread((mm_nt(normed, wv_ref[...]) + bv_ref[...]).astype(BF16), v_ref, ones)

    wide = ((total, heads * LANES), BF16)
    return run(
        body,
        [((total, width), BF16), wide, wide, wide],
        (info, xm, xo, gain, bias, wq, bq, wk, wv, bv),
        scalars=1,
        flops=6 * total * width * cols,
    )


def attend(first_row, q, k, v, wout, out_type):
    total, wide = q.shape
    heads = wide // LANES
    half = total // 2
    step = half // 2

    def body(q_ref, k_ref, v_ref, w_ref, z_ref, o_ref, l_ref):
        for at in range(0, half, step):
            outs, logs = [], []
            for h in range(heads):
                lanes = slice(h * LANES, (h + 1) * LANES)
                scores = mm_nt(q_ref[first_row + at : first_row + at + step, lanes], k_ref[:, lanes])
                highest = jnp.max(scores, 1, keepdims=True)
                weights = jnp.exp2((scores - highest) * (SCALE * LOG2E)).astype(BF16)
                mixed = mm(weights, v_ref[:, lanes])
                sums = mixed[:, HD : HD + 1]
                outs.append((mixed / sums).astype(BF16)[:, :HD])
                logs.append(highest * (SCALE * LOG2E) + jnp.log(sums) * LOG2E)
            mixed = jnp.concatenate(outs, axis=1)
            o_ref[at : at + step, :] = mixed
            z_ref[at : at + step, :] = mm(mixed, w_ref[...]).astype(out_type)
            logs = jnp.concatenate(logs + [jnp.zeros((step, LANES - heads), F32)], axis=1)
            l_ref[:, at : at + step] = logs.T[:8, :]

    return run(
        body,
        [((half, wout.shape[1]), out_type), ((half, heads * HD), BF16), ((8, half), F32)],
        (q, k, v, wout),
        flops=4 * half * total * LANES * heads + 2 * half * heads * HD * wout.shape[1],
    )


def middle(xm, own, arrived, out_bias, gain, bias):
    half, width = xm.shape
    parts = len(arrived) + 1
    rows = half // parts

    def body(x_ref, own_ref, *refs):
        got = refs[: parts - 1]
        ob_ref, g_ref, b_ref, h_ref, n_ref = refs[parts - 1 :]
        for p in range(parts):
            here = slice(p * rows, (p + 1) * rows)
            value = x_ref[here, :].astype(F32) + ob_ref[...]
            total = own_ref[here, :].astype(F32)
            for shift, ref in enumerate(got, 1):
                there = (p + shift) % parts
                total = total + ref[there * rows : (there + 1) * rows, :].astype(F32)
            value = value + total
            h_ref[here, :] = value
            unit, _ = unit_rows(value)
            n_ref[here, :] = (unit * g_ref[...] + b_ref[...]).astype(BF16)

    return run(
        body,
        [((half, width), F32), ((half, width), BF16)],
        (xm, own, *arrived, out_bias, gain, bias),
        flops=20 * half * width,
    )


def mlp(n2, w_up, b_up, w_down, out_type, save):
    half, width = n2.shape
    hidden = w_up.shape[0]
    step = half // 2

    def body(n_ref, wu_ref, bu_ref, wd_ref, z_ref, *saved):
        for at in range(0, half, step):
            here = slice(at, at + step)
            u = mm_nt(n_ref[here, :], wu_ref[...]) + bu_ref[...]
            square = u * u
            t = jnp.tanh(GELU_A * u * (1.0 + GELU_B * square))
            low = 0.5 * (1.0 + t)
            active = (u * low).astype(BF16)
            if save:
                slope = low + (0.5 * GELU_A) * u * (1.0 - t * t) * (1.0 + (3 * GELU_B) * square)
                saved[0][here, :] = active
                saved[1][here, :] = slope.astype(BF16)
            z_ref[here, :] = mm(active, wd_ref[...]).astype(out_type)

    outs = [((half, width), out_type)]
    if save:
        outs += [((half, hidden), BF16)] * 2
    return run(body, outs, (n2, w_up, b_up, w_down), flops=4 * half * width * hidden)


def mlp_back(g, slope, w_up, w_down, out_type):
    half, width = g.shape
    hidden = w_up.shape[0]
    step = half // 2

    def body(g_ref, s_ref, wu_ref, wd_ref, z_ref, d_ref):
        for at in range(0, half, step):
            here = slice(at, at + step)
            grad = mm_nt(g_ref[here, :], wd_ref[...]) * s_ref[here, :].astype(F32)
            grad = grad.astype(BF16)
            d_ref[here, :] = grad
            z_ref[here, :] = mm(grad, wu_ref[...]).astype(out_type)

    return run(
        body,
        [((half, width), out_type), ((half, hidden), BF16)],
        (g, slope, w_up, w_down),
        flops=4 * half * width * hidden,
    )


def middle_back(g, h, own, arrived, gain, quarter):
    half, width = g.shape
    parts = len(arrived) + 1
    rows = half // parts

    def body(g_ref, h_ref, own_ref, *refs):
        got = refs[: parts - 1]
        gain_ref, d_ref, low_ref, sums_ref = refs[parts - 1 :]
        for p in range(parts):
            here = slice(p * rows, (p + 1) * rows)
            grad = own_ref[here, :].astype(F32)
            for shift, ref in enumerate(got, 1):
                there = (p + shift) % parts
                grad = grad + ref[there * rows : (there + 1) * rows, :].astype(F32)
            unit, inverse = unit_rows(h_ref[here, :])
            scaled = grad * gain_ref[...]
            first = jnp.mean(scaled, 1, keepdims=True)
            second = jnp.mean(scaled * unit, 1, keepdims=True)
            upstream = g_ref[here, :].astype(F32)
            total = upstream + inverse * (scaled - first - unit * second)
            d_ref[here, :] = total
            low = total.astype(BF16)
            low_ref[here, :] = low
            if p == 0:
                sums_ref[...] = jnp.concatenate(
                    [
                        jnp.sum(grad * unit, 0, keepdims=True),
                        jnp.sum(grad, 0, keepdims=True),
                        jnp.sum(upstream, 0, keepdims=True),
                        jnp.sum(low.astype(F32), 0, keepdims=True),
                        jnp.zeros((4, width), F32),
                    ],
                    axis=0,
                )

    return run(
        body,
        [((half, width), F32), ((half, width), BF16), ((8, width), F32)],
        (g, h, own, *arrived, gain),
        flops=30 * half * width,
    )


def attend_back(dm, do, wout, q, k, v, lm, lo):
    half = dm.shape[0]
    total, wide = q.shape
    heads = wide // LANES
    step = total // 3

    def body(dm_ref, do_ref, w_ref, q_ref, k_ref, v_ref, lm_ref, lo_ref,
             dq_ref, dk_ref, dv_ref, up_ref, log_ref, p_ref, w_ref2):
        for index, ref in enumerate((dm_ref, do_ref)):
            here = slice(index * half, (index + 1) * half)
            grad = mm_nt(ref[...], w_ref[...]).astype(BF16)
            fill = jnp.zeros((half, LANES - HD), BF16)
            for h in range(heads):
                cols = slice(h * HD, (h + 1) * HD)
                up = jnp.concatenate([grad[:, cols], fill], axis=1)
                up_ref[here, h * LANES : (h + 1) * LANES] = up
        log_ref[0:8, 0:half] = lm_ref[...]
        log_ref[0:8, half:total] = lo_ref[...]
        dqs, dks, dvs = [], [], []
        for h in range(heads):
            lanes = slice(h * LANES, (h + 1) * LANES)
            up = up_ref[:, lanes]
            queries = q_ref[:, lanes]
            sums = jnp.zeros((1, total), F32)
            dv_h = []
            for at in range(0, total, step):
                here = slice(at, at + step)
                scores = mm_nt(k_ref[here, lanes], queries)
                probs = jnp.exp2(scores * (SCALE * LOG2E) - log_ref[h : h + 1, :])
                weighted = probs * mm_nt(v_ref[here, lanes], up)
                sums = sums + jnp.sum(weighted, 0, keepdims=True)
                p_ref[here, :] = probs
                w_ref2[here, :] = weighted
                dv_h.append(mm(probs.astype(BF16), up).astype(BF16)[:, :HD])
            dq_t = jnp.zeros((LANES, total), F32)
            dk_h = []
            for at in range(0, total, step):
                here = slice(at, at + step)
                dscores = (w_ref2[here, :] - p_ref[here, :] * sums).astype(BF16)
                dk_h.append((mm(dscores, queries) * SCALE).astype(BF16)[:, :HD])
                dq_t = dq_t + mm_tn(k_ref[here, lanes], dscores)
            dqs.append((dq_t * SCALE).T.astype(BF16)[:, :HD])
            dks.append(jnp.concatenate(dk_h, axis=0))
            dvs.append(jnp.concatenate(dv_h, axis=0))
        dq_ref[...] = jnp.concatenate(dqs, axis=1)
        dk_ref[...] = jnp.concatenate(dks, axis=1)
        dv_ref[...] = jnp.concatenate(dvs, axis=1)

    out = ((total, heads * HD), BF16)
    return run(
        body,
        [out, out, out],
        (dm, do, wout, q, k, v, lm, lo),
        flops=10 * total * total * LANES * heads + 2 * total * heads * HD * dm.shape[1],
        scratch=(
            pltpu.VMEM((total, wide), BF16),
            pltpu.VMEM((8, total), F32),
            pltpu.VMEM((total, total), F32),
            pltpu.VMEM((total, total), F32),
        ),
    )


def project_back(first_row, dq, dk, dv, wq, wk, wv, out_type):
    total, cols = dq.shape
    half = total // 2
    width = wq.shape[1]

    def body(dq_ref, dk_ref, dv_ref, wq_ref, wk_ref, wv_ref, z_ref):
        here = slice(first_row, first_row + half)
        z_ref[...] = (
            mm(dq_ref[here, :], wq_ref[...])
            + mm(dk_ref[here, :], wk_ref[...])
            + mm(dv_ref[here, :], wv_ref[...])
        ).astype(out_type)

    return run(
        body, [((half, width), out_type)], (dq, dk, dv, wq, wk, wv), flops=6 * half * cols * width
    )[0]


def start_back(xm, dh, own, arrived, gain):
    rows, width = own.shape
    count = len(arrived)

    def body(x_ref, dh_ref, own_ref, *refs):
        got = refs[:count]
        gain_ref, d_ref, low_ref, sums_ref = refs[count:]
        grad = own_ref[...]
        for ref in got:
            grad = grad + ref[...].astype(F32)
        unit, inverse = unit_rows(x_ref[0:rows, :].astype(F32))
        scaled = grad * gain_ref[...]
        first = jnp.mean(scaled, 1, keepdims=True)
        second = jnp.mean(scaled * unit, 1, keepdims=True)
        total = dh_ref[0:rows, :] + inverse * (scaled - first - unit * second)
        d_ref[...] = total
        low_ref[...] = total.astype(BF16)
        sums_ref[...] = jnp.concatenate(
            [
                jnp.sum(grad * unit, 0, keepdims=True),
                jnp.sum(grad, 0, keepdims=True),
                jnp.zeros((6, width), F32),
            ],
            axis=0,
        )

    return run(
        body,
        [((rows, width), F32), ((rows, width), BF16), ((8, width), F32)],
        (xm, dh, own, *arrived, gain),
        flops=30 * rows * width,
    )


def core_swap(value):
    size = lax.axis_size("tensor")
    return lax.ppermute(value, "tensor", [(i, i ^ 1) for i in range(size)])


def chip_shift(value, shift):
    size = lax.axis_size("tensor")
    return lax.ppermute(value, "tensor", [(i, (i + 2 * shift) % size) for i in range(size)])


def share_half(half, chips):
    return [chip_shift(half, s) for s in range(1, chips)]


def spread_block(block, chips):
    mine = [block] + [chip_shift(block, chips - p) for p in range(1, chips)]
    return mine, [core_swap(b) for b in mine]


def sum_blocks(half, chips):
    rows = half.shape[0] // chips
    return half[:rows], [
        chip_shift(half[p * rows : (p + 1) * rows].astype(BF16), p) for p in range(1, chips)
    ]


def to_section(value, step):
    pairs = [(0, 1)] if step > 0 else [(1, 0)]
    return lax.ppermute(value, "section", pairs)


def forward(x, w, info, chips, save, end):
    xm, xo = x
    normed, q, k, v = project(
        info, xm, xo, w["gain"][0], w["bias"][0], w["wq"], w["bq"], w["wk"], w["wv"], w["bv"]
    )
    half = xm.shape[0]
    z_other, o_other, l_other = attend(half, q, k, v, w["wout"], BF16)
    z_other = core_swap(z_other)
    z_mine, o_mine, l_mine = attend(0, q, k, v, w["wout"], F32)
    own = (z_mine + z_other.astype(F32)).astype(BF16)
    hidden, n2m = middle(
        xm, own, share_half(own, chips), w["out_bias"][0], w["gain"][1], w["bias"][1]
    )
    n2o = core_swap(n2m)
    other = mlp(n2o, w["w_up"], w["b_up"], w["w_down"], BF16, save)
    y_other = core_swap(other[0])
    mine = mlp(n2m, w["w_up"], w["b_up"], w["w_down"], F32, save)
    total, arrived = sum_blocks(mine[0] + y_other.astype(F32), chips)
    for value in arrived:
        total = total + value.astype(F32)
    result = hidden[: total.shape[0]] + total + w["out_bias"][1]
    saved = None
    if save:
        saved = dict(
            x=x, normed=normed, q=q, k=k, v=v, o=(o_mine, o_other), l=(l_mine, l_other),
            h=hidden, n2=(n2m, n2o), m=(mine[1], other[1]), slope=(mine[2], other[2]),
        )
    return result, saved


def backward(g, saved, w, chips):
    gm, go = g
    z_other, du_other = mlp_back(go, saved["slope"][1], w["w_up"], w["w_down"], BF16)
    z_other = core_swap(z_other)
    z_mine, du_mine = mlp_back(gm, saved["slope"][0], w["w_up"], w["w_down"], F32)
    own = (z_mine + z_other.astype(F32)).astype(BF16)
    dh, dhm, sums_two = middle_back(
        gm, saved["h"], own, share_half(own, chips), w["gain"][1], None
    )
    dho = core_swap(dhm)
    q, k, v = saved["q"], saved["k"], saved["v"]
    dq, dk, dv = attend_back(dhm, dho, w["wout"], q, k, v, *saved["l"])
    half = gm.shape[0]
    d_other = core_swap(project_back(half, dq, dk, dv, w["wq"], w["wk"], w["wv"], BF16))
    d_mine = project_back(0, dq, dk, dv, w["wq"], w["wk"], w["wv"], F32)
    total, arrived = sum_blocks(d_mine + d_other.astype(F32), chips)
    dx, dx_low, sums_one = start_back(saved["x"][0], dh, total, arrived, w["gain"][0])
    work = dict(
        du=(du_mine, du_other), dh=(dhm, dho), dq=dq, dk=dk, dv=dv, sums=(sums_one, sums_two)
    )
    return dx, dx_low, work


def line_sum(pieces):
    place = lax.axis_index("dp")
    inner = (place == 1) | (place == 2)
    results, done = [], []
    for index, piece in enumerate(pieces):
        if index >= 2:
            piece, done[index - 2] = lax.optimization_barrier((piece, done[index - 2]))
        here = piece + lax.ppermute(piece, "dp", [(0, 1), (3, 2)])
        both = here + lax.ppermute(here, "dp", [(1, 2), (2, 1)])
        done.append(both)
    for both in done:
        back = lax.ppermute(both, "dp", [(1, 0), (2, 3)])
        results.append(jnp.where(inner, both, back))
    return results


def finish(value):
    rows, width = value.shape
    step = 128

    def body(value_ref, out_ref):
        out_ref[...] = value_ref[...].astype(F32).reshape(step, 1, width)

    return pl.pallas_call(
        body,
        out_shape=jax.ShapeDtypeStruct((rows, 1, width), F32),
        grid=(pl.cdiv(rows, step),),
        in_specs=[pl.BlockSpec((step, width), lambda i: (i, 0))],
        out_specs=pl.BlockSpec((step, 1, width), lambda i: (i, 0, 0)),
        compiler_params=pltpu.CompilerParams(vmem_limit_bytes=8 * 2**20),
    )(value)


def dp_sum(pieces):
    if lax.axis_size("dp") == 4:
        return line_sum(pieces)
    return [lax.psum(piece, "dp") for piece in pieces]


def per_device(inputs, norm_gain, norm_bias, w_query, b_query, w_key, w_value, b_value, w_out,
               out_bias, w_up, b_up, w_down):
    first = lax.axis_index("section") == 0
    flag = first.astype(jnp.int32)[None]
    me = lax.axis_index("tensor")
    size = lax.axis_size("tensor")
    chips = size // 2
    chip, core = me // 2, me % 2
    _, micro, images, length, cols = inputs.shape
    unit = 16 * size
    total = -(-length // unit) * unit
    rows = total // size
    pad = total - length
    places = jnp.arange(size)
    order = ((chip + places % chips) % chips) * 2 + (core + places // chips) % 2
    order = order.astype(jnp.int32)
    rel = ((places // 2 - chip) % chips + chips * ((places + core) % 2)).astype(jnp.int32)
    info = jnp.stack([rel[size - 1] * rows + rows - pad, jnp.int32(pad)])
    images_all = micro * images

    small = jnp.concatenate([norm_gain[0], norm_bias[0], out_bias[0]], axis=0)
    small = lax.all_gather(small, "tensor", axis=1, tiled=True)
    w = dict(
        gain=(small[0:1], small[1:2]), bias=(small[2:3], small[3:4]),
        out_bias=(small[4:5], small[5:6]),
        wq=w_query[0].T, bq=b_query, wk=w_key[0].T, wv=w_value[0].T, bv=b_value,
        wout=w_out[0], w_up=w_up[0].T, b_up=b_up, w_down=w_down[0],
    )
    own = jnp.pad(
        inputs[0].reshape(images_all, length, cols), ((0, 0), (0, pad), (0, 0))
    )
    full = []
    for n in range(images_all):
        mine, other = spread_block(own[n], chips)
        full.append(assemble(jnp.stack(mine + other), rel, order, rows))

    def widen(block, base):
        mine, other = spread_block(block, chips)
        return (
            select_rows(flag, base[0], mine),
            select_rows(flag, base[1], other),
        )

    streams, results, saves = [], [], []
    for n in range(images_all):
        result, _ = forward(full[n], w, info, chips, False, False)
        streams.append(widen(to_section(result.astype(BF16), 1), full[n]))
    for n in range(images_all):
        result, saved = forward(streams[n], w, info, chips, True, True)
        results.append(result)
        saves.append(saved)
    ends, works, upstreams = [], [], []
    for n in range(images_all):
        _, low, _ = backward(full[n], saves[n], w, chips)
        mine, other = spread_block(to_section(low, -1), chips)
        flip = 1 - flag
        upstreams.append(
            (select_rows(flip, full[n][0], mine), select_rows(flip, full[n][1], other))
        )
    for n in range(images_all):
        dx, _, work = backward(upstreams[n], saves[n], w, chips)
        ends.append(jnp.where(first, dx, results[n]))
        works.append(work)

    def outer(pairs):
        acc = None
        for left, right in pairs:
            term = lax.dot_general(
                left, right, (((0,), (0,)), ((), ())), preferred_element_type=F32
            )
            acc = term if acc is None else acc + term
        return acc.astype(BF16)

    span = range(images_all)
    g_down = outer([(saves[n]["m"][i], upstreams[n][i]) for n in span for i in (0, 1)])
    g_up = outer([(works[n]["du"][i], saves[n]["n2"][i]) for n in span for i in (0, 1)])
    g_out = outer([(saves[n]["o"][i], works[n]["dh"][i]) for n in span for i in (0, 1)])
    g_query = outer([(works[n]["dq"], saves[n]["normed"]) for n in span])
    g_key = outer([(works[n]["dk"], saves[n]["normed"]) for n in span])
    g_value = outer([(works[n]["dv"], saves[n]["normed"]) for n in span])
    g_down, g_up, g_out, g_query, g_key, g_value = dp_sum(
        [g_down, g_up, g_out, g_query, g_key, g_value]
    )

    def total_of(parts):
        return sum(jnp.sum(p.astype(F32), 0) for p in parts)

    wide = sum(
        jnp.stack(
            [
                works[n]["sums"][0][0], works[n]["sums"][1][0],
                works[n]["sums"][0][1], works[n]["sums"][1][1],
                works[n]["sums"][1][3], works[n]["sums"][1][2],
            ]
        )
        for n in span
    )
    wide = lax.psum(wide, ("tensor", "dp"))
    wide = lax.dynamic_slice_in_dim(wide, me * cols, cols, 1)
    narrow = jnp.concatenate(
        [
            total_of([works[n]["dq"] for n in span]),
            total_of([works[n]["dv"] for n in span]),
            total_of([works[n]["du"][i] for n in span for i in (0, 1)]),
        ]
    )
    narrow = lax.psum(narrow, "dp")
    heads = b_query.shape[1]

    ends = jnp.stack(ends).reshape(images_all, rows, size, cols)
    ends = lax.all_to_all(ends, "tensor", split_axis=2, concat_axis=1, tiled=True)
    ends = ends.reshape(images_all, total, cols)[:, :length]
    ends = ends.reshape(1, micro, images, length, cols)
    return (
        ends, wide[None, 0:2], wide[None, 2:4], g_query.T[None].astype(F32), narrow[None, :heads], g_key.T[None].astype(F32),
        g_value.T[None].astype(F32), narrow[None, heads : 2 * heads], g_out[None].astype(F32), wide[None, 4:6],
        finish(g_up).transpose(1, 2, 0),
        narrow[None, 2 * heads :], finish(g_down).transpose(1, 0, 2),
    )


def solution(mesh):
    columns = P("section", None, "tensor")
    vector = P("section", "tensor")
    stacked = P("section", "tensor", None)
    tokens = P("section", None, "dp", None, "tensor")
    weights = (columns, columns, columns, vector, columns, columns, vector, stacked, columns,
               columns, vector, stacked)
    return jax.shard_map(
        per_device, mesh=mesh, in_specs=(tokens, *weights), out_specs=(tokens, *weights),
        check_vma=False,
    )
```

time: 2060 us -> 1030 us (0.50)
  waiting for transfers between devices: 1380 us -> 448 us
  matrix products: 305 us -> 35.3 us
  Pallas kernels: 0 us -> 192 us
  starting transfers between devices: 16.2 us -> 118 us
  other arithmetic: 141 us -> 42.2 us
    reduce_scatter x15 -> x0, waiting for transfers between devices: 541 us -> none  [the longest x9 299 us: collect(): lax.psum_scatter(partial_value, 'tensor', scatter_dimension=1, tiled=True)]
    psum x1 -> x0, waiting for transfers between devices: 482 us -> none  [per_device(): totals = lax.psum(totals, 'dp')]
    ppermute x4 -> x80, waiting for transfers between devices: 36 us -> 448 us  [the longest x22 263 us: chip_shift(): lax.ppermute(value, 'tensor', [(i, (i + 2 * shift) % size) for i in range...]
    all_gather x18 -> x0, waiting for transfers between devices: 321 us -> none  [the longest x12 203 us: widen(): return lax.all_gather(piece, 'tensor', axis=1, tiled=True)]
    dot_general x87 -> x18, matrix products: 282 us -> 35.3 us  [outer(): lax.dot_general(left, right, (((0,), (0,)), ((), ())), preferred_element_...]
    pallas_call x0 -> x64, Pallas kernels: none -> 192 us  [the longest x62 182 us: run(): pl.pallas_call(body, out_shape=[jax.ShapeDtypeStruct(shape, dtype) for sh...]
    ppermute x4 -> x80, starting transfers between devices: 10.9 us -> 113 us  [the longest x6 60.6 us: line_sum(): here = piece + lax.ppermute(piece, 'dp', [(0, 1), (3, 2)])]
    convert_element_type x19 -> x13, other arithmetic: 67.2 us -> 7.47 us  [the longest x1 2.25 us: per_device(): g_out[None].astype(F32)]
  transfers between devices with their start and end apart: 38 -> 81, of which waited for: 38 -> 37; matrix products, arithmetic and copies ran while one was open for 6% -> 10% of each run, Pallas kernels for 0% -> 11%
where the time goes in v1:
time: 1030 us; the launch traced here: 1020 us
  waiting for transfers between devices  448 us (43%)
  Pallas kernels  192 us (19%)
  blocking collectives  120 us (12%)
  starting transfers between devices  118 us (11%)
  local copies, waits for them, and re-layouts  60.5 us (6%)
  other arithmetic  42.2 us (4%)
  matrix products  35.3 us (3%)
    ppermute x22, waiting for transfers between devices, chip_shift(): lax.ppermute(value, 'tensor', [(i, (i + 2 * shift) % size) for i in range...  263 us
    pallas_call x62, Pallas kernels, run(): pl.pallas_call(body, out_shape=[jax.ShapeDtypeStruct(shape, dtype) for sh...  182 us
    psum x1, blocking collectives, per_device(): wide = lax.psum(wide, ('tensor', 'dp'))  102 us
    ppermute x6, waiting for transfers between devices, line_sum(): here = piece + lax.ppermute(piece, 'dp', [(0, 1), (3, 2)])  70.2 us
    ppermute x6, waiting for transfers between devices, line_sum(): back = lax.ppermute(both, 'dp', [(1, 0), (2, 3)])  68.2 us
    ppermute x6, starting transfers between devices, line_sum(): here = piece + lax.ppermute(piece, 'dp', [(0, 1), (3, 2)])  60.6 us
    dot_general x18, matrix products, outer(): lax.dot_general(left, right, (((0,), (0,)), ((), ())), preferred_element_...  35.3 us
    unnamed x319, local copies, waits for them, and re-layouts  31.8 us
  transfers between devices with their start and end apart: 81, of which 37 were waited for; matrix products, arithmetic and copies ran while one was open for 10% of the time, Pallas kernels for 11%

profile of v1, /device:TPU:0, one launch (start us, length us, event | category | flops | bytes accessed | tf_op | source)
XLA Modules:
  0.0 1019.1 jit_solution(9148669343471151831)
XLA Ops:
  7.4 9.6 collective-permute-done
  42.5 20.2 %collective-permute-done.4.refs_0_ = bf16[384,1152]{1,0:T(8,128)(2,1)S(1)} collective-permute-done((bf16[384,1152]{1,0:T(8,128)(2,1)S(1)}, bf16[384,1152]{1,0:T(8,128)(2,1)S(1)}, u32[]{:S(2)}, u32[]{:S(2)}) %collective-permute-start.4) | collective-permute-done | bytes 884768 | tf_op jit(solution)/shard_map/ppermute | solution.py:407
  74.9 10.9 %collective-permute-done.7 = bf16[192,1152]{1,0:T(8,128)(2,1)S(1)} collective-permute-done((bf16[192,1152]{1,0:T(8,128)(2,1)S(1)}, bf16[192,1152]{1,0:T(8,128)(2,1)S(1)}, u32[]{:S(2)}, u32[]{:S(2)}) %collective-permute-start.7) | collective-permute-done | bytes 442400 | tf_op jit(solution)/shard_map/ppermute | solution.py:407
  89.4 9.1 collective-permute-done.8.refs_0_
  100.0 9.3 collective-permute-done.9.refs_1_
  130.0 20.1 %collective-permute-done.13.refs_0_ = bf16[384,1152]{1,0:T(8,128)(2,1)S(1)} collective-permute-done((bf16[384,1152]{1,0:T(8,128)(2,1)S(1)}, bf16[384,1152]{1,0:T(8,128)(2,1)S(1)}, u32[]{:S(2)}, u32[]{:S(2)}) %collective-permute-start.13) | collective-permute-done | bytes 884768 | tf_op jit(solution)/shard_map/ppermute | solution.py:407
  173.3 20.4 %collective-permute-done.16.refs_0_ = bf16[384,1152]{1,0:T(8,128)(2,1)S(1)} collective-permute-done((bf16[384,1152]{1,0:T(8,128)(2,1)S(1)}, bf16[384,1152]{1,0:T(8,128)(2,1)S(1)}, u32[]{:S(2)}, u32[]{:S(2)}) %collective-permute-start.16) | collective-permute-done | bytes 884768 | tf_op jit(solution)/shard_map/ppermute | solution.py:407
  283.7 15.6 %collective-permute-done.35.refs_0_ = bf16[384,1152]{1,0:T(8,128)(2,1)S(1)} collective-permute-done((bf16[384,1152]{1,0:T(8,128)(2,1)S(1)}, bf16[384,1152]{1,0:T(8,128)(2,1)S(1)}, u32[]{:S(2)}, u32[]{:S(2)}) %collective-permute-start.35) | collective-permute-done | bytes 884768 | tf_op jit(solution)/shard_map/ppermute | solution.py:407
  300.3 17.4 %collective-permute-done.25.refs_0_ = bf16[384,1152]{1,0:T(8,128)(2,1)S(1)} collective-permute-done((bf16[384,1152]{1,0:T(8,128)(2,1)S(1)}, bf16[384,1152]{1,0:T(8,128)(2,1)S(1)}, u32[]{:S(2)}, u32[]{:S(2)}) %collective-permute-start.25) | collective-permute-done | bytes 884768 | tf_op jit(solution)/shard_map/ppermute | solution.py:407
  343.0 17.1 %collective-permute-done.28.refs_0_ = bf16[192,1152]{1,0:T(8,128)(2,1)S(1)} collective-permute-done((bf16[192,1152]{1,0:T(8,128)(2,1)S(1)}, bf16[192,1152]{1,0:T(8,128)(2,1)S(1)}, u32[]{:S(2)}, u32[]{:S(2)}) %collective-permute-start.28) | collective-permute-done | bytes 442400 | tf_op jit(solution)/shard_map/ppermute | solution.py:407
  380.8 9.8 collective-permute-done.40.refs_1_
  408.2 21.4 %collective-permute-done.44.refs_0_ = bf16[384,1152]{1,0:T(8,128)(2,1)S(1)} collective-permute-done((bf16[384,1152]{1,0:T(8,128)(2,1)S(1)}, bf16[384,1152]{1,0:T(8,128)(2,1)S(1)}, u32[]{:S(2)}, u32[]{:S(2)}) %collective-permute-start.44) | collective-permute-done | bytes 884768 | tf_op jit(solution)/shard_map/ppermute | solution.py:407
  452.0 21.4 %collective-permute-done.47.refs_0_ = bf16[384,1152]{1,0:T(8,128)(2,1)S(1)} collective-permute-done((bf16[384,1152]{1,0:T(8,128)(2,1)S(1)}, bf16[384,1152]{1,0:T(8,128)(2,1)S(1)}, u32[]{:S(2)}, u32[]{:S(2)}) %collective-permute-start.47) | collective-permute-done | bytes 884768 | tf_op jit(solution)/shard_map/ppermute | solution.py:407
  484.5 9.5 shard_map.277
  508.8 11.2 %collective-permute-done.50.refs_0_ = bf16[192,1152]{1,0:T(8,128)(2,1)S(1)} collective-permute-done((bf16[192,1152]{1,0:T(8,128)(2,1)S(1)}, bf16[192,1152]{1,0:T(8,128)(2,1)S(1)}, u32[]{:S(2)}, u32[]{:S(2)}) %collective-permute-start.50) | collective-permute-done | bytes 442400 | tf_op jit(solution)/shard_map/ppermute | solution.py:407
  581.6 18.7 %collective-permute-done.56.refs_0_ = bf16[384,1152]{1,0:T(8,128)(2,1)S(1)} collective-permute-done((bf16[384,1152]{1,0:T(8,128)(2,1)S(1)}, bf16[384,1152]{1,0:T(8,128)(2,1)S(1)}, u32[]{:S(2)}, u32[]{:S(2)}) %collective-permute-start.56) | collective-permute-done | bytes 884768 | tf_op jit(solution)/shard_map/ppermute | solution.py:407
  603.8 21.2 %collective-permute-done.67 = bf16[1076,1152]{1,0:T(8,128)(2,1)} collective-permute-done((bf16[1076,1152]{1,0:T(8,128)(2,1)S(1)}, bf16[1076,1152]{1,0:T(8,128)(2,1)}, u32[]{:S(2)}, u32[]{:S(2)}) %collective-permute-start.67) | collective-permute-done | bytes 2479136 | tf_op jit(solution)/shard_map/ppermute | solution.py:491
  628.3 49.0 %collective-permute-done.62 = bf16[1076,1152]{1,0:T(8,128)(2,1)S(1)} collective-permute-done((bf16[1076,1152]{1,0:T(8,128)(2,1)S(1)}, bf16[1076,1152]{1,0:T(8,128)(2,1)S(1)}, u32[]{:S(2)}, u32[]{:S(2)}) %collective-permute-start.62) | collective-permute-done | bytes 2479136 | tf_op jit(solution)/shard_map/ppermute | solution.py:491
  701.6 9.6 collective-permute-done.59.refs_0_
  725.0 19.5 %collective-permute-start.64 = (bf16[288,1152]{1,0:T(8,128)(2,1)}, bf16[288,1152]{1,0:T(8,128)(2,1)}, u32[]{:S(2)}, u32[]{:S(2)}) collective-permute-start(bf16[288,1152]{1,0:T(8,128)(2,1)} %fusion.9), channel_id=1, source_target_pairs={{0,1},{3,2},{4,5},{7,6},{8,9},{11,10},{12,13},{15,14},{16,17},{19,... | collective-permute-start | bytes 1990664 | tf_op jit(solution)/shard_map/ppermute | solution.py:491
  761.2 12.5 %psum.15 = f32[1652]{0:T(1024)S(1)} all-reduce(f32[1652]{0:T(1024)S(1)} %concatenate.8), channel_id=1, replica_groups=mesh['section'=2,'tensor'=4,'dp'=4] {'dp'}, use_global_device_ids=true, to_apply=%region_9.10 | all-reduce | flops 1652 | bytes 13216 | tf_op jit(solution)/shard_map/psum | solution.py:629
  781.3 20.2 %collective-permute-start.71 = (bf16[288,1152]{1,0:T(8,128)(2,1)}, bf16[288,1152]{1,0:T(8,128)(2,1)}, u32[]{:S(2)}, u32[]{:S(2)}) collective-permute-start(bf16[288,1152]{1,0:T(8,128)(2,1)} %fusion.10), channel_id=1, source_target_pairs={{0,1},{3,2},{4,5},{7,6},{8,9},{11,10},{12,13},{15,14},{16,17},{19,... | collective-permute-start | bytes 1990664 | tf_op jit(solution)/shard_map/ppermute | solution.py:491
  811.5 101.6 %psum.14 = f32[6,1152]{1,0:T(8,128)S(1)} all-reduce(f32[6,1152]{1,0:T(8,128)S(1)} %add.294), channel_id=1, replica_groups=mesh['section'=2,'tensor'=4,'dp'=4] {'tensor','dp'}, use_global_device_ids=true, to_apply=%region_0.1 | all-reduce | flops 6912 | bytes 55296 | tf_op jit(solution)/shard_map/psum | solution.py:620
  945.9 47.1 %collective-permute-done.78 = bf16[1076,1152]{1,0:T(8,128)(2,1)S(1)} collective-permute-done((bf16[1076,1152]{1,0:T(8,128)(2,1)S(1)}, bf16[1076,1152]{1,0:T(8,128)(2,1)S(1)}, u32[]{:S(2)}, u32[]{:S(2)}) %collective-permute-start.78) | collective-permute-done | bytes 2479136 | tf_op jit(solution)/shard_map/ppermute | solution.py:495
  (641 shorter events, 492.7 us)
Async XLA Ops:
  282.5 35.2 %collective-permute-start.25 = (bf16[384,1152]{1,0:T(8,128)(2,1)S(1)}, bf16[384,1152]{1,0:T(8,128)(2,1)S(1)}, u32[]{:S(2)}, u32[]{:S(2)}) collective-permute-start(bf16[384,1152]{1,0:T(8,128)(2,1)S(1)} %add_convert_fusion.4.own_ref), channel_id=1, source_target_pairs={{0,8},{4,12},{8,0},{12,4},{1,9},{5,13},{9,1},{13,5},{2,10},{6,14},... | collective-permute-start | bytes 2654216 | tf_op jit(solution)/shard_map/ppermute | solution.py:407
  337.5 24.1 %collective-permute-start.38 = (bf16[192,1152]{1,0:T(8,128)(2,1)S(1)}, bf16[192,1152]{1,0:T(8,128)(2,1)S(1)}, u32[]{:S(2)}, u32[]{:S(2)}) collective-permute-start(bf16[192,1152]{1,0:T(8,128)(2,1)S(1)} %slice.277), channel_id=1, source_target_pairs={{0,8},{4,12},{8,0},{12,4},{1,9},{5,13},{9,1},{13,5},{2,10},{6,14},... | collective-permute-start | bytes 1327112 | tf_op jit(solution)/shard_map/ppermute | solution.py:407
  341.8 26.9 %collective-permute-start.30 = (bf16[192,1152]{1,0:T(8,128)(2,1)S(1)}, bf16[192,1152]{1,0:T(8,128)(2,1)S(1)}, u32[]{:S(2)}, u32[]{:S(2)}) collective-permute-start(bf16[192,1152]{1,0:T(8,128)(2,1)S(1)} %slice.278), channel_id=1, source_target_pairs={{0,8},{4,12},{8,0},{12,4},{1,9},{5,13},{9,1},{13,5},{2,10},{6,14},... | collective-permute-start | bytes 1327112 | tf_op jit(solution)/shard_map/ppermute | solution.py:407
  537.3 40.9 %collective-permute-start.60 = (bf16[384,1152]{1,0:T(8,128)(2,1)}, bf16[384,1152]{1,0:T(8,128)(2,1)}, u32[]{:S(2)}, u32[]{:S(2)}) collective-permute-start(bf16[384,1152]{1,0:T(8,128)(2,1)} %copy-done.91), channel_id=1, source_target_pairs={{0,4},{4,0},{8,12},{12,8},{1,5},{5,1},{9,13},{13,9},{2,6},{6,2},{1... | collective-permute-start | bytes 2654216 | tf_op jit(solution)/shard_map/ppermute | solution.py:402
  537.4 23.1 %collective-permute-start.53 = (bf16[192,1152]{1,0:T(8,128)(2,1)}, bf16[192,1152]{1,0:T(8,128)(2,1)S(1)}, u32[]{:S(2)}, u32[]{:S(2)}) collective-permute-start(bf16[192,1152]{1,0:T(8,128)(2,1)} %collective-permute-done.51.refs_0_), channel_id=1, source_target_pairs={{0,4},{4,0},{8,12},{12,8},{1,5},{5,1},{9,13},{13,9},{2,6},{6,2},{1... | collective-permute-start | bytes 1327112 | tf_op jit(solution)/shard_map/ppermute | solution.py:402
  567.1 57.9 %collective-permute-start.67 = (bf16[1076,1152]{1,0:T(8,128)(2,1)S(1)}, bf16[1076,1152]{1,0:T(8,128)(2,1)}, u32[]{:S(2)}, u32[]{:S(2)}) collective-permute-start(bf16[1076,1152]{1,0:T(8,128)(2,1)S(1)} %fusion.4), channel_id=1, source_target_pairs={{0,1},{3,2},{4,5},{7,6},{8,9},{11,10},{12,13},{15,14},{16,17},{19,... | collective-permute-start | bytes 7437320 | tf_op jit(solution)/shard_map/ppermute | solution.py:491
  576.0 101.3 %collective-permute-start.62 = (bf16[1076,1152]{1,0:T(8,128)(2,1)S(1)}, bf16[1076,1152]{1,0:T(8,128)(2,1)S(1)}, u32[]{:S(2)}, u32[]{:S(2)}) collective-permute-start(bf16[1076,1152]{1,0:T(8,128)(2,1)S(1)} %fusion.3), channel_id=1, source_target_pairs={{0,1},{3,2},{4,5},{7,6},{8,9},{11,10},{12,13},{15,14},{16,17},{19,... | collective-permute-start | bytes 7437320 | tf_op jit(solution)/shard_map/ppermute | solution.py:491
  577.7 22.6 %collective-permute-start.56 = (bf16[384,1152]{1,0:T(8,128)(2,1)S(1)}, bf16[384,1152]{1,0:T(8,128)(2,1)S(1)}, u32[]{:S(2)}, u32[]{:S(2)}) collective-permute-start(bf16[384,1152]{1,0:T(8,128)(2,1)S(1)} %add_convert_fusion.own_ref), channel_id=1, source_target_pairs={{0,8},{4,12},{8,0},{12,4},{1,9},{5,13},{9,1},{13,5},{2,10},{6,14},... | collective-permute-start | bytes 2654216 | tf_op jit(solution)/shard_map/ppermute | solution.py:407
  580.4 164.1 %collective-permute-start.61 = (bf16[192,1152]{1,0:T(8,128)(2,1)S(1)}, bf16[192,1152]{1,0:T(8,128)(2,1)S(1)}, u32[]{:S(2)}, u32[]{:S(2)}) collective-permute-start(bf16[192,1152]{1,0:T(8,128)(2,1)S(1)} %slice.274), channel_id=1, source_target_pairs={{0,8},{4,12},{8,0},{12,4},{1,9},{5,13},{9,1},{13,5},{2,10},{6,14},... | collective-permute-start | bytes 1327112 | tf_op jit(solution)/shard_map/ppermute | solution.py:407
  601.9 77.3 %collective-permute-start.57 = (bf16[384,1152]{1,0:T(8,128)(2,1)S(1)}, bf16[384,1152]{1,0:T(8,128)(2,1)S(1)}, u32[]{:S(2)}, u32[]{:S(2)}) collective-permute-start(bf16[384,1152]{1,0:T(8,128)(2,1)S(1)} %get-tuple-element.184.dm_ref), channel_id=1, source_target_pairs={{0,4},{4,0},{8,12},{12,8},{1,5},{5,1},{9,13},{13,9},{2,6},{6,2},{1... | collective-permute-start | bytes 2654216 | tf_op jit(solution)/shard_map/ppermute | solution.py:402
  627.4 85.3 %collective-permute-start.68 = (bf16[1076,1152]{1,0:T(8,128)(2,1)S(1)}, bf16[1076,1152]{1,0:T(8,128)(2,1)S(1)}, u32[]{:S(2)}, u32[]{:S(2)}) collective-permute-start(bf16[1076,1152]{1,0:T(8,128)(2,1)S(1)} %add.317), channel_id=1, source_target_pairs={{1,2},{2,1},{5,6},{6,5},{9,10},{10,9},{13,14},{14,13},{17,18},{18,... | collective-permute-start | bytes 7437320 | tf_op jit(solution)/shard_map/ppermute | solution.py:492
  678.0 44.8 %collective-permute-start.63 = (bf16[1076,1152]{1,0:T(8,128)(2,1)S(1)}, bf16[1076,1152]{1,0:T(8,128)(2,1)S(1)}, u32[]{:S(2)}, u32[]{:S(2)}) collective-permute-start(bf16[1076,1152]{1,0:T(8,128)(2,1)S(1)} %add.301), channel_id=1, source_target_pairs={{1,2},{2,1},{5,6},{6,5},{9,10},{10,9},{13,14},{14,13},{17,18},{18,... | collective-permute-start | bytes 7437320 | tf_op jit(solution)/shard_map/ppermute | solution.py:492
  714.8 38.4 %collective-permute-start.69 = (bf16[288,1152]{1,0:T(8,128)(2,1)}, bf16[288,1152]{1,0:T(8,128)(2,1)}, u32[]{:S(2)}, u32[]{:S(2)}) collective-permute-start(bf16[288,1152]{1,0:T(8,128)(2,1)} %fusion.7), channel_id=1, source_target_pairs={{0,1},{3,2},{4,5},{7,6},{8,9},{11,10},{12,13},{15,14},{16,17},{19,... | collective-permute-start | bytes 1990664 | tf_op jit(solution)/shard_map/ppermute | solution.py:491
  725.0 32.1 %collective-permute-start.64 = (bf16[288,1152]{1,0:T(8,128)(2,1)}, bf16[288,1152]{1,0:T(8,128)(2,1)}, u32[]{:S(2)}, u32[]{:S(2)}) collective-permute-start(bf16[288,1152]{1,0:T(8,128)(2,1)} %fusion.9), channel_id=1, source_target_pairs={{0,1},{3,2},{4,5},{7,6},{8,9},{11,10},{12,13},{15,14},{16,17},{19,... | collective-permute-start | bytes 1990664 | tf_op jit(solution)/shard_map/ppermute | solution.py:491
  748.4 165.4 %all-to-all-start = ((f32[2,192,4,288]{3,1,0,2:T(8,128)}), f32[2,192,4,288]{3,1,0,2:T(8,128)}, u32[]{:S(2)}, u32[]{:S(2)}) async-start(f32[2,192,4,288]{3,1,0,2:T(8,128)} %pad_maximum_fusion.2), calls=%async_computation | async-start | bytes 4718592 | tf_op jit(solution)/shard_map/all_to_all | solution.py:633
  755.5 24.4 %collective-permute-start.70 = (bf16[288,1152]{1,0:T(8,128)(2,1)}, bf16[288,1152]{1,0:T(8,128)(2,1)}, u32[]{:S(2)}, u32[]{:S(2)}) collective-permute-start(bf16[288,1152]{1,0:T(8,128)(2,1)} %add.319), channel_id=1, source_target_pairs={{1,2},{2,1},{5,6},{6,5},{9,10},{10,9},{13,14},{14,13},{17,18},{18,... | collective-permute-start | bytes 1990664 | tf_op jit(solution)/shard_map/ppermute | solution.py:492
  759.4 43.5 %collective-permute-start.65 = (bf16[288,1152]{1,0:T(8,128)(2,1)}, bf16[288,1152]{1,0:T(8,128)(2,1)}, u32[]{:S(2)}, u32[]{:S(2)}) collective-permute-start(bf16[288,1152]{1,0:T(8,128)(2,1)} %add.303), channel_id=1, source_target_pairs={{1,2},{2,1},{5,6},{6,5},{9,10},{10,9},{13,14},{14,13},{17,18},{18,... | collective-permute-start | bytes 1990664 | tf_op jit(solution)/shard_map/ppermute | solution.py:492
  774.4 166.5 %collective-permute-start.79 = (bf16[1076,1152]{1,0:T(8,128)(2,1)}, bf16[1076,1152]{1,0:T(8,128)(2,1)}, u32[]{:S(2)}, u32[]{:S(2)}) collective-permute-start(bf16[1076,1152]{1,0:T(8,128)(2,1)} %add.318), channel_id=1, source_target_pairs={{1,0},{2,3},{5,4},{6,7},{9,8},{10,11},{13,12},{14,15},{17,16},{18,... | collective-permute-start | bytes 7437320 | tf_op jit(solution)/shard_map/ppermute | solution.py:495
  781.3 142.5 %collective-permute-start.71 = (bf16[288,1152]{1,0:T(8,128)(2,1)}, bf16[288,1152]{1,0:T(8,128)(2,1)}, u32[]{:S(2)}, u32[]{:S(2)}) collective-permute-start(bf16[288,1152]{1,0:T(8,128)(2,1)} %fusion.10), channel_id=1, source_target_pairs={{0,1},{3,2},{4,5},{7,6},{8,9},{11,10},{12,13},{15,14},{16,17},{19,... | collective-permute-start | bytes 1990664 | tf_op jit(solution)/shard_map/ppermute | solution.py:491
  801.6 127.5 %collective-permute-start.77 = (bf16[288,1152]{1,0:T(8,128)(2,1)S(1)}, bf16[288,1152]{1,0:T(8,128)(2,1)}, u32[]{:S(2)}, u32[]{:S(2)}) collective-permute-start(bf16[288,1152]{1,0:T(8,128)(2,1)S(1)} %add.320), channel_id=1, source_target_pairs={{1,0},{2,3},{5,4},{6,7},{9,8},{10,11},{13,12},{14,15},{17,16},{18,... | collective-permute-start | bytes 1990664 | tf_op jit(solution)/shard_map/ppermute | solution.py:495
  805.2 121.4 %collective-permute-start.74 = (bf16[288,1152]{1,0:T(8,128)(2,1)}, bf16[288,1152]{1,0:T(8,128)(2,1)}, u32[]{:S(2)}, u32[]{:S(2)}) collective-permute-start(bf16[288,1152]{1,0:T(8,128)(2,1)} %fusion.8), channel_id=1, source_target_pairs={{0,1},{3,2},{4,5},{7,6},{8,9},{11,10},{12,13},{15,14},{16,17},{19,... | collective-permute-start | bytes 1990664 | tf_op jit(solution)/shard_map/ppermute | solution.py:491
  923.8 69.2 %collective-permute-start.78 = (bf16[1076,1152]{1,0:T(8,128)(2,1)S(1)}, bf16[1076,1152]{1,0:T(8,128)(2,1)S(1)}, u32[]{:S(2)}, u32[]{:S(2)}) collective-permute-start(bf16[1076,1152]{1,0:T(8,128)(2,1)S(1)} %copy-done.134), channel_id=1, source_target_pairs={{1,0},{2,3},{5,4},{6,7},{9,8},{10,11},{13,12},{14,15},{17,16},{18,... | collective-permute-start | bytes 7437320 | tf_op jit(solution)/shard_map/ppermute | solution.py:495
  943.1 64.1 %collective-permute-start.73 = (bf16[288,1152]{1,0:T(8,128)(2,1)S(1)}, bf16[288,1152]{1,0:T(8,128)(2,1)S(1)}, u32[]{:S(2)}, u32[]{:S(2)}) collective-permute-start(bf16[288,1152]{1,0:T(8,128)(2,1)S(1)} %add.322), channel_id=1, source_target_pairs={{1,0},{2,3},{5,4},{6,7},{9,8},{10,11},{13,12},{14,15},{17,16},{18,... | collective-permute-start | bytes 1990664 | tf_op jit(solution)/shard_map/ppermute | solution.py:495
  944.6 72.8 %collective-permute-start.76 = (bf16[288,1152]{1,0:T(8,128)(2,1)S(1)}, bf16[288,1152]{1,0:T(8,128)(2,1)S(1)}, u32[]{:S(2)}, u32[]{:S(2)}) collective-permute-start(bf16[288,1152]{1,0:T(8,128)(2,1)S(1)} %add.324), channel_id=1, source_target_pairs={{1,0},{2,3},{5,4},{6,7},{9,8},{10,11},{13,12},{14,15},{17,16},{18,... | collective-permute-start | bytes 1990664 | tf_op jit(solution)/shard_map/ppermute | solution.py:495
  (215 other events, 3257.3 us)

commit v2 on v1

--- a/solution.py
+++ b/solution.py
@@ -13,6 +13,9 @@
 SCALE = HD**-0.5
 LOG2E = 1.4426950408889634
 FAR = -1e30
+LIMIT = 6
+COST = 14
+STEP = 48
 GELU_A = 0.7978845608028654
 GELU_B = 0.044715
 F32 = jnp.float32
@@ -21,19 +24,28 @@
 SMEM = pl.BlockSpec(memory_space=pltpu.SMEM)
 
 
-def run(body, outs, args, scalars=0, flops=0, scratch=(), limit=16):
-    bytes_accessed = sum(a.size * a.dtype.itemsize for a in args)
+def run(body, outs, args, scalars=0, flops=0, scratch=(), limit=LIMIT, after=()):
+    bytes_accessed = sum(a.size * a.dtype.itemsize for a in args) + sum(
+        jnp.dtype(dtype).itemsize * shape[0] * shape[1] for shape, dtype in outs
+    )
+    count, extra = len(args), len(after)
+
+    def kernel(*refs):
+        body(*refs[:count], *refs[count + extra :])
+
     return pl.pallas_call(
-        body,
+        kernel,
         out_shape=[jax.ShapeDtypeStruct(shape, dtype) for shape, dtype in outs],
-        in_specs=[SMEM] * scalars + [VMEM] * (len(args) - scalars),
+        in_specs=[SMEM] * scalars
+        + [VMEM] * (count - scalars)
+        + [pl.BlockSpec(memory_space=pl.ANY)] * extra,
         out_specs=[VMEM] * len(outs),
         scratch_shapes=list(scratch),
         compiler_params=pltpu.CompilerParams(vmem_limit_bytes=limit * 2**20),
         cost_estimate=pl.CostEstimate(
-            flops=int(flops), bytes_accessed=int(bytes_accessed), transcendentals=0
+            flops=int(flops) * COST, bytes_accessed=int(bytes_accessed), transcendentals=0
         ),
-    )(*args)
+    )(*args, *after)
 
 
 def mm(left, right):
@@ -54,54 +66,102 @@
     return center * inverse, inverse
 
 
-def assemble(stack, rel, order, rows):
-    parts, _, cols = stack.shape
-    half = parts // 2
-
-    def body(rel_ref, order_ref, stack_ref, mine_ref, other_ref):
-        for place in range(parts):
+def assemble(parts, length, sources, order, rows, extra, after=()):
+    count = len(parts)
+    cols = parts[0].shape[0]
+    half, total, width = count // 2, rows * count, cols * count
+
+    def body(*refs):
+        src_ref, order_ref = refs[:2]
+        part_refs = refs[2 : 2 + count]
+        mine_ref, other_ref, *small_out, wide_ref, tall_ref = refs[2 + count :]
+        edge = length // LANES * LANES
+        wide_ref[:, edge:] = jnp.zeros((width, wide_ref.shape[1] - edge), BF16)
+        for i in range(count):
+            start = pl.multiple_of(src_ref[i] * cols, 16)
+            wide_ref[pl.ds(start, cols), 0 : parts[i].shape[1]] = part_refs[i][...]
+        tall_ref[...] = wide_ref[...].T
+        if extra:
+            behind = tall_ref[total : total + 3 * extra, :].astype(F32)
+            small_out[0][...] = (
+                behind[0:extra] + behind[extra : 2 * extra] + behind[2 * extra :]
+            )
+            tall_ref[total : total + LANES, :] = jnp.zeros((LANES, width), BF16)
+        for place in range(count):
             start = pl.multiple_of(order_ref[place] * rows, 16)
-            block = jnp.concatenate(
-                [stack_ref[rel_ref[s], pl.ds(start, rows), :] for s in range(parts)], axis=1
-            )
             out = mine_ref if place < half else other_ref
             at = (place % half) * rows
-            out[at : at + rows, :] = block
-
-    shape = ((half * rows, parts * cols), BF16)
-    return run(body, [shape, shape], (rel, order, stack), scalars=2)
-
-
-def select_rows(flag, base, blocks):
-    def body(flag_ref, base_ref, *refs):
-        out = refs[-1]
-
-        @pl.when(flag_ref[0] != 0)
-        def _():
-            out[...] = base_ref[...]
-
-        @pl.when(flag_ref[0] == 0)
-        def _():
-            at = 0
-            for ref in refs[:-1]:
-                out[at : at + ref.shape[0], :] = ref[...]
-                at += ref.shape[0]
-
-    return run(body, [(base.shape, BF16)], (flag, base, *blocks), scalars=1)[0]
-
-
-def project(info, xm, xo, gain, bias, wq, bq, wk, wv, bv):
-    half, width = xm.shape
-    total = 2 * half
-    cols = wq.shape[0]
+            out[at : at + rows, :] = tall_ref[pl.ds(start, rows), :]
+
+    shape = ((half * rows, width), BF16)
+    deep = total + (LANES if extra else 0)
+    mine, other, *small = run(
+        body,
+        [shape, shape] + ([((extra, width), F32)] if extra else []),
+        (sources, order, *parts),
+        scalars=2,
+        scratch=(pltpu.VMEM((width, deep), BF16), pltpu.VMEM((deep, width), BF16)),
+        limit=10,
+        after=after,
+    )
+    return (mine, other), small
+
+
+class Source:
+    def __init__(self, halves=None, blocks=None, flag=None):
+        self.halves, self.blocks, self.flag = halves, blocks, flag
+
+    def operands(self, which):
+        scalars = [] if self.flag is None else [self.flag]
+        arrays = []
+        for i in which:
+            arrays += [] if self.halves is None else [self.halves[i]]
+            arrays += [] if self.blocks is None else self.blocks[i]
+        return scalars, arrays
+
+    def reader(self, which, scalar_refs, refs):
+        refs, table = list(refs), {}
+        for i in which:
+            base = None if self.halves is None else refs.pop(0)
+            count = 0 if self.blocks is None else len(self.blocks[i])
+            table[i] = (base, [refs.pop(0) for _ in range(count)])
+
+        def read(i, start, rows):
+            base, blocks = table[i]
+            value = None
+            if blocks:
+                size = blocks[0].shape[0]
+                value = blocks[start // size][start % size : start % size + rows, :]
+            if base is not None:
+                at_hand = base[start : start + rows, :]
+                if value is None:
+                    return at_hand
+                value = jnp.where(scalar_refs[0][0] != 0, at_hand, value)
+            return value
+
+        return read
+
+
+def project(info, source, gain, bias, wq, bq, wk, wv, bv, rows, after=()):
+    cols, width = wq.shape
     heads = cols // HD
-
-    def body(info_ref, xm_ref, xo_ref, g_ref, b_ref, wq_ref, bq_ref, wk_ref, wv_ref, bv_ref,
-             n_ref, q_ref, k_ref, v_ref):
-        step = half // 2
-        for index, ref in enumerate((xm_ref, xo_ref)):
+    scalars, arrays = source.operands((0, 1))
+    count, total = len(arrays), rows
+    half = total // 2
+    step = STEP
+
+    def body(*refs):
+        info_ref, flags = refs[0], refs[1 : 1 + len(scalars)]
+        refs = refs[1 + len(scalars) :]
+        read = source.reader((0, 1), flags, refs[:count])
+        (g_ref, b_ref, wq_ref, bq_ref, wk_ref, wv_ref, bv_ref,
+         x_ref, n_ref, q_ref, k_ref, v_ref) = refs[count:]
+        for index in (0, 1):
             for at in range(0, half, step):
-                unit, _ = unit_rows(ref[at : at + step, :].astype(F32))
+                value = read(index, at, step)
+                if index == 0:
+                    x_ref[at : at + step, :] = value
+                unit, _ = unit_rows(value.astype(F32))
                 n_ref[index * half + at : index * half + at + step, :] = (
                     unit * g_ref[...] + b_ref[...]
                 ).astype(BF16)
@@ -126,10 +186,11 @@
     wide = ((total, heads * LANES), BF16)
     return run(
         body,
-        [((total, width), BF16), wide, wide, wide],
-        (info, xm, xo, gain, bias, wq, bq, wk, wv, bv),
-        scalars=1,
+        [((half, width), BF16), ((total, width), BF16), wide, wide, wide],
+        (info, *scalars, *arrays, gain, bias, wq, bq, wk, wv, bv),
+        scalars=1 + len(scalars),
         flops=6 * total * width * cols,
+        after=after,
     )
 
 
@@ -165,7 +226,7 @@
     )
 
 
-def middle(xm, own, arrived, out_bias, gain, bias):
+def middle(xm, own, arrived, out_bias, gain, bias, after=()):
     half, width = xm.shape
     parts = len(arrived) + 1
     rows = half // parts
@@ -173,23 +234,28 @@
     def body(x_ref, own_ref, *refs):
         got = refs[: parts - 1]
         ob_ref, g_ref, b_ref, h_ref, n_ref = refs[parts - 1 :]
-        for p in range(parts):
-            here = slice(p * rows, (p + 1) * rows)
+        def step(i, carry):
+            at = pl.multiple_of(i * STEP, 16)
+            here = pl.ds(at, STEP)
             value = x_ref[here, :].astype(F32) + ob_ref[...]
             total = own_ref[here, :].astype(F32)
             for shift, ref in enumerate(got, 1):
-                there = (p + shift) % parts
-                total = total + ref[there * rows : (there + 1) * rows, :].astype(F32)
+                there = pl.multiple_of(lax.rem(at + shift * rows, half), 16)
+                total = total + ref[pl.ds(there, STEP), :].astype(F32)
             value = value + total
             h_ref[here, :] = value
             unit, _ = unit_rows(value)
             n_ref[here, :] = (unit * g_ref[...] + b_ref[...]).astype(BF16)
+            return carry
+
+        lax.fori_loop(0, half // STEP, step, 0)
 
     return run(
         body,
         [((half, width), F32), ((half, width), BF16)],
         (xm, own, *arrived, out_bias, gain, bias),
         flops=20 * half * width,
+        after=after,
     )
 
 
@@ -218,14 +284,20 @@
     return run(body, outs, (n2, w_up, b_up, w_down), flops=4 * half * width * hidden)
 
 
-def mlp_back(g, slope, w_up, w_down, out_type):
-    half, width = g.shape
-    hidden = w_up.shape[0]
-    step = half // 2
-
-    def body(g_ref, s_ref, wu_ref, wd_ref, z_ref, d_ref):
+def mlp_back(which, source, slope, w_up, w_down, out_type, after=()):
+    half, hidden = slope.shape
+    width = w_up.shape[1]
+    scalars, arrays = source.operands((which,))
+    count = len(arrays)
+    step = half // 2 if source.blocks is None else source.blocks[0][0].shape[0]
+
+    def body(*refs):
+        read = source.reader((which,), refs[: len(scalars)], refs[len(scalars) :][:count])
+        s_ref, wu_ref, wd_ref, g_ref, z_ref, d_ref = refs[len(scalars) + count :]
         for at in range(0, half, step):
-            here = slice(at, at + step)
+            g_ref[at : at + step, :] = read(which, at, step)
+        for at in range(0, half, half // 2):
+            here = slice(at, at + half // 2)
             grad = mm_nt(g_ref[here, :], wd_ref[...]) * s_ref[here, :].astype(F32)
             grad = grad.astype(BF16)
             d_ref[here, :] = grad
@@ -233,13 +305,15 @@
 
     return run(
         body,
-        [((half, width), out_type), ((half, hidden), BF16)],
-        (g, slope, w_up, w_down),
+        [((half, width), BF16), ((half, width), out_type), ((half, hidden), BF16)],
+        (*scalars, *arrays, slope, w_up, w_down),
+        scalars=len(scalars),
         flops=4 * half * width * hidden,
-    )
-
-
-def middle_back(g, h, own, arrived, gain, quarter):
+        after=after,
+    )
+
+
+def middle_back(g, h, own, arrived, gain, after=()):
     half, width = g.shape
     parts = len(arrived) + 1
     rows = half // parts
@@ -247,12 +321,13 @@
     def body(g_ref, h_ref, own_ref, *refs):
         got = refs[: parts - 1]
         gain_ref, d_ref, low_ref, sums_ref = refs[parts - 1 :]
-        for p in range(parts):
-            here = slice(p * rows, (p + 1) * rows)
+        def step(i, sums):
+            at = pl.multiple_of(i * STEP, 16)
+            here = pl.ds(at, STEP)
             grad = own_ref[here, :].astype(F32)
             for shift, ref in enumerate(got, 1):
-                there = (p + shift) % parts
-                grad = grad + ref[there * rows : (there + 1) * rows, :].astype(F32)
+                there = pl.multiple_of(lax.rem(at + shift * rows, half), 16)
+                grad = grad + ref[pl.ds(there, STEP), :].astype(F32)
             unit, inverse = unit_rows(h_ref[here, :])
             scaled = grad * gain_ref[...]
             first = jnp.mean(scaled, 1, keepdims=True)
@@ -262,23 +337,21 @@
             d_ref[here, :] = total
             low = total.astype(BF16)
             low_ref[here, :] = low
-            if p == 0:
-                sums_ref[...] = jnp.concatenate(
-                    [
-                        jnp.sum(grad * unit, 0, keepdims=True),
-                        jnp.sum(grad, 0, keepdims=True),
-                        jnp.sum(upstream, 0, keepdims=True),
-                        jnp.sum(low.astype(F32), 0, keepdims=True),
-                        jnp.zeros((4, width), F32),
-                    ],
-                    axis=0,
-                )
+            terms = (grad * unit, grad, upstream, low.astype(F32))
+            return tuple(a + jnp.sum(t, 0, keepdims=True) for a, t in zip(sums, terms))
+
+        zeros = (jnp.zeros((1, width), F32),) * 4
+        sums = lax.fori_loop(0, rows // STEP, step, zeros)
+        lax.fori_loop(rows // STEP, half // STEP, lambda i, c: (step(i, zeros), c)[1], 0)
+        for i in range(4):
+            sums_ref[i : i + 1, :] = sums[i]
 
     return run(
         body,
         [((half, width), F32), ((half, width), BF16), ((8, width), F32)],
         (g, h, own, *arrived, gain),
         flops=30 * half * width,
+        after=after,
     )
 
 
@@ -342,6 +415,7 @@
             pltpu.VMEM((total, total), F32),
             pltpu.VMEM((total, total), F32),
         ),
+        limit=12,
     )
 
 
@@ -363,38 +437,108 @@
     )[0]
 
 
-def start_back(xm, dh, own, arrived, gain):
+def start_back(xm, dh, own, arrived, gain, after=()):
     rows, width = own.shape
+    part = rows // pieces_of(rows)
     count = len(arrived)
 
     def body(x_ref, dh_ref, own_ref, *refs):
         got = refs[:count]
-        gain_ref, d_ref, low_ref, sums_ref = refs[count:]
-        grad = own_ref[...]
-        for ref in got:
-            grad = grad + ref[...].astype(F32)
-        unit, inverse = unit_rows(x_ref[0:rows, :].astype(F32))
-        scaled = grad * gain_ref[...]
-        first = jnp.mean(scaled, 1, keepdims=True)
-        second = jnp.mean(scaled * unit, 1, keepdims=True)
-        total = dh_ref[0:rows, :] + inverse * (scaled - first - unit * second)
-        d_ref[...] = total
-        low_ref[...] = total.astype(BF16)
-        sums_ref[...] = jnp.concatenate(
-            [
-                jnp.sum(grad * unit, 0, keepdims=True),
-                jnp.sum(grad, 0, keepdims=True),
-                jnp.zeros((6, width), F32),
-            ],
-            axis=0,
-        )
-
-    return run(
-        body,
-        [((rows, width), F32), ((rows, width), BF16), ((8, width), F32)],
+        gain_ref, d_ref, sums_ref, *low_refs = refs[count:]
+        def step(i, sums):
+            here = pl.ds(pl.multiple_of(i * STEP, 16), STEP)
+            grad = own_ref[here, :]
+            for ref in got:
+                grad = grad + ref[here, :].astype(F32)
+            unit, inverse = unit_rows(x_ref[here, :].astype(F32))
+            scaled = grad * gain_ref[...]
+            first = jnp.mean(scaled, 1, keepdims=True)
+            second = jnp.mean(scaled * unit, 1, keepdims=True)
+            total = dh_ref[here, :] + inverse * (scaled - first - unit * second)
+            d_ref[here, :] = total
+            return tuple(
+                a + jnp.sum(t, 0, keepdims=True) for a, t in zip(sums, (grad * unit, grad))
+            )
+
+        sums = lax.fori_loop(0, rows // STEP, step, (jnp.zeros((1, width), F32),) * 2)
+        for i in range(2):
+            sums_ref[i : i + 1, :] = sums[i]
+        for i, ref in enumerate(low_refs):
+            ref[...] = d_ref[i * part : (i + 1) * part, :].astype(BF16)
+
+    d, sums, *low = run(
+        body,
+        [((rows, width), F32), ((8, width), F32)]
+        + [((part, width), BF16)] * (rows // part),
         (xm, dh, own, *arrived, gain),
         flops=30 * rows * width,
-    )
+        after=after,
+    )
+    return d, low, sums
+
+
+def finish_rows(hidden, total, arrived, out_bias, after=()):
+    rows, width = total[0].shape
+    part = rows // pieces_of(rows)
+
+    def body(h_ref, total_ref, *refs):
+        bias_ref, y_ref, *low_refs = refs[len(arrived) :]
+        value = total_ref[...]
+        for ref in refs[: len(arrived)]:
+            value = value + ref[...].astype(F32)
+        value = h_ref[0:rows, :] + value + bias_ref[...]
+        y_ref[...] = value
+        for i, ref in enumerate(low_refs):
+            ref[...] = value[i * part : (i + 1) * part, :].astype(BF16)
+
+    y, *low = run(
+        body,
+        [((rows, width), F32)] + [((part, width), BF16)] * (rows // part),
+        (hidden, total[0], *arrived, out_bias),
+        flops=4 * rows * width,
+        after=after,
+    )
+    return y, low
+
+
+def outer(pairs, low, high, after=()):
+    width = pairs[0][1].shape[1]
+
+    def body(*refs):
+        out = refs[-1]
+        total = None
+        for i in range(len(pairs)):
+            term = mm_tn(refs[2 * i][:, low:high], refs[2 * i + 1][...])
+            total = term if total is None else total + term
+        out[...] = total.astype(BF16)
+
+    return run(
+        body,
+        [((high - low, width), BF16)],
+        [array for pair in pairs for array in pair],
+        flops=2 * (high - low) * width * sum(pair[0].shape[0] for pair in pairs),
+        limit=16,
+        after=after,
+    )[0]
+
+
+def add(left, right, after=()):
+    def body(left_ref, right_ref, out):
+        out[...] = (left_ref[...].astype(F32) + right_ref[...].astype(F32)).astype(BF16)
+
+    return run(body, [(left.shape, BF16)], (left, right), flops=left.size, after=after)[0]
+
+
+def hold(arrays, after):
+    count = len(arrays)
+    anywhere = pl.BlockSpec(memory_space=pl.ANY)
+    return pl.pallas_call(
+        lambda *refs: None,
+        out_shape=[jax.ShapeDtypeStruct(a.shape, a.dtype) for a in arrays],
+        in_specs=[anywhere] * (count + len(after)),
+        out_specs=[anywhere] * count,
+        input_output_aliases={i: i for i in range(count)},
+    )(*arrays, *after)
 
 
 def core_swap(value):
@@ -416,11 +560,27 @@
     return mine, [core_swap(b) for b in mine]
 
 
-def sum_blocks(half, chips):
-    rows = half.shape[0] // chips
-    return half[:rows], [
-        chip_shift(half[p * rows : (p + 1) * rows].astype(BF16), p) for p in range(1, chips)
-    ]
+def hand_over(block, step, chips):
+    pieces = [spread_block(to_section(piece, step), chips) for piece in block]
+    return [[piece[i][p] for p in range(chips) for piece in pieces] for i in (0, 1)]
+
+
+def pieces_of(rows):
+    return 2 if rows % 32 == 0 and rows >= 128 else 1
+
+
+def sum_blocks(mine, other, chips):
+    rows = mine.shape[0] // chips
+
+    def body(mine_ref, other_ref, own_ref, *sends):
+        own_ref[...] = mine_ref[0:rows, :] + other_ref[0:rows, :].astype(F32)
+        for p, ref in enumerate(sends, 1):
+            here = slice(p * rows, (p + 1) * rows)
+            ref[...] = (mine_ref[here, :] + other_ref[here, :].astype(F32)).astype(BF16)
+
+    shape = (rows, mine.shape[1])
+    own, *sends = run(body, [(shape, F32)] + [(shape, BF16)] * (chips - 1), (mine, other))
+    return (own, *sends), [chip_shift(send, p) for p, send in enumerate(sends, 1)]
 
 
 def to_section(value, step):
@@ -428,44 +588,67 @@
     return lax.ppermute(value, "section", pairs)
 
 
-def forward(x, w, info, chips, save, end):
-    xm, xo = x
-    normed, q, k, v = project(
-        info, xm, xo, w["gain"][0], w["bias"][0], w["wq"], w["bq"], w["wk"], w["wv"], w["bv"]
-    )
-    half = xm.shape[0]
+class Turns:
+    def __init__(self):
+        self.last = ()
+
+    def take(self):
+        return self.last
+
+    def end(self, *arrays):
+        self.last = tuple(arrays)
+
+
+def forward(source, w, info, chips, rows, save, turns):
+    xm, normed, q, k, v = project(
+        info, source, w["gain"][0], w["bias"][0], w["wq"], w["bq"], w["wk"], w["wv"], w["bv"],
+        rows, turns.take(),
+    )
+    half = rows // 2
     z_other, o_other, l_other = attend(half, q, k, v, w["wout"], BF16)
     z_other = core_swap(z_other)
     z_mine, o_mine, l_mine = attend(0, q, k, v, w["wout"], F32)
-    own = (z_mine + z_other.astype(F32)).astype(BF16)
+    own = add(z_mine, z_other)
+    turns.end(own)
+    arrived = share_half(own, chips)
+    yield
     hidden, n2m = middle(
-        xm, own, share_half(own, chips), w["out_bias"][0], w["gain"][1], w["bias"][1]
+        xm, own, arrived, w["out_bias"][0], w["gain"][1], w["bias"][1], turns.take()
     )
     n2o = core_swap(n2m)
+    mine = mlp(n2m, w["w_up"], w["b_up"], w["w_down"], F32, save)
     other = mlp(n2o, w["w_up"], w["b_up"], w["w_down"], BF16, save)
     y_other = core_swap(other[0])
-    mine = mlp(n2m, w["w_up"], w["b_up"], w["w_down"], F32, save)
-    total, arrived = sum_blocks(mine[0] + y_other.astype(F32), chips)
-    for value in arrived:
-        total = total + value.astype(F32)
-    result = hidden[: total.shape[0]] + total + w["out_bias"][1]
+    total, arrived = sum_blocks(mine[0], y_other, chips)
     saved = None
     if save:
         saved = dict(
-            x=x, normed=normed, q=q, k=k, v=v, o=(o_mine, o_other), l=(l_mine, l_other),
+            x=xm, normed=normed, q=q, k=k, v=v, o=(o_mine, o_other), l=(l_mine, l_other),
             h=hidden, n2=(n2m, n2o), m=(mine[1], other[1]), slope=(mine[2], other[2]),
         )
-    return result, saved
-
-
-def backward(g, saved, w, chips):
-    gm, go = g
-    z_other, du_other = mlp_back(go, saved["slope"][1], w["w_up"], w["w_down"], BF16)
+        turns.end(mine[2], other[2])
+        result, _ = finish_rows(hidden, total, arrived, w["out_bias"][1])
+        return result, saved
+    turns.end(*total)
+    yield
+    _, low = finish_rows(hidden, total, arrived, w["out_bias"][1], turns.take())
+    turns.end(low[0])
+    return low
+
+
+def backward(source, saved, w, chips, turns):
+    go, z_other, du_other = mlp_back(
+        1, source, saved["slope"][1], w["w_up"], w["w_down"], BF16, turns.take()
+    )
     z_other = core_swap(z_other)
-    z_mine, du_mine = mlp_back(gm, saved["slope"][0], w["w_up"], w["w_down"], F32)
-    own = (z_mine + z_other.astype(F32)).astype(BF16)
+    gm, z_mine, du_mine = mlp_back(0, source, saved["slope"][0], w["w_up"], w["w_down"], F32)
+    own = add(z_mine, z_other)
+    turns.end(own)
+    arrived = share_half(own, chips)
+    work = dict(g=(gm, go), du=(du_mine, du_other))
+    yield work
     dh, dhm, sums_two = middle_back(
-        gm, saved["h"], own, share_half(own, chips), w["gain"][1], None
+        gm, saved["h"], own, arrived, w["gain"][1], turns.take()
     )
     dho = core_swap(dhm)
     q, k, v = saved["q"], saved["k"], saved["v"]
@@ -473,28 +656,30 @@
     half = gm.shape[0]
     d_other = core_swap(project_back(half, dq, dk, dv, w["wq"], w["wk"], w["wv"], BF16))
     d_mine = project_back(0, dq, dk, dv, w["wq"], w["wk"], w["wv"], F32)
-    total, arrived = sum_blocks(d_mine + d_other.astype(F32), chips)
-    dx, dx_low, sums_one = start_back(saved["x"][0], dh, total, arrived, w["gain"][0])
-    work = dict(
-        du=(du_mine, du_other), dh=(dhm, dho), dq=dq, dk=dk, dv=dv, sums=(sums_one, sums_two)
-    )
-    return dx, dx_low, work
-
-
-def line_sum(pieces):
-    place = lax.axis_index("dp")
-    inner = (place == 1) | (place == 2)
-    results, done = [], []
-    for index, piece in enumerate(pieces):
-        if index >= 2:
-            piece, done[index - 2] = lax.optimization_barrier((piece, done[index - 2]))
-        here = piece + lax.ppermute(piece, "dp", [(0, 1), (3, 2)])
-        both = here + lax.ppermute(here, "dp", [(1, 2), (2, 1)])
-        done.append(both)
-    for both in done:
-        back = lax.ppermute(both, "dp", [(1, 0), (2, 3)])
-        results.append(jnp.where(inner, both, back))
-    return results
+    total, arrived = sum_blocks(d_mine, d_other, chips)
+    turns.end(*total)
+    work.update(dh=(dhm, dho), dq=dq, dk=dk, dv=dv)
+    yield work
+    dx, low, sums_one = start_back(saved["x"], dh, total[0], arrived, w["gain"][0], turns.take())
+    turns.end(low[0])
+    work.update(sums=(sums_one, sums_two))
+    return dx, low, work
+
+
+def step_all(steps):
+    results = [None] * len(steps)
+    live = list(range(len(steps)))
+    rounds = []
+    while live:
+        given = {}
+        for i in list(live):
+            try:
+                given[i] = next(steps[i])
+            except StopIteration as end:
+                results[i] = end.value
+                live.remove(i)
+        rounds.append(given)
+        yield results if not live else given
 
 
 def finish(value):
@@ -539,70 +724,68 @@
     rel = ((places // 2 - chip) % chips + chips * ((places + core) % 2)).astype(jnp.int32)
     info = jnp.stack([rel[size - 1] * rows + rows - pad, jnp.int32(pad)])
     images_all = micro * images
-
-    small = jnp.concatenate([norm_gain[0], norm_bias[0], out_bias[0]], axis=0)
-    small = lax.all_gather(small, "tensor", axis=1, tiled=True)
+    sources = order
+    small = jnp.concatenate(
+        [norm_gain[0], norm_bias[0], out_bias[0], jnp.zeros((2, cols), F32)], axis=0
+    )
+    high = lax.reduce_precision(small, 8, 7)
+    middle_part = lax.reduce_precision(small - high, 8, 7)
+    thirds = jnp.concatenate([high, middle_part, small - high - middle_part], axis=0)
+    features = inputs[0].reshape(images_all, length, cols).transpose(0, 2, 1)
+    full = []
+    for n in range(images_all):
+        block = features[n]
+        if n == 0:
+            block = jnp.pad(block, ((0, 0), (0, pad)))
+            block = jnp.concatenate([block, thirds.astype(BF16).T], axis=1)
+        mine, other = spread_block(block, chips)
+        halves, extras = assemble(
+            mine + other, length, sources, order, rows, 0 if n else small.shape[0]
+        )
+        full.append(halves)
+        if n == 0:
+            small = extras[0]
     w = dict(
         gain=(small[0:1], small[1:2]), bias=(small[2:3], small[3:4]),
         out_bias=(small[4:5], small[5:6]),
         wq=w_query[0].T, bq=b_query, wk=w_key[0].T, wv=w_value[0].T, bv=b_value,
         wout=w_out[0], w_up=w_up[0].T, b_up=b_up, w_down=w_down[0],
     )
-    own = jnp.pad(
-        inputs[0].reshape(images_all, length, cols), ((0, 0), (0, pad), (0, 0))
-    )
-    full = []
-    for n in range(images_all):
-        mine, other = spread_block(own[n], chips)
-        full.append(assemble(jnp.stack(mine + other), rel, order, rows))
-
-    def widen(block, base):
-        mine, other = spread_block(block, chips)
-        return (
-            select_rows(flag, base[0], mine),
-            select_rows(flag, base[1], other),
-        )
-
-    streams, results, saves = [], [], []
-    for n in range(images_all):
-        result, _ = forward(full[n], w, info, chips, False, False)
-        streams.append(widen(to_section(result.astype(BF16), 1), full[n]))
-    for n in range(images_all):
-        result, saved = forward(streams[n], w, info, chips, True, True)
-        results.append(result)
-        saves.append(saved)
-    ends, works, upstreams = [], [], []
-    for n in range(images_all):
-        _, low, _ = backward(full[n], saves[n], w, chips)
-        mine, other = spread_block(to_section(low, -1), chips)
-        flip = 1 - flag
-        upstreams.append(
-            (select_rows(flip, full[n][0], mine), select_rows(flip, full[n][1], other))
-        )
-    for n in range(images_all):
-        dx, _, work = backward(upstreams[n], saves[n], w, chips)
-        ends.append(jnp.where(first, dx, results[n]))
-        works.append(work)
-
-    def outer(pairs):
-        acc = None
-        for left, right in pairs:
-            term = lax.dot_general(
-                left, right, (((0,), (0,)), ((), ())), preferred_element_type=F32
-            )
-            acc = term if acc is None else acc + term
-        return acc.astype(BF16)
-
     span = range(images_all)
-    g_down = outer([(saves[n]["m"][i], upstreams[n][i]) for n in span for i in (0, 1)])
-    g_up = outer([(works[n]["du"][i], saves[n]["n2"][i]) for n in span for i in (0, 1)])
-    g_out = outer([(saves[n]["o"][i], works[n]["dh"][i]) for n in span for i in (0, 1)])
-    g_query = outer([(works[n]["dq"], saves[n]["normed"]) for n in span])
-    g_key = outer([(works[n]["dk"], saves[n]["normed"]) for n in span])
-    g_value = outer([(works[n]["dv"], saves[n]["normed"]) for n in span])
-    g_down, g_up, g_out, g_query, g_key, g_value = dp_sum(
-        [g_down, g_up, g_out, g_query, g_key, g_value]
-    )
+    turns = Turns()
+
+    def widen(block, step, base, chosen):
+        return Source(base, hand_over(block, step, chips), chosen)
+
+    *_, lows = step_all(
+        [forward(Source(full[n]), w, info, chips, total, False, turns) for n in span]
+    )
+    streams = [widen(lows[n], 1, full[n], flag) for n in span]
+    *_, done = step_all([forward(streams[n], w, info, chips, total, True, turns) for n in span])
+    results, saves = [d[0] for d in done], [d[1] for d in done]
+    *_, done = step_all([backward(Source(full[n]), saves[n], w, chips, turns) for n in span])
+    grads = [widen(done[n][1], -1, full[n], 1 - flag) for n in span]
+
+    steps = step_all([backward(grads[n], saves[n], w, chips, turns) for n in span])
+    works = next(steps)
+    hidden = w_up.shape[2]
+    both = (0, 1)
+    g_down = outer([(saves[n]["m"][i], works[n]["g"][i]) for n in span for i in both], 0, hidden)
+    g_up = outer(
+        [(works[n]["du"][i], saves[n]["n2"][i]) for n in span for i in both], 0, hidden,
+        (g_down,),
+    )
+    turns.end(g_down, g_up)
+    g_down, g_up = lax.psum([g_down, g_up], "dp")
+    works = next(steps)
+    width = cols * size
+    heads = b_query.shape[1]
+    rest = [outer([(saves[n]["o"][i], works[n]["dh"][i]) for n in span for i in both], 0, heads)]
+    for left in ("dq", "dk", "dv"):
+        rest.append(outer([(works[n][left], saves[n]["normed"]) for n in span], 0, heads))
+    done = next(steps)
+    works = [d[2] for d in done]
+    ends = [jnp.where(first, done[n][0], results[n]) for n in span]
 
     def total_of(parts):
         return sum(jnp.sum(p.astype(F32), 0) for p in parts)
@@ -617,17 +800,23 @@
         )
         for n in span
     )
-    wide = lax.psum(wide, ("tensor", "dp"))
+    wide = lax.psum(wide, "tensor")
     wide = lax.dynamic_slice_in_dim(wide, me * cols, cols, 1)
-    narrow = jnp.concatenate(
+    vector = jnp.concatenate(
         [
+            wide.reshape(-1),
             total_of([works[n]["dq"] for n in span]),
             total_of([works[n]["dv"] for n in span]),
-            total_of([works[n]["du"][i] for n in span for i in (0, 1)]),
+            total_of([works[n]["du"][i] for n in span for i in both]),
         ]
     )
-    narrow = lax.psum(narrow, "dp")
-    heads = b_query.shape[1]
+    count = vector.size
+    lines = -(-count // (16 * width)) * 16
+    vector = jnp.pad(vector, (0, lines * width - count)).reshape(lines, width).astype(BF16)
+    g_out, g_query, g_key, g_value, vector = lax.psum(hold([*rest, vector], (g_down,)), "dp")
+    vector = vector.astype(F32).reshape(-1)
+    wide = vector[: 6 * cols].reshape(6, cols)
+    narrow = vector[6 * cols : count]
 
     ends = jnp.stack(ends).reshape(images_all, rows, size, cols)
     ends = lax.all_to_all(ends, "tensor", split_axis=2, concat_axis=1, tiled=True)

time: 1030 us -> 713 us (0.69)
  waiting for transfers between devices: 448 us -> 277 us
  blocking collectives: 120 us -> 31.6 us
  starting transfers between devices: 118 us -> 68 us
  Pallas kernels: 192 us -> 231 us
  matrix products: 35.3 us -> 0 us
  other arithmetic: 42.2 us -> 14.7 us
  between operations: 4.2 us -> 17 us
    ppermute x22 -> x26, waiting for transfers between devices: 263 us -> 110 us  [chip_shift(): lax.ppermute(value, 'tensor', [(i, (i + 2 * shift) % size) for i in range...]
    ppermute x18 -> x0, waiting for transfers between devices: 138 us -> none  [the longest x6 70.2 us: line_sum(): here = piece + lax.ppermute(piece, 'dp', [(0, 1), (3, 2)])]
    psum x0 -> x2, waiting for transfers between devices: none -> 132 us  [the longest x1 121 us: per_device(): lax.psum(hold([*rest, vector], (g_down,)), 'dp')]
    psum x2, blocking collectives: 114 us -> 31.6 us  [the longest x1 20.3 us: per_device(): lax.psum(hold([*rest, vector], (g_down,)), 'dp')]
    ppermute x18 -> x0, starting transfers between devices: 75.5 us -> none  [the longest x6 60.6 us: line_sum(): here = piece + lax.ppermute(piece, 'dp', [(0, 1), (3, 2)])]
    pallas_call x62 -> x81, Pallas kernels: 182 us -> 221 us  [the longest x80 221 us: run(): pl.pallas_call(kernel, out_shape=[jax.ShapeDtypeStruct(shape, dtype) for...]
    dot_general x18 -> x0, matrix products: 35.3 us -> none  [outer(): lax.dot_general(left, right, (((0,), (0,)), ((), ())), preferred_element_...]
    add x23 -> x1, other arithmetic: 23.4 us -> 0.01 us  [per_device(): order = (chip + places % chips) % chips * 2 + (core + places // chips) % 2]
  transfers between devices with their start and end apart: 81 -> 81, of which waited for: 37 -> 36; matrix products, arithmetic and copies ran while one was open for 10% -> 4% of each run, Pallas kernels for 11% -> 27%
where the time goes in v2:
time: 713 us; the launch traced here: 703 us
  waiting for transfers between devices  277 us (39%)
  Pallas kernels  231 us (32%)
  starting transfers between devices  68 us (10%)
  local copies, waits for them, and re-layouts  64.1 us (9%)
  blocking collectives  31.6 us (4%)
  between operations  17 us (2%)
  other arithmetic  14.7 us (2%)
    pallas_call x80, Pallas kernels, run(): pl.pallas_call(kernel, out_shape=[jax.ShapeDtypeStruct(shape, dtype) for...  221 us
    psum x1, waiting for transfers between devices, per_device(): lax.psum(hold([*rest, vector], (g_down,)), 'dp')  121 us
    ppermute x26, waiting for transfers between devices, chip_shift(): lax.ppermute(value, 'tensor', [(i, (i + 2 * shift) % size) for i in range...  110 us
    unnamed x333, local copies, waits for them, and re-layouts  44.9 us
    ppermute x26, starting transfers between devices, chip_shift(): lax.ppermute(value, 'tensor', [(i, (i + 2 * shift) % size) for i in range...  36.8 us
    ppermute x8, waiting for transfers between devices, to_section(): return lax.ppermute(value, 'section', pairs)  26 us
    psum x1, blocking collectives, per_device(): lax.psum(hold([*rest, vector], (g_down,)), 'dp')  20.3 us
    ppermute x8, starting transfers between devices, to_section(): return lax.ppermute(value, 'section', pairs)  18.8 us
  transfers between devices with their start and end apart: 81, of which 36 were waited for; matrix products, arithmetic and copies ran while one was open for 4% of the time, Pallas kernels for 27%

profile of v2, /device:TPU:0, one launch (start us, length us, event | category | flops | bytes accessed | tf_op | source)
XLA Modules:
  0.0 702.9 jit_solution(2688289027959150031)
XLA Ops:
  12.6 12.5 %collective-permute-done.refs_3_ = bf16[288,792]{1,0:T(8,128)(2,1)S(1)} collective-permute-done((bf16[288,792]{1,0:T(8,128)(2,1)S(1)}, bf16[288,792]{1,0:T(8,128)(2,1)S(1)}, u32[]{:S(2)}, u32[]{:S(2)}) %collective-permute-start) | collective-permute-done | bytes 456224 | tf_op jit(solution)/shard_map/ppermute | solution.py:551
  25.6 8.1 %collective-permute-done.5.refs_3_ = bf16[288,729]{1,0:T(8,128)(2,1)S(1)} collective-permute-done((bf16[288,729]{1,0:T(8,128)(2,1)S(1)}, bf16[288,729]{1,0:T(8,128)(2,1)S(1)}, u32[]{:S(2)}, u32[]{:S(2)}) %collective-permute-start.5) | collective-permute-done | bytes 419936 | tf_op jit(solution)/shard_map/ppermute | solution.py:551
  69.6 6.0 collective-permute-done.4.refs_2_
  87.4 12.5 %collective-permute-done.12.refs_2_ = bf16[384,1152]{1,0:T(8,128)(2,1)S(1)} collective-permute-done((bf16[384,1152]{1,0:T(8,128)(2,1)S(1)}, bf16[384,1152]{1,0:T(8,128)(2,1)S(1)}, u32[]{:S(2)}, u32[]{:S(2)}) %collective-permute-start.12) | collective-permute-done | bytes 884768 | tf_op jit(solution)/shard_map/ppermute | solution.py:551
  153.1 5.6 shard_map.248
  172.3 5.4 shard_map.252
  204.8 6.9 collective-permute-done.36.refs_2_
  240.6 12.5 %collective-permute-done.39.refs_3_ = bf16[384,1152]{1,0:T(8,128)(2,1)S(1)} collective-permute-done((bf16[384,1152]{1,0:T(8,128)(2,1)S(1)}, bf16[384,1152]{1,0:T(8,128)(2,1)S(1)}, u32[]{:S(2)}, u32[]{:S(2)}) %collective-permute-start.39) | collective-permute-done | bytes 884768 | tf_op jit(solution)/shard_map/ppermute | solution.py:551
  258.9 8.0 %shard_map.269 = (bf16[768,288]{1,0:T(8,128)(2,1)S(1)}, bf16[768,288]{1,0:T(8,128)(2,1)S(1)}, bf16[768,288]{1,0:T(8,128)(2,1)S(1)}) custom-call(bf16[384,1152]{1,0:T(8,128)(2,1)S(1)} %get-tuple-element.202.refs_0_, bf16[384,1152]{1,0:T(8,128)(2,1)S(1)} %collective-permute-done.41.refs_1_, bf16[288,1152]{1,0:T(8,128)(2,1)S(1)} %bitcast.91, ...), custom_call_target="tpu_custom_call" | custom-call | flops 49413095424 | bytes 6144000 | tf_op jit(solution)/shard_map/pallas_call | solution.py:36
  271.3 7.2 %collective-permute-done.44.refs_3_ = bf16[384,1152]{1,0:T(8,128)(2,1)S(1)} collective-permute-done((bf16[384,1152]{1,0:T(8,128)(2,1)S(1)}, bf16[384,1152]{1,0:T(8,128)(2,1)S(1)}, u32[]{:S(2)}, u32[]{:S(2)}) %collective-permute-start.44) | collective-permute-done | bytes 884768 | tf_op jit(solution)/shard_map/ppermute | solution.py:551
  284.6 8.0 %shard_map.274 = (bf16[768,288]{1,0:T(8,128)(2,1)S(1)}, bf16[768,288]{1,0:T(8,128)(2,1)S(1)}, bf16[768,288]{1,0:T(8,128)(2,1)S(1)}) custom-call(bf16[384,1152]{1,0:T(8,128)(2,1)S(1)} %get-tuple-element.212.refs_0_, bf16[384,1152]{1,0:T(8,128)(2,1)S(1)} %collective-permute-done.45.refs_1_, bf16[288,1152]{1,0:T(8,128)(2,1)S(1)} %bitcast.92, ...), custom_call_target="tpu_custom_call" | custom-call | flops 49413095424 | bytes 6144000 | tf_op jit(solution)/shard_map/pallas_call | solution.py:36
  303.6 6.0 collective-permute-done.48.refs_3_
  359.1 7.4 %shard_map.285.refs_8_.refs_5_ = bf16[1076,1152]{1,0:T(8,128)(2,1)} custom-call(bf16[384,1076]{1,0:T(8,128)(2,1)S(1)} %get-tuple-element.227.refs_0_, bf16[384,1152]{1,0:T(8,128)(2,1)S(1)} %get-tuple-element.222.refs_1_.refs_0_, bf16[384,1076]{1,0:T(8,128)(2,1)S(1)} %get-tuple-element.228.refs_2_, bf16[384,1152]{1,0:T(8,128)(2,1)S(1)} %get-tuple-element.229.refs_3_, ...), custom_call_target="tpu_custom_call" | custom-call | flops 53310652416 | bytes 9323520 | tf_op jit(solution)/shard_map/pallas_call | solution.py:36
  375.8 5.7 shard_map.286.refs_6_
  397.0 9.2 %shard_map.288 = (bf16[768,288]{1,0:T(8,128)(2,1)S(1)}, bf16[768,288]{1,0:T(8,128)(2,1)S(1)}, bf16[768,288]{1,0:T(8,128)(2,1)S(1)}) custom-call(bf16[384,1152]{1,0:T(8,128)(2,1)S(1)} %copy-done.93, bf16[384,1152]{1,0:T(8,128)(2,1)} %collective-permute-done.66.refs_1_.refs_3_, bf16[288,1152]{1,0:T(8,128)(2,1)S(1)} %bitcast.93, ...), custom_call_target="tpu_custom_call" | custom-call | flops 49413095424 | bytes 6144000 | tf_op jit(solution)/shard_map/pallas_call | solution.py:36
  410.5 7.1 %collective-permute-done.70.refs_3_ = bf16[384,1152]{1,0:T(8,128)(2,1)S(1)} collective-permute-done((bf16[384,1152]{1,0:T(8,128)(2,1)S(1)}, bf16[384,1152]{1,0:T(8,128)(2,1)S(1)}, u32[]{:S(2)}, u32[]{:S(2)}) %collective-permute-start.70) | collective-permute-done | bytes 884768 | tf_op jit(solution)/shard_map/ppermute | solution.py:551
  424.6 8.0 %shard_map.294 = (bf16[768,288]{1,0:T(8,128)(2,1)S(1)}, bf16[768,288]{1,0:T(8,128)(2,1)S(1)}, bf16[768,288]{1,0:T(8,128)(2,1)S(1)}) custom-call(bf16[384,1152]{1,0:T(8,128)(2,1)S(1)} %get-tuple-element.248.refs_0_.refs_5_, bf16[384,1152]{1,0:T(8,128)(2,1)S(1)} %collective-permute-done.71.refs_1_.refs_7_, bf16[288,1152]{1,0:T(8,128)(2,1)S(1)} %bitcast.94, ...), custom_call_target="tpu_custom_call" | custom-call | flops 49413095424 | bytes 6144000 | tf_op jit(solution)/shard_map/pallas_call | solution.py:36
  453.8 6.2 collective-permute-done.75.refs_3_
  468.0 11.3 %psum.56 = bf16[6,1152]{1,0:T(8,128)(2,1)S(1)} all-reduce(f32[6,1152]{1,0:T(8,128)S(1)} %add.106), channel_id=1, replica_groups=mesh['section'=2,'tensor'=4,'dp'=4] {'tensor'}, use_global_device_ids=true, to_apply=%region_0.1 | all-reduce | flops 6912 | bytes 41472 | tf_op jit(solution)/shard_map/psum | solution.py:803
  482.3 11.4 %all-reduce.6.cloned.1.call-done.refs_5_.value_ref = bf16[1076,1152]{1,0:T(8,128)(2,1)} async-done(((bf16[1076,1152]{1,0:T(8,128)(2,1)}), bf16[1076,1152]{1,0:T(8,128)(2,1)}) %all-reduce.6.cloned.1.call-update) | async-done | bytes 2479120 | tf_op jit(solution)/shard_map/psum | solution.py:779
  499.4 10.4 %collective-permute-done.74.refs_2_ = bf16[192,1152]{1,0:T(8,128)(2,1)S(1)} collective-permute-done((bf16[192,1152]{1,0:T(8,128)(2,1)S(1)}, bf16[192,1152]{1,0:T(8,128)(2,1)S(1)}, u32[]{:S(2)}, u32[]{:S(2)}) %collective-permute-start.74) | collective-permute-done | bytes 442400 | tf_op jit(solution)/shard_map/ppermute | solution.py:551
  510.6 7.8 %collective-permute-done.77.refs_2_ = bf16[192,1152]{1,0:T(8,128)(2,1)S(1)} collective-permute-done((bf16[192,1152]{1,0:T(8,128)(2,1)S(1)}, bf16[192,1152]{1,0:T(8,128)(2,1)S(1)}, u32[]{:S(2)}, u32[]{:S(2)}) %collective-permute-start.77) | collective-permute-done | bytes 442400 | tf_op jit(solution)/shard_map/ppermute | solution.py:551
  532.2 20.3 %psum.58 = bf16[16,1152]{1,0:T(8,128)(2,1)S(1)} all-reduce(bf16[16,1152]{1,0:T(8,128)(2,1)S(1)} %copy-done.165), channel_id=1, replica_groups=mesh['section'=2,'tensor'=4,'dp'=4] {'dp'}, use_global_device_ids=true, to_apply=%region_10.11 | all-reduce | flops 18432 | bytes 73728 | tf_op jit(solution)/shard_map/psum | solution.py:816
  564.7 120.7 %all-reduce.8.cloned.1.call-done = (bf16[1,1152,288]{1,2,0:T(8,128)(2,1)}, bf16[1,1152,288]{1,2,0:T(8,128)(2,1)}, bf16[1,1152,288]{1,2,0:T(8,128)(2,1)}, bf16[1,288,1152]{2,1,0:T(8,128)(2,1)}, bf16[1076,1152]{1,0:T(8,128)(2,1)}) async-done(((bf16[1,1152,288]{1,2,0:T(8,128)(2,1)}, bf16[1,1152,288]{1,2,0:T(8,128)(2,1)}, bf16[1,1152,288]{1,2,0:T(8,128)(2,1)}, bf16[1,288,1152]{2,1,0:T(8,128)(2,1)}, ...) | async-done | bytes 5133328 | tf_op jit(solution)/shard_map/psum | solution.py:816
  (611 shorter events, 361.7 us)
Async XLA Ops:
  12.5 21.2 %collective-permute-start.5 = (bf16[288,729]{1,0:T(8,128)(2,1)S(1)}, bf16[288,729]{1,0:T(8,128)(2,1)S(1)}, u32[]{:S(2)}, u32[]{:S(2)}) collective-permute-start(bf16[288,729]{1,0:T(8,128)(2,1)S(1)} %get-tuple-element.302.refs_2_), channel_id=1, source_target_pairs={{0,8},{4,12},{8,0},{12,4},{1,9},{5,13},{9,1},{13,5},{2,10},{6,14},... | collective-permute-start | bytes 1259720 | tf_op jit(solution)/shard_map/ppermute | solution.py:551
  12.5 25.0 %collective-permute-start.1 = (bf16[288,792]{1,0:T(8,128)(2,1)S(1)}, bf16[288,792]{1,0:T(8,128)(2,1)S(1)}, u32[]{:S(2)}, u32[]{:S(2)}) collective-permute-start(bf16[288,792]{1,0:T(8,128)(2,1)S(1)} %fusion.1.refs_2_), channel_id=1, source_target_pairs={{0,4},{4,0},{8,12},{12,8},{1,5},{5,1},{9,13},{13,9},{2,6},{6,2},{1... | collective-permute-start | bytes 1368584 | tf_op jit(solution)/shard_map/ppermute | solution.py:546
  53.7 21.9 %collective-permute-start.4 = (bf16[384,1152]{1,0:T(8,128)(2,1)S(1)}, bf16[384,1152]{1,0:T(8,128)(2,1)S(1)}, u32[]{:S(2)}, u32[]{:S(2)}) collective-permute-start(bf16[384,1152]{1,0:T(8,128)(2,1)S(1)} %shard_map.232.refs_10_.refs_1_), channel_id=1, source_target_pairs={{0,8},{4,12},{8,0},{12,4},{1,9},{5,13},{9,1},{13,5},{2,10},{6,14},... | collective-permute-start | bytes 2654216 | tf_op jit(solution)/shard_map/ppermute | solution.py:551
  77.8 22.1 %collective-permute-start.12 = (bf16[384,1152]{1,0:T(8,128)(2,1)S(1)}, bf16[384,1152]{1,0:T(8,128)(2,1)S(1)}, u32[]{:S(2)}, u32[]{:S(2)}) collective-permute-start(bf16[384,1152]{1,0:T(8,128)(2,1)S(1)} %shard_map.237.refs_6_.refs_1_), channel_id=1, source_target_pairs={{0,8},{4,12},{8,0},{12,4},{1,9},{5,13},{9,1},{13,5},{2,10},{6,14},... | collective-permute-start | bytes 2654216 | tf_op jit(solution)/shard_map/ppermute | solution.py:551
  111.5 18.7 %collective-permute-start.23 = (bf16[192,1152]{1,0:T(8,128)(2,1)S(1)}, bf16[192,1152]{1,0:T(8,128)(2,1)S(1)}, u32[]{:S(2)}, u32[]{:S(2)}) collective-permute-start(bf16[192,1152]{1,0:T(8,128)(2,1)S(1)} %get-tuple-element.171.refs_5_), channel_id=1, source_target_pairs={{0,8},{4,12},{8,0},{12,4},{1,9},{5,13},{9,1},{13,5},{2,10},{6,14},... | collective-permute-start | bytes 1327112 | tf_op jit(solution)/shard_map/ppermute | solution.py:551
  130.1 16.6 %collective-permute-start.19 = (bf16[96,1152]{1,0:T(8,128)(2,1)}, bf16[96,1152]{1,0:T(8,128)(2,1)}, u32[]{:S(2)}, u32[]{:S(2)}) collective-permute-start(bf16[96,1152]{1,0:T(8,128)(2,1)} %collective-permute-done.15.refs_3_), channel_id=1, source_target_pairs={{0,4},{4,0},{8,12},{12,8},{1,5},{5,1},{9,13},{13,9},{2,6},{6,2},{1... | collective-permute-start | bytes 663560 | tf_op jit(solution)/shard_map/ppermute | solution.py:546
  141.8 23.5 %collective-permute-start.29 = (bf16[96,1152]{1,0:T(8,128)(2,1)}, bf16[96,1152]{1,0:T(8,128)(2,1)S(1)}, u32[]{:S(2)}, u32[]{:S(2)}) collective-permute-start(bf16[96,1152]{1,0:T(8,128)(2,1)} %collective-permute-done.27.refs_4_), channel_id=1, source_target_pairs={{0,8},{4,12},{8,0},{12,4},{1,9},{5,13},{9,1},{13,5},{2,10},{6,14},... | collective-permute-start | bytes 663560 | tf_op jit(solution)/shard_map/ppermute | solution.py:551
  146.2 19.6 %collective-permute-start.28 = (bf16[96,1152]{1,0:T(8,128)(2,1)}, bf16[96,1152]{1,0:T(8,128)(2,1)S(1)}, u32[]{:S(2)}, u32[]{:S(2)}) collective-permute-start(bf16[96,1152]{1,0:T(8,128)(2,1)} %collective-permute-done.26.refs_3_), channel_id=1, source_target_pairs={{0,8},{4,12},{8,0},{12,4},{1,9},{5,13},{9,1},{13,5},{2,10},{6,14},... | collective-permute-start | bytes 663560 | tf_op jit(solution)/shard_map/ppermute | solution.py:551
  170.7 22.4 %collective-permute-start.25 = (bf16[384,1152]{1,0:T(8,128)(2,1)S(1)}, bf16[384,1152]{1,0:T(8,128)(2,1)S(1)}, u32[]{:S(2)}, u32[]{:S(2)}) collective-permute-start(bf16[384,1152]{1,0:T(8,128)(2,1)S(1)} %shard_map.251.refs_19_.refs_1_), channel_id=1, source_target_pairs={{0,8},{4,12},{8,0},{12,4},{1,9},{5,13},{9,1},{13,5},{2,10},{6,14},... | collective-permute-start | bytes 2654216 | tf_op jit(solution)/shard_map/ppermute | solution.py:551
  188.6 23.0 %collective-permute-start.36 = (bf16[384,1152]{1,0:T(8,128)(2,1)S(1)}, bf16[384,1152]{1,0:T(8,128)(2,1)S(1)}, u32[]{:S(2)}, u32[]{:S(2)}) collective-permute-start(bf16[384,1152]{1,0:T(8,128)(2,1)S(1)} %shard_map.255.refs_6_.refs_1_), channel_id=1, source_target_pairs={{0,8},{4,12},{8,0},{12,4},{1,9},{5,13},{9,1},{13,5},{2,10},{6,14},... | collective-permute-start | bytes 2654216 | tf_op jit(solution)/shard_map/ppermute | solution.py:551
  231.5 21.6 %collective-permute-start.39 = (bf16[384,1152]{1,0:T(8,128)(2,1)S(1)}, bf16[384,1152]{1,0:T(8,128)(2,1)S(1)}, u32[]{:S(2)}, u32[]{:S(2)}) collective-permute-start(bf16[384,1152]{1,0:T(8,128)(2,1)S(1)} %shard_map.264.refs_4_.refs_2_), channel_id=1, source_target_pairs={{0,8},{4,12},{8,0},{12,4},{1,9},{5,13},{9,1},{13,5},{2,10},{6,14},... | collective-permute-start | bytes 2654216 | tf_op jit(solution)/shard_map/ppermute | solution.py:551
  256.4 22.1 %collective-permute-start.44 = (bf16[384,1152]{1,0:T(8,128)(2,1)S(1)}, bf16[384,1152]{1,0:T(8,128)(2,1)S(1)}, u32[]{:S(2)}, u32[]{:S(2)}) collective-permute-start(bf16[384,1152]{1,0:T(8,128)(2,1)S(1)} %shard_map.267.refs_5_.refs_2_), channel_id=1, source_target_pairs={{0,8},{4,12},{8,0},{12,4},{1,9},{5,13},{9,1},{13,5},{2,10},{6,14},... | collective-permute-start | bytes 2654216 | tf_op jit(solution)/shard_map/ppermute | solution.py:551
  302.1 22.0 %collective-permute-start.55 = (bf16[192,1152]{1,0:T(8,128)(2,1)S(1)}, bf16[192,1152]{1,0:T(8,128)(2,1)S(1)}, u32[]{:S(2)}, u32[]{:S(2)}) collective-permute-start(bf16[192,1152]{1,0:T(8,128)(2,1)S(1)} %get-tuple-element.219.refs_6_), channel_id=1, source_target_pairs={{0,8},{4,12},{8,0},{12,4},{1,9},{5,13},{9,1},{13,5},{2,10},{6,14},... | collective-permute-start | bytes 1327112 | tf_op jit(solution)/shard_map/ppermute | solution.py:551
  315.4 27.0 %collective-permute-start.51 = (bf16[96,1152]{1,0:T(8,128)(2,1)S(1)}, bf16[96,1152]{1,0:T(8,128)(2,1)S(1)}, u32[]{:S(2)}, u32[]{:S(2)}) collective-permute-start(bf16[96,1152]{1,0:T(8,128)(2,1)S(1)} %collective-permute-done.47.refs_2_), channel_id=1, source_target_pairs={{0,4},{4,0},{8,12},{12,8},{1,5},{5,1},{9,13},{13,9},{2,6},{6,2},{1... | collective-permute-start | bytes 663560 | tf_op jit(solution)/shard_map/ppermute | solution.py:546
  319.9 22.5 %collective-permute-start.54 = (bf16[96,1152]{1,0:T(8,128)(2,1)S(1)}, bf16[96,1152]{1,0:T(8,128)(2,1)S(1)}, u32[]{:S(2)}, u32[]{:S(2)}) collective-permute-start(bf16[96,1152]{1,0:T(8,128)(2,1)S(1)} %collective-permute-done.50.refs_5_), channel_id=1, source_target_pairs={{0,4},{4,0},{8,12},{12,8},{1,5},{5,1},{9,13},{13,9},{2,6},{6,2},{1... | collective-permute-start | bytes 663560 | tf_op jit(solution)/shard_map/ppermute | solution.py:546
  324.0 18.3 %collective-permute-start.53 = (bf16[96,1152]{1,0:T(8,128)(2,1)S(1)}, bf16[96,1152]{1,0:T(8,128)(2,1)S(1)}, u32[]{:S(2)}, u32[]{:S(2)}) collective-permute-start(bf16[96,1152]{1,0:T(8,128)(2,1)S(1)} %collective-permute-done.49.refs_4_), channel_id=1, source_target_pairs={{0,4},{4,0},{8,12},{12,8},{1,5},{5,1},{9,13},{13,9},{2,6},{6,2},{1... | collective-permute-start | bytes 663560 | tf_op jit(solution)/shard_map/ppermute | solution.py:546
  352.1 29.4 %collective-permute-start.57 = (bf16[384,1152]{1,0:T(8,128)(2,1)S(1)}, bf16[384,1152]{1,0:T(8,128)(2,1)}, u32[]{:S(2)}, u32[]{:S(2)}) collective-permute-start(bf16[384,1152]{1,0:T(8,128)(2,1)S(1)} %shard_map.282.refs_9_.refs_2_), channel_id=1, source_target_pairs={{0,8},{4,12},{8,0},{12,4},{1,9},{5,13},{9,1},{13,5},{2,10},{6,14},... | collective-permute-start | bytes 2654216 | tf_op jit(solution)/shard_map/ppermute | solution.py:551
  358.8 35.4 %collective-permute-start.69 = (bf16[384,1152]{1,0:T(8,128)(2,1)}, bf16[384,1152]{1,0:T(8,128)(2,1)}, u32[]{:S(2)}, u32[]{:S(2)}) collective-permute-start(bf16[384,1152]{1,0:T(8,128)(2,1)} %get-tuple-element.247), channel_id=1, source_target_pairs={{0,4},{4,0},{8,12},{12,8},{1,5},{5,1},{9,13},{13,9},{2,6},{6,2},{1... | collective-permute-start | bytes 2654216 | tf_op jit(solution)/shard_map/ppermute | solution.py:546
  389.7 104.0 %all-reduce.6.cloned.1.call-start = ((), (), s32[]{:S(2)}) async-start(), calls=%async_computation.1 | async-start | bytes 4976640 | tf_op jit(solution)/shard_map/psum | solution.py:779
  393.7 291.6 %all-reduce.8.cloned.1.call-start = ((), (), s32[]{:S(2)}) async-start(), calls=%async_computation.2 | async-start | bytes 10285056 | tf_op jit(solution)/shard_map/psum | solution.py:816
  395.8 21.8 %collective-permute-start.70 = (bf16[384,1152]{1,0:T(8,128)(2,1)S(1)}, bf16[384,1152]{1,0:T(8,128)(2,1)S(1)}, u32[]{:S(2)}, u32[]{:S(2)}) collective-permute-start(bf16[384,1152]{1,0:T(8,128)(2,1)S(1)} %shard_map.292.refs_2_), channel_id=1, source_target_pairs={{0,8},{4,12},{8,0},{12,4},{1,9},{5,13},{9,1},{13,5},{2,10},{6,14},... | collective-permute-start | bytes 2654216 | tf_op jit(solution)/shard_map/ppermute | solution.py:551
  422.5 25.6 %collective-permute-start.68 = (bf16[192,1152]{1,0:T(8,128)(2,1)S(1)}, bf16[192,1152]{1,0:T(8,128)(2,1)S(1)}, u32[]{:S(2)}, u32[]{:S(2)}) collective-permute-start(bf16[192,1152]{1,0:T(8,128)(2,1)S(1)} %get-tuple-element.245.refs_6_), channel_id=1, source_target_pairs={{0,8},{4,12},{8,0},{12,4},{1,9},{5,13},{9,1},{13,5},{2,10},{6,14},... | collective-permute-start | bytes 1327112 | tf_op jit(solution)/shard_map/ppermute | solution.py:551
  498.4 20.1 %collective-permute-start.77 = (bf16[192,1152]{1,0:T(8,128)(2,1)S(1)}, bf16[192,1152]{1,0:T(8,128)(2,1)S(1)}, u32[]{:S(2)}, u32[]{:S(2)}) collective-permute-start(bf16[192,1152]{1,0:T(8,128)(2,1)S(1)} %get-tuple-element.266), channel_id=1, source_target_pairs={{0,8},{4,12},{8,0},{12,4},{1,9},{5,13},{9,1},{13,5},{2,10},{6,14},... | collective-permute-start | bytes 1327112 | tf_op jit(solution)/shard_map/ppermute | solution.py:551
  522.9 33.2 %all-to-all-start = ((f32[2,192,4,288]{3,1,0,2:T(8,128)}), f32[2,192,4,288]{3,1,0,2:T(8,128)}, u32[]{:S(2)}, u32[]{:S(2)}) async-start(f32[2,192,4,288]{3,1,0,2:T(8,128)} %pad_maximum_fusion), calls=%async_computation | async-start | bytes 4718592 | tf_op jit(solution)/shard_map/all_to_all | solution.py:822
  (223 other events, 2388.1 us)
Sparse Core Ops, SparseCore 0:
  393.9 99.7 all-reduce.5
  497.6 187.7 all-reduce.7

commit v3 on v2

--- a/solution.py
+++ b/solution.py
@@ -24,11 +24,11 @@
 SMEM = pl.BlockSpec(memory_space=pltpu.SMEM)
 
 
-def run(body, outs, args, scalars=0, flops=0, scratch=(), limit=LIMIT, after=()):
+def run(body, outs, args, scalars=0, flops=0, scratch=(), limit=LIMIT, after=(), near=()):
     bytes_accessed = sum(a.size * a.dtype.itemsize for a in args) + sum(
         jnp.dtype(dtype).itemsize * shape[0] * shape[1] for shape, dtype in outs
     )
-    count, extra = len(args), len(after)
+    count, extra = len(args), len(near) + len(after)
 
     def kernel(*refs):
         body(*refs[:count], *refs[count + extra :])
@@ -38,14 +38,15 @@
         out_shape=[jax.ShapeDtypeStruct(shape, dtype) for shape, dtype in outs],
         in_specs=[SMEM] * scalars
         + [VMEM] * (count - scalars)
-        + [pl.BlockSpec(memory_space=pl.ANY)] * extra,
+        + [VMEM] * len(near)
+        + [pl.BlockSpec(memory_space=pl.ANY)] * len(after),
         out_specs=[VMEM] * len(outs),
         scratch_shapes=list(scratch),
         compiler_params=pltpu.CompilerParams(vmem_limit_bytes=limit * 2**20),
         cost_estimate=pl.CostEstimate(
             flops=int(flops) * COST, bytes_accessed=int(bytes_accessed), transcendentals=0
         ),
-    )(*args, *after)
+    )(*args, *near, *after)
 
 
 def mm(left, right):
@@ -140,6 +141,20 @@
             return value
 
         return read
+
+
+def collect(source, rows, width):
+    half = rows // 2
+    scalars, arrays = source.operands((0, 1))
+
+    def body(*refs):
+        read = source.reader((0, 1), refs[: len(scalars)], refs[len(scalars) : -2])
+        for i, out in enumerate(refs[-2:]):
+            for at in range(0, half, STEP):
+                out[at : at + STEP, :] = read(i, at, STEP)
+
+    shape = ((half, width), BF16)
+    return run(body, [shape, shape], (*scalars, *arrays), scalars=len(scalars), flops=rows * width)
 
 
 def project(info, source, gain, bias, wq, bq, wk, wv, bv, rows, after=()):
@@ -439,12 +454,11 @@
 
 def start_back(xm, dh, own, arrived, gain, after=()):
     rows, width = own.shape
-    part = rows // pieces_of(rows)
     count = len(arrived)
 
     def body(x_ref, dh_ref, own_ref, *refs):
         got = refs[:count]
-        gain_ref, d_ref, sums_ref, *low_refs = refs[count:]
+        gain_ref, d_ref, low_ref, sums_ref = refs[count:]
         def step(i, sums):
             here = pl.ds(pl.multiple_of(i * STEP, 16), STEP)
             grad = own_ref[here, :]
@@ -456,6 +470,7 @@
             second = jnp.mean(scaled * unit, 1, keepdims=True)
             total = dh_ref[here, :] + inverse * (scaled - first - unit * second)
             d_ref[here, :] = total
+            low_ref[here, :] = total.astype(BF16)
             return tuple(
                 a + jnp.sum(t, 0, keepdims=True) for a, t in zip(sums, (grad * unit, grad))
             )
@@ -463,42 +478,35 @@
         sums = lax.fori_loop(0, rows // STEP, step, (jnp.zeros((1, width), F32),) * 2)
         for i in range(2):
             sums_ref[i : i + 1, :] = sums[i]
-        for i, ref in enumerate(low_refs):
-            ref[...] = d_ref[i * part : (i + 1) * part, :].astype(BF16)
-
-    d, sums, *low = run(
-        body,
-        [((rows, width), F32), ((8, width), F32)]
-        + [((part, width), BF16)] * (rows // part),
+
+    return run(
+        body,
+        [((rows, width), F32), ((rows, width), BF16), ((8, width), F32)],
         (xm, dh, own, *arrived, gain),
         flops=30 * rows * width,
         after=after,
     )
-    return d, low, sums
 
 
 def finish_rows(hidden, total, arrived, out_bias, after=()):
     rows, width = total[0].shape
-    part = rows // pieces_of(rows)
 
     def body(h_ref, total_ref, *refs):
-        bias_ref, y_ref, *low_refs = refs[len(arrived) :]
+        bias_ref, y_ref, low_ref = refs[len(arrived) :]
         value = total_ref[...]
         for ref in refs[: len(arrived)]:
             value = value + ref[...].astype(F32)
         value = h_ref[0:rows, :] + value + bias_ref[...]
         y_ref[...] = value
-        for i, ref in enumerate(low_refs):
-            ref[...] = value[i * part : (i + 1) * part, :].astype(BF16)
-
-    y, *low = run(
-        body,
-        [((rows, width), F32)] + [((part, width), BF16)] * (rows // part),
+        low_ref[...] = value.astype(BF16)
+
+    return run(
+        body,
+        [((rows, width), F32), ((rows, width), BF16)],
         (hidden, total[0], *arrived, out_bias),
         flops=4 * rows * width,
         after=after,
     )
-    return y, low
 
 
 def outer(pairs, low, high, after=()):
@@ -561,12 +569,13 @@
 
 
 def hand_over(block, step, chips):
-    pieces = [spread_block(to_section(piece, step), chips) for piece in block]
-    return [[piece[i][p] for p in range(chips) for piece in pieces] for i in (0, 1)]
-
-
-def pieces_of(rows):
-    return 2 if rows % 32 == 0 and rows >= 128 else 1
+    size = lax.axis_size("tensor")
+    source, target = (0, size) if step > 0 else (size, 0)
+    mine = []
+    for p in range(chips):
+        pairs = [(source + (i + 2 * p) % size, target + i) for i in range(size)]
+        mine.append(lax.ppermute(block, ("section", "tensor"), pairs))
+    return [mine, [core_swap(b) for b in mine]]
 
 
 def sum_blocks(mine, other, chips):
@@ -583,14 +592,9 @@
     return (own, *sends), [chip_shift(send, p) for p, send in enumerate(sends, 1)]
 
 
-def to_section(value, step):
-    pairs = [(0, 1)] if step > 0 else [(1, 0)]
-    return lax.ppermute(value, "section", pairs)
-
-
 class Turns:
     def __init__(self):
-        self.last = ()
+        self.last, self.first = (), ()
 
     def take(self):
         return self.last
@@ -600,10 +604,12 @@
 
 
 def forward(source, w, info, chips, rows, save, turns):
+    source = source()
     xm, normed, q, k, v = project(
         info, source, w["gain"][0], w["bias"][0], w["wq"], w["bq"], w["wk"], w["wv"], w["bv"],
         rows, turns.take(),
     )
+    turns.first = (q,)
     half = rows // 2
     z_other, o_other, l_other = attend(half, q, k, v, w["wout"], BF16)
     z_other = core_swap(z_other)
@@ -632,14 +638,16 @@
     turns.end(*total)
     yield
     _, low = finish_rows(hidden, total, arrived, w["out_bias"][1], turns.take())
-    turns.end(low[0])
-    return low
-
-
-def backward(source, saved, w, chips, turns):
+    turns.end(low)
+    return hand_over(low, 1, chips)
+
+
+def backward(source, saved, w, chips, turns, pass_on):
+    source = source()
     go, z_other, du_other = mlp_back(
         1, source, saved["slope"][1], w["w_up"], w["w_down"], BF16, turns.take()
     )
+    turns.first = (go,)
     z_other = core_swap(z_other)
     gm, z_mine, du_mine = mlp_back(0, source, saved["slope"][0], w["w_up"], w["w_down"], F32)
     own = add(z_mine, z_other)
@@ -661,9 +669,9 @@
     work.update(dh=(dhm, dho), dq=dq, dk=dk, dv=dv)
     yield work
     dx, low, sums_one = start_back(saved["x"], dh, total[0], arrived, w["gain"][0], turns.take())
-    turns.end(low[0])
+    turns.end(low)
     work.update(sums=(sums_one, sums_two))
-    return dx, low, work
+    return dx, hand_over(low, -1, chips) if pass_on else None, work
 
 
 def step_all(steps):
@@ -732,19 +740,28 @@
     middle_part = lax.reduce_precision(small - high, 8, 7)
     thirds = jnp.concatenate([high, middle_part, small - high - middle_part], axis=0)
     features = inputs[0].reshape(images_all, length, cols).transpose(0, 2, 1)
-    full = []
+    spread = []
     for n in range(images_all):
         block = features[n]
         if n == 0:
             block = jnp.pad(block, ((0, 0), (0, pad)))
             block = jnp.concatenate([block, thirds.astype(BF16).T], axis=1)
+        else:
+            (block,) = hold([block], full[0][:1])
         mine, other = spread_block(block, chips)
-        halves, extras = assemble(
-            mine + other, length, sources, order, rows, 0 if n else small.shape[0]
-        )
-        full.append(halves)
+        spread.append(mine + other)
         if n == 0:
-            small = extras[0]
+            halves, (small,) = assemble(
+                spread[0], length, sources, order, rows, small.shape[0]
+            )
+            full = {0: halves}
+    turns = Turns()
+
+    def whole(n):
+        if n not in full:
+            full[n], _ = assemble(spread[n], length, sources, order, rows, 0, turns.take())
+        return Source(full[n])
+
     w = dict(
         gain=(small[0:1], small[1:2]), bias=(small[2:3], small[3:4]),
         out_bias=(small[4:5], small[5:6]),
@@ -752,34 +769,52 @@
         wout=w_out[0], w_up=w_up[0].T, b_up=b_up, w_down=w_down[0],
     )
     span = range(images_all)
-    turns = Turns()
-
-    def widen(block, step, base, chosen):
-        return Source(base, hand_over(block, step, chips), chosen)
+
+    def widen(n, blocks, chosen):
+        return Source(full[n], blocks, chosen)
 
     *_, lows = step_all(
-        [forward(Source(full[n]), w, info, chips, total, False, turns) for n in span]
-    )
-    streams = [widen(lows[n], 1, full[n], flag) for n in span]
-    *_, done = step_all([forward(streams[n], w, info, chips, total, True, turns) for n in span])
+        [
+            forward(functools.partial(whole, n), w, info, chips, total, False, turns)
+            for n in span
+        ]
+    )
+    *_, done = step_all(
+        [
+            forward(
+                functools.partial(widen, n, lows[n], flag), w, info, chips, total, True, turns
+            )
+            for n in span
+        ]
+    )
     results, saves = [d[0] for d in done], [d[1] for d in done]
-    *_, done = step_all([backward(Source(full[n]), saves[n], w, chips, turns) for n in span])
-    grads = [widen(done[n][1], -1, full[n], 1 - flag) for n in span]
-
-    steps = step_all([backward(grads[n], saves[n], w, chips, turns) for n in span])
-    works = next(steps)
+    *_, done = step_all(
+        [backward(functools.partial(whole, n), saves[n], w, chips, turns, True) for n in span]
+    )
+    lows = [d[1] for d in done]
+    grads = [collect(widen(n, lows[n], 1 - flag), total, cols * size) for n in span]
+    both = (0, 1)
     hidden = w_up.shape[2]
-    both = (0, 1)
-    g_down = outer([(saves[n]["m"][i], works[n]["g"][i]) for n in span for i in both], 0, hidden)
-    g_up = outer(
-        [(works[n]["du"][i], saves[n]["n2"][i]) for n in span for i in both], 0, hidden,
-        (g_down,),
-    )
-    turns.end(g_down, g_up)
-    g_down, g_up = lax.psum([g_down, g_up], "dp")
+    steps = [
+        backward(functools.partial(Source, grads[n]), saves[n], w, chips, turns, False)
+        for n in span
+    ]
+    next(steps[0])
+    g_down = outer(
+        [(saves[n]["m"][i], grads[n][i]) for n in span for i in both], 0, hidden, turns.take()
+    )
+    turns.end(g_down)
+    g_down = lax.psum(g_down, "dp")
+    for step in steps[1:]:
+        next(step)
+    steps = step_all(steps)
     works = next(steps)
     width = cols * size
     heads = b_query.shape[1]
+    g_up = outer(
+        [(works[n]["du"][i], saves[n]["n2"][i]) for n in span for i in both], 0, hidden,
+        turns.take(),
+    )
     rest = [outer([(saves[n]["o"][i], works[n]["dh"][i]) for n in span for i in both], 0, heads)]
     for left in ("dq", "dk", "dv"):
         rest.append(outer([(works[n][left], saves[n]["normed"]) for n in span], 0, heads))
@@ -813,7 +848,8 @@
     count = vector.size
     lines = -(-count // (16 * width)) * 16
     vector = jnp.pad(vector, (0, lines * width - count)).reshape(lines, width).astype(BF16)
-    g_out, g_query, g_key, g_value, vector = lax.psum(hold([*rest, vector], (g_down,)), "dp")
+    rest = hold([g_up, *rest, vector], (g_down,))
+    g_up, g_out, g_query, g_key, g_value, vector = lax.psum(rest, "dp")
     vector = vector.astype(F32).reshape(-1)
     wide = vector[: 6 * cols].reshape(6, cols)
     narrow = vector[6 * cols : count]

time: 713 us -> 720 us (level)
  starting transfers between devices: 68 us -> 51.9 us
  Pallas kernels: 231 us -> 240 us
  waiting for transfers between devices: 277 us -> 286 us
    ppermute x8, waiting for transfers between devices: 26 us -> 58.2 us  [hand_over(): mine.append(lax.ppermute(block, ('section', 'tensor'), pairs))]
    ppermute x26 -> x18, waiting for transfers between devices: 110 us -> 84.4 us  [chip_shift(): lax.ppermute(value, 'tensor', [(i, (i + 2 * shift) % size) for i in range...]
    ppermute x26 -> x18, starting transfers between devices: 36.8 us -> 23.9 us  [chip_shift(): lax.ppermute(value, 'tensor', [(i, (i + 2 * shift) % size) for i in range...]
    pallas_call x80 -> x82, Pallas kernels: 221 us -> 231 us  [run(): pl.pallas_call(kernel, out_shape=[jax.ShapeDtypeStruct(shape, dtype) for...]
    unnamed x333 -> x367, local copies, waits for them, and re-layouts: 44.9 us -> 49 us
  transfers between devices with their start and end apart: 81 -> 65, of which waited for: 36 -> 32; matrix products, arithmetic and copies ran while one was open for 4% -> 4% of each run, Pallas kernels for 27% -> 28%
where the time goes in v3:
time: 720 us; the launch traced here: 709 us
  waiting for transfers between devices  286 us (40%)
  Pallas kernels  240 us (33%)
  local copies, waits for them, and re-layouts  65 us (9%)
  starting transfers between devices  51.9 us (7%)
  blocking collectives  30.9 us (4%)
  other arithmetic  17.5 us (2%)
  between operations  17.3 us (2%)
    pallas_call x82, Pallas kernels, run(): pl.pallas_call(kernel, out_shape=[jax.ShapeDtypeStruct(shape, dtype) for...  231 us
    psum x1, waiting for transfers between devices, per_device(): g_up, g_out, g_query, g_key, g_value, vector = lax.psum(rest, 'dp')  119 us
    ppermute x18, waiting for transfers between devices, chip_shift(): lax.ppermute(value, 'tensor', [(i, (i + 2 * shift) % size) for i in range...  84.4 us
    ppermute x8, waiting for transfers between devices, hand_over(): mine.append(lax.ppermute(block, ('section', 'tensor'), pairs))  58.2 us
    unnamed x367, local copies, waits for them, and re-layouts  49 us
    ppermute x18, starting transfers between devices, chip_shift(): lax.ppermute(value, 'tensor', [(i, (i + 2 * shift) % size) for i in range...  23.9 us
    psum x1, blocking collectives, per_device(): g_up, g_out, g_query, g_key, g_value, vector = lax.psum(rest, 'dp')  19.2 us
    ppermute x8, starting transfers between devices, hand_over(): mine.append(lax.ppermute(block, ('section', 'tensor'), pairs))  18.3 us
  transfers between devices with their start and end apart: 65, of which 32 were waited for; matrix products, arithmetic and copies ran while one was open for 4% of the time, Pallas kernels for 28%

profile of v3, /device:TPU:0, one launch (start us, length us, event | category | flops | bytes accessed | tf_op | source)
XLA Modules:
  0.0 709.2 jit_solution(46556439856286478)
XLA Ops:
  13.2 11.7 %collective-permute-done.refs_3_ = bf16[288,792]{1,0:T(8,128)(2,1)S(1)} collective-permute-done((bf16[288,792]{1,0:T(8,128)(2,1)S(1)}, bf16[288,792]{1,0:T(8,128)(2,1)S(1)}, u32[]{:S(2)}, u32[]{:S(2)}) %collective-permute-start) | collective-permute-done | bytes 456224 | tf_op jit(solution)/shard_map/ppermute | solution.py:559
  70.8 10.7 %shard_map.239 = (f32[384,1152]{1,0:T(8,128)S(1)}, bf16[384,1152]{1,0:T(8,128)(2,1)S(1)}) custom-call(bf16[384,1152]{1,0:T(8,128)(2,1)S(1)} %get-tuple-element.150.refs_0_, bf16[384,1152]{1,0:T(8,128)(2,1)S(1)} %shard_map.232.refs_6_.refs_10_.refs_1_, bf16[384,1152]{1,0:T(8,128)(2,1)S(1)} %collective-permute-done.4.refs_2_, ...), custom_call_target="tpu_custom_call" | custom-call | flops 123863040 | bytes 5322240 | tf_op jit(solution)/shard_map/pallas_call | solution.py:36
  91.1 12.6 %collective-permute-done.12.refs_2_ = bf16[384,1152]{1,0:T(8,128)(2,1)S(1)} collective-permute-done((bf16[384,1152]{1,0:T(8,128)(2,1)S(1)}, bf16[384,1152]{1,0:T(8,128)(2,1)S(1)}, u32[]{:S(2)}, u32[]{:S(2)}) %collective-permute-start.12) | collective-permute-done | bytes 884768 | tf_op jit(solution)/shard_map/ppermute | solution.py:559
  127.9 6.3 collective-permute-done.16.refs_4_
  134.1 8.3 %collective-permute-done.15.refs_3_ = bf16[192,1152]{1,0:T(8,128)(2,1)} collective-permute-done((bf16[192,1152]{1,0:T(8,128)(2,1)S(1)}, bf16[192,1152]{1,0:T(8,128)(2,1)}, u32[]{:S(2)}, u32[]{:S(2)}) %collective-permute-start.15) | collective-permute-done | bytes 442400 | tf_op jit(solution)/shard_map/ppermute | solution.py:577
  208.7 7.7 %collective-permute-done.28.refs_2_ = bf16[384,1152]{1,0:T(8,128)(2,1)S(1)} collective-permute-done((bf16[384,1152]{1,0:T(8,128)(2,1)S(1)}, bf16[384,1152]{1,0:T(8,128)(2,1)S(1)}, u32[]{:S(2)}, u32[]{:S(2)}) %collective-permute-start.28) | collective-permute-done | bytes 884768 | tf_op jit(solution)/shard_map/ppermute | solution.py:559
  244.4 12.8 %collective-permute-done.31.refs_3_ = bf16[384,1152]{1,0:T(8,128)(2,1)S(1)} collective-permute-done((bf16[384,1152]{1,0:T(8,128)(2,1)S(1)}, bf16[384,1152]{1,0:T(8,128)(2,1)S(1)}, u32[]{:S(2)}, u32[]{:S(2)}) %collective-permute-start.31) | collective-permute-done | bytes 884768 | tf_op jit(solution)/shard_map/ppermute | solution.py:559
  263.0 8.0 %shard_map.270 = (bf16[768,288]{1,0:T(8,128)(2,1)S(1)}, bf16[768,288]{1,0:T(8,128)(2,1)S(1)}, bf16[768,288]{1,0:T(8,128)(2,1)S(1)}) custom-call(bf16[384,1152]{1,0:T(8,128)(2,1)S(1)} %get-tuple-element.199.refs_0_, bf16[384,1152]{1,0:T(8,128)(2,1)S(1)} %collective-permute-done.33.refs_1_, bf16[288,1152]{1,0:T(8,128)(2,1)S(1)} %bitcast.91, ...), custom_call_target="tpu_custom_call" | custom-call | flops 49413095424 | bytes 6144000 | tf_op jit(solution)/shard_map/pallas_call | solution.py:36
  275.4 7.2 %collective-permute-done.36.refs_3_ = bf16[384,1152]{1,0:T(8,128)(2,1)S(1)} collective-permute-done((bf16[384,1152]{1,0:T(8,128)(2,1)S(1)}, bf16[384,1152]{1,0:T(8,128)(2,1)S(1)}, u32[]{:S(2)}, u32[]{:S(2)}) %collective-permute-start.36) | collective-permute-done | bytes 884768 | tf_op jit(solution)/shard_map/ppermute | solution.py:559
  288.8 8.0 %shard_map.275 = (bf16[768,288]{1,0:T(8,128)(2,1)S(1)}, bf16[768,288]{1,0:T(8,128)(2,1)S(1)}, bf16[768,288]{1,0:T(8,128)(2,1)S(1)}) custom-call(bf16[384,1152]{1,0:T(8,128)(2,1)S(1)} %get-tuple-element.209.refs_0_, bf16[384,1152]{1,0:T(8,128)(2,1)S(1)} %collective-permute-done.37.refs_1_, bf16[288,1152]{1,0:T(8,128)(2,1)S(1)} %bitcast.92, ...), custom_call_target="tpu_custom_call" | custom-call | flops 49413095424 | bytes 6144000 | tf_op jit(solution)/shard_map/pallas_call | solution.py:36
  307.5 11.9 %collective-permute-done.40.refs_3_ = bf16[192,1152]{1,0:T(8,128)(2,1)S(1)} collective-permute-done((bf16[192,1152]{1,0:T(8,128)(2,1)S(1)}, bf16[192,1152]{1,0:T(8,128)(2,1)S(1)}, u32[]{:S(2)}, u32[]{:S(2)}) %collective-permute-start.40) | collective-permute-done | bytes 442400 | tf_op jit(solution)/shard_map/ppermute | solution.py:577
  319.4 8.9 %collective-permute-done.39.refs_2_ = bf16[192,1152]{1,0:T(8,128)(2,1)S(1)} collective-permute-done((bf16[192,1152]{1,0:T(8,128)(2,1)S(1)}, bf16[192,1152]{1,0:T(8,128)(2,1)S(1)}, u32[]{:S(2)}, u32[]{:S(2)}) %collective-permute-start.39) | collective-permute-done | bytes 442400 | tf_op jit(solution)/shard_map/ppermute | solution.py:577
  338.5 7.8 %collective-permute-done.47.refs_3_ = bf16[192,1152]{1,0:T(8,128)(2,1)S(1)} collective-permute-done((bf16[192,1152]{1,0:T(8,128)(2,1)S(1)}, bf16[192,1152]{1,0:T(8,128)(2,1)S(1)}, u32[]{:S(2)}, u32[]{:S(2)}) %collective-permute-start.47) | collective-permute-done | bytes 442400 | tf_op jit(solution)/shard_map/ppermute | solution.py:577
  346.2 9.4 %collective-permute-done.46.refs_2_ = bf16[192,1152]{1,0:T(8,128)(2,1)S(1)} collective-permute-done((bf16[192,1152]{1,0:T(8,128)(2,1)S(1)}, bf16[192,1152]{1,0:T(8,128)(2,1)S(1)}, u32[]{:S(2)}, u32[]{:S(2)}) %collective-permute-start.46) | collective-permute-done | bytes 442400 | tf_op jit(solution)/shard_map/ppermute | solution.py:577
  361.6 7.2 %shard_map.287.refs_4_ = bf16[1076,1152]{1,0:T(8,128)(2,1)} custom-call(bf16[384,1076]{1,0:T(8,128)(2,1)S(1)} %get-tuple-element.228.refs_0_, bf16[384,1152]{1,0:T(8,128)(2,1)S(1)} %get-tuple-element.218.refs_0_.refs_1_, bf16[384,1076]{1,0:T(8,128)(2,1)S(1)} %get-tuple-element.229.refs_2_, bf16[384,1152]{1,0:T(8,128)(2,1)S(1)} %get-tuple-element.221.refs_0_.refs_3_, ...), custom_call_target="tpu_custom_call" | custom-call | flops 53310652416 | bytes 9323520 | tf_op jit(solution)/shard_map/pallas_call | solution.py:36
  409.3 9.6 %shard_map.291 = (bf16[768,288]{1,0:T(8,128)(2,1)S(1)}, bf16[768,288]{1,0:T(8,128)(2,1)S(1)}, bf16[768,288]{1,0:T(8,128)(2,1)S(1)}) custom-call(bf16[384,1152]{1,0:T(8,128)(2,1)} %get-tuple-element.234.refs_0_.refs_1_, bf16[384,1152]{1,0:T(8,128)(2,1)} %collective-permute-done.51.refs_1_.refs_3_, bf16[288,1152]{1,0:T(8,128)(2,1)S(1)} %bitcast.93, ...), custom_call_target="tpu_custom_call" | custom-call | flops 49413095424 | bytes 6144000 | tf_op jit(solution)/shard_map/pallas_call | solution.py:36
  431.5 8.1 %shard_map.296 = (bf16[768,288]{1,0:T(8,128)(2,1)S(1)}, bf16[768,288]{1,0:T(8,128)(2,1)S(1)}, bf16[768,288]{1,0:T(8,128)(2,1)S(1)}) custom-call(bf16[384,1152]{1,0:T(8,128)(2,1)S(1)} %get-tuple-element.241.refs_0_.refs_5_, bf16[384,1152]{1,0:T(8,128)(2,1)S(1)} %collective-permute-done.55.refs_1_.refs_7_, bf16[288,1152]{1,0:T(8,128)(2,1)S(1)} %bitcast.94, ...), custom_call_target="tpu_custom_call" | custom-call | flops 49413095424 | bytes 6144000 | tf_op jit(solution)/shard_map/pallas_call | solution.py:36
  455.5 5.7 shard_map.306.refs_0_
  474.0 11.7 %psum.56 = bf16[6,1152]{1,0:T(8,128)(2,1)S(1)} all-reduce(f32[6,1152]{1,0:T(8,128)S(1)} %add.106), channel_id=1, replica_groups=mesh['section'=2,'tensor'=4,'dp'=4] {'tensor'}, use_global_device_ids=true, to_apply=%region_0.1 | all-reduce | flops 6912 | bytes 41472 | tf_op jit(solution)/shard_map/psum | solution.py:838
  486.7 13.7 %all-reduce.6.cloned.1.call-done.refs_6_.value_ref = bf16[1076,1152]{1,0:T(8,128)(2,1)} async-done(((bf16[1076,1152]{1,0:T(8,128)(2,1)}), bf16[1076,1152]{1,0:T(8,128)(2,1)}) %all-reduce.6.cloned.1.call-update) | async-done | bytes 2479120 | tf_op jit(solution)/shard_map/psum | solution.py:807
  507.0 10.3 %collective-permute-done.58.refs_2_ = bf16[192,1152]{1,0:T(8,128)(2,1)S(1)} collective-permute-done((bf16[192,1152]{1,0:T(8,128)(2,1)S(1)}, bf16[192,1152]{1,0:T(8,128)(2,1)S(1)}, u32[]{:S(2)}, u32[]{:S(2)}) %collective-permute-start.58) | collective-permute-done | bytes 442400 | tf_op jit(solution)/shard_map/ppermute | solution.py:559
  518.2 7.7 %collective-permute-done.61.refs_2_ = bf16[192,1152]{1,0:T(8,128)(2,1)S(1)} collective-permute-done((bf16[192,1152]{1,0:T(8,128)(2,1)S(1)}, bf16[192,1152]{1,0:T(8,128)(2,1)S(1)}, u32[]{:S(2)}, u32[]{:S(2)}) %collective-permute-start.61) | collective-permute-done | bytes 442400 | tf_op jit(solution)/shard_map/ppermute | solution.py:559
  539.7 19.2 %psum.58 = bf16[16,1152]{1,0:T(8,128)(2,1)S(1)} all-reduce(bf16[16,1152]{1,0:T(8,128)(2,1)S(1)} %copy-done.175), channel_id=1, replica_groups=mesh['section'=2,'tensor'=4,'dp'=4] {'dp'}, use_global_device_ids=true, to_apply=%region_10.11 | all-reduce | flops 18432 | bytes 73728 | tf_op jit(solution)/shard_map/psum | solution.py:852
  572.3 119.1 %all-reduce.8.cloned.1.call-done = (bf16[1,1152,288]{1,2,0:T(8,128)(2,1)}, bf16[1,1152,288]{1,2,0:T(8,128)(2,1)}, bf16[1,1152,288]{1,2,0:T(8,128)(2,1)}, bf16[1,288,1152]{2,1,0:T(8,128)(2,1)}, bf16[1076,1152]{1,0:T(8,128)(2,1)}) async-done(((bf16[1,1152,288]{1,2,0:T(8,128)(2,1)}, bf16[1,1152,288]{1,2,0:T(8,128)(2,1)}, bf16[1,1152,288]{1,2,0:T(8,128)(2,1)}, bf16[1,288,1152]{2,1,0:T(8,128)(2,1)}, ...) | async-done | bytes 5133328 | tf_op jit(solution)/shard_map/psum | solution.py:852
  (616 shorter events, 348.2 us)
Async XLA Ops:
  29.3 21.1 %collective-permute-start.6 = (bf16[288,729]{1,0:T(8,128)(2,1)}, bf16[288,729]{1,0:T(8,128)(2,1)S(1)}, u32[]{:S(2)}, u32[]{:S(2)}) collective-permute-start(bf16[288,729]{1,0:T(8,128)(2,1)} %shard_map.233.refs_2_), channel_id=1, source_target_pairs={{0,4},{4,0},{8,12},{12,8},{1,5},{5,1},{9,13},{13,9},{2,6},{6,2},{1... | collective-permute-start | bytes 1259720 | tf_op jit(solution)/shard_map/ppermute | solution.py:554
  49.1 21.7 %collective-permute-start.4 = (bf16[384,1152]{1,0:T(8,128)(2,1)S(1)}, bf16[384,1152]{1,0:T(8,128)(2,1)S(1)}, u32[]{:S(2)}, u32[]{:S(2)}) collective-permute-start(bf16[384,1152]{1,0:T(8,128)(2,1)S(1)} %shard_map.232.refs_6_.refs_10_.refs_1_), channel_id=1, source_target_pairs={{0,8},{4,12},{8,0},{12,4},{1,9},{5,13},{9,1},{13,5},{2,10},{6,14},... | collective-permute-start | bytes 2654216 | tf_op jit(solution)/shard_map/ppermute | solution.py:559
  81.6 22.1 %collective-permute-start.12 = (bf16[384,1152]{1,0:T(8,128)(2,1)S(1)}, bf16[384,1152]{1,0:T(8,128)(2,1)S(1)}, u32[]{:S(2)}, u32[]{:S(2)}) collective-permute-start(bf16[384,1152]{1,0:T(8,128)(2,1)S(1)} %shard_map.238.refs_6_.refs_1_), channel_id=1, source_target_pairs={{0,8},{4,12},{8,0},{12,4},{1,9},{5,13},{9,1},{13,5},{2,10},{6,14},... | collective-permute-start | bytes 2654216 | tf_op jit(solution)/shard_map/ppermute | solution.py:559
  124.3 18.2 %collective-permute-start.15 = (bf16[192,1152]{1,0:T(8,128)(2,1)S(1)}, bf16[192,1152]{1,0:T(8,128)(2,1)}, u32[]{:S(2)}, u32[]{:S(2)}) collective-permute-start(bf16[192,1152]{1,0:T(8,128)(2,1)S(1)} %get-tuple-element.171.refs_4_), channel_id=1, source_target_pairs={{0,16},{4,20},{8,24},{12,28},{1,17},{5,21},{9,25},{13,29},{2,18},{... | collective-permute-start | bytes 1327112 | tf_op jit(solution)/shard_map/ppermute | solution.py:577
  127.1 16.5 %collective-permute-start.19 = (bf16[192,1152]{1,0:T(8,128)(2,1)}, bf16[192,1152]{1,0:T(8,128)(2,1)}, u32[]{:S(2)}, u32[]{:S(2)}) collective-permute-start(bf16[192,1152]{1,0:T(8,128)(2,1)} %get-tuple-element.170.refs_5_), channel_id=1, source_target_pairs={{0,8},{4,12},{8,0},{12,4},{1,9},{5,13},{9,1},{13,5},{2,10},{6,14},... | collective-permute-start | bytes 1327112 | tf_op jit(solution)/shard_map/ppermute | solution.py:559
  134.1 18.5 %collective-permute-start.18 = (bf16[192,1152]{1,0:T(8,128)(2,1)}, bf16[192,1152]{1,0:T(8,128)(2,1)}, u32[]{:S(2)}, u32[]{:S(2)}) collective-permute-start(bf16[192,1152]{1,0:T(8,128)(2,1)} %collective-permute-done.16.refs_4_), channel_id=1, source_target_pairs={{0,4},{4,0},{8,12},{12,8},{1,5},{5,1},{9,13},{13,9},{2,6},{6,2},{1... | collective-permute-start | bytes 1327112 | tf_op jit(solution)/shard_map/ppermute | solution.py:554
  146.9 17.8 %collective-permute-start.23 = (bf16[192,1152]{1,0:T(8,128)(2,1)S(1)}, bf16[192,1152]{1,0:T(8,128)(2,1)S(1)}, u32[]{:S(2)}, u32[]{:S(2)}) collective-permute-start(bf16[192,1152]{1,0:T(8,128)(2,1)S(1)} %get-tuple-element.173.refs_15_), channel_id=1, source_target_pairs={{8,16},{12,20},{0,24},{4,28},{9,17},{13,21},{1,25},{5,29},{10,18},... | collective-permute-start | bytes 1327112 | tf_op jit(solution)/shard_map/ppermute | solution.py:577
  150.9 19.7 %collective-permute-start.22 = (bf16[192,1152]{1,0:T(8,128)(2,1)S(1)}, bf16[192,1152]{1,0:T(8,128)(2,1)S(1)}, u32[]{:S(2)}, u32[]{:S(2)}) collective-permute-start(bf16[192,1152]{1,0:T(8,128)(2,1)S(1)} %get-tuple-element.173.refs_15_), channel_id=1, source_target_pairs={{0,16},{4,20},{8,24},{12,28},{1,17},{5,21},{9,25},{13,29},{2,18},{... | collective-permute-start | bytes 1327112 | tf_op jit(solution)/shard_map/ppermute | solution.py:577
  175.5 22.4 %collective-permute-start.21 = (bf16[384,1152]{1,0:T(8,128)(2,1)S(1)}, bf16[384,1152]{1,0:T(8,128)(2,1)S(1)}, u32[]{:S(2)}, u32[]{:S(2)}) collective-permute-start(bf16[384,1152]{1,0:T(8,128)(2,1)S(1)} %shard_map.252.refs_15_.refs_1_), channel_id=1, source_target_pairs={{0,8},{4,12},{8,0},{12,4},{1,9},{5,13},{9,1},{13,5},{2,10},{6,14},... | collective-permute-start | bytes 2654216 | tf_op jit(solution)/shard_map/ppermute | solution.py:559
  192.1 24.4 %collective-permute-start.28 = (bf16[384,1152]{1,0:T(8,128)(2,1)S(1)}, bf16[384,1152]{1,0:T(8,128)(2,1)S(1)}, u32[]{:S(2)}, u32[]{:S(2)}) collective-permute-start(bf16[384,1152]{1,0:T(8,128)(2,1)S(1)} %shard_map.256.refs_6_.refs_1_), channel_id=1, source_target_pairs={{0,8},{4,12},{8,0},{12,4},{1,9},{5,13},{9,1},{13,5},{2,10},{6,14},... | collective-permute-start | bytes 2654216 | tf_op jit(solution)/shard_map/ppermute | solution.py:559
  235.6 21.6 %collective-permute-start.31 = (bf16[384,1152]{1,0:T(8,128)(2,1)S(1)}, bf16[384,1152]{1,0:T(8,128)(2,1)S(1)}, u32[]{:S(2)}, u32[]{:S(2)}) collective-permute-start(bf16[384,1152]{1,0:T(8,128)(2,1)S(1)} %shard_map.265.refs_4_.refs_2_), channel_id=1, source_target_pairs={{0,8},{4,12},{8,0},{12,4},{1,9},{5,13},{9,1},{13,5},{2,10},{6,14},... | collective-permute-start | bytes 2654216 | tf_op jit(solution)/shard_map/ppermute | solution.py:559
  260.5 22.1 %collective-permute-start.36 = (bf16[384,1152]{1,0:T(8,128)(2,1)S(1)}, bf16[384,1152]{1,0:T(8,128)(2,1)S(1)}, u32[]{:S(2)}, u32[]{:S(2)}) collective-permute-start(bf16[384,1152]{1,0:T(8,128)(2,1)S(1)} %shard_map.268.refs_5_.refs_2_), channel_id=1, source_target_pairs={{0,8},{4,12},{8,0},{12,4},{1,9},{5,13},{9,1},{13,5},{2,10},{6,14},... | collective-permute-start | bytes 2654216 | tf_op jit(solution)/shard_map/ppermute | solution.py:559
  303.6 15.8 %collective-permute-start.40 = (bf16[192,1152]{1,0:T(8,128)(2,1)S(1)}, bf16[192,1152]{1,0:T(8,128)(2,1)S(1)}, u32[]{:S(2)}, u32[]{:S(2)}) collective-permute-start(bf16[192,1152]{1,0:T(8,128)(2,1)S(1)} %get-tuple-element.217.refs_5_), channel_id=1, source_target_pairs={{24,0},{28,4},{16,8},{20,12},{25,1},{29,5},{17,9},{21,13},{26,2},{... | collective-permute-start | bytes 1327112 | tf_op jit(solution)/shard_map/ppermute | solution.py:577
  304.9 23.4 %collective-permute-start.39 = (bf16[192,1152]{1,0:T(8,128)(2,1)S(1)}, bf16[192,1152]{1,0:T(8,128)(2,1)S(1)}, u32[]{:S(2)}, u32[]{:S(2)}) collective-permute-start(bf16[192,1152]{1,0:T(8,128)(2,1)S(1)} %get-tuple-element.217.refs_5_), channel_id=1, source_target_pairs={{16,0},{20,4},{24,8},{28,12},{17,1},{21,5},{25,9},{29,13},{18,2},{... | collective-permute-start | bytes 1327112 | tf_op jit(solution)/shard_map/ppermute | solution.py:577
  306.2 22.2 %collective-permute-start.43 = (bf16[192,1152]{1,0:T(8,128)(2,1)S(1)}, bf16[192,1152]{1,0:T(8,128)(2,1)S(1)}, u32[]{:S(2)}, u32[]{:S(2)}) collective-permute-start(bf16[192,1152]{1,0:T(8,128)(2,1)S(1)} %get-tuple-element.216.refs_6_), channel_id=1, source_target_pairs={{0,8},{4,12},{8,0},{12,4},{1,9},{5,13},{9,1},{13,5},{2,10},{6,14},... | collective-permute-start | bytes 1327112 | tf_op jit(solution)/shard_map/ppermute | solution.py:559
  332.1 23.5 %collective-permute-start.46 = (bf16[192,1152]{1,0:T(8,128)(2,1)S(1)}, bf16[192,1152]{1,0:T(8,128)(2,1)S(1)}, u32[]{:S(2)}, u32[]{:S(2)}) collective-permute-start(bf16[192,1152]{1,0:T(8,128)(2,1)S(1)} %get-tuple-element.223.refs_4_), channel_id=1, source_target_pairs={{16,0},{20,4},{24,8},{28,12},{17,1},{21,5},{25,9},{29,13},{18,2},{... | collective-permute-start | bytes 1327112 | tf_op jit(solution)/shard_map/ppermute | solution.py:577
  338.0 22.1 %collective-permute-start.44 = (bf16[384,1152]{1,0:T(8,128)(2,1)S(1)}, bf16[384,1152]{1,0:T(8,128)(2,1)S(1)}, u32[]{:S(2)}, u32[]{:S(2)}) collective-permute-start(bf16[384,1152]{1,0:T(8,128)(2,1)S(1)} %get-tuple-element.224), channel_id=1, source_target_pairs={{0,4},{4,0},{8,12},{12,8},{1,5},{5,1},{9,13},{13,9},{2,6},{6,2},{1... | collective-permute-start | bytes 2654216 | tf_op jit(solution)/shard_map/ppermute | solution.py:554
  360.2 27.6 %collective-permute-start.45 = (bf16[384,1152]{1,0:T(8,128)(2,1)S(1)}, bf16[384,1152]{1,0:T(8,128)(2,1)S(1)}, u32[]{:S(2)}, u32[]{:S(2)}) collective-permute-start(bf16[384,1152]{1,0:T(8,128)(2,1)S(1)} %shard_map.284.refs_8_.refs_2_), channel_id=1, source_target_pairs={{0,8},{4,12},{8,0},{12,4},{1,9},{5,13},{9,1},{13,5},{2,10},{6,14},... | collective-permute-start | bytes 2654216 | tf_op jit(solution)/shard_map/ppermute | solution.py:559
  378.7 121.7 %all-reduce.6.cloned.1.call-start = ((), (), s32[]{:S(2)}) async-start(), calls=%async_computation.1 | async-start | bytes 4976640 | tf_op jit(solution)/shard_map/psum | solution.py:807
  400.9 290.6 %all-reduce.8.cloned.1.call-start = ((), (), s32[]{:S(2)}) async-start(), calls=%async_computation.2 | async-start | bytes 10285056 | tf_op jit(solution)/shard_map/psum | solution.py:852
  402.4 21.7 %collective-permute-start.54 = (bf16[384,1152]{1,0:T(8,128)(2,1)S(1)}, bf16[384,1152]{1,0:T(8,128)(2,1)S(1)}, u32[]{:S(2)}, u32[]{:S(2)}) collective-permute-start(bf16[384,1152]{1,0:T(8,128)(2,1)S(1)} %shard_map.289.refs_5_.refs_2_), channel_id=1, source_target_pairs={{0,8},{4,12},{8,0},{12,4},{1,9},{5,13},{9,1},{13,5},{2,10},{6,14},... | collective-permute-start | bytes 2654216 | tf_op jit(solution)/shard_map/ppermute | solution.py:559
  429.6 31.7 %collective-permute-start.53 = (bf16[192,1152]{1,0:T(8,128)(2,1)}, bf16[192,1152]{1,0:T(8,128)(2,1)}, u32[]{:S(2)}, u32[]{:S(2)}) collective-permute-start(bf16[192,1152]{1,0:T(8,128)(2,1)} %get-tuple-element.239.refs_6_), channel_id=1, source_target_pairs={{0,8},{4,12},{8,0},{12,4},{1,9},{5,13},{9,1},{13,5},{2,10},{6,14},... | collective-permute-start | bytes 1327112 | tf_op jit(solution)/shard_map/ppermute | solution.py:559
  505.9 20.1 %collective-permute-start.61 = (bf16[192,1152]{1,0:T(8,128)(2,1)S(1)}, bf16[192,1152]{1,0:T(8,128)(2,1)S(1)}, u32[]{:S(2)}, u32[]{:S(2)}) collective-permute-start(bf16[192,1152]{1,0:T(8,128)(2,1)S(1)} %get-tuple-element.259), channel_id=1, source_target_pairs={{0,8},{4,12},{8,0},{12,4},{1,9},{5,13},{9,1},{13,5},{2,10},{6,14},... | collective-permute-start | bytes 1327112 | tf_op jit(solution)/shard_map/ppermute | solution.py:559
  530.4 33.2 %all-to-all-start = ((f32[2,192,4,288]{3,1,0,2:T(8,128)}), f32[2,192,4,288]{3,1,0,2:T(8,128)}, u32[]{:S(2)}, u32[]{:S(2)}) async-start(f32[2,192,4,288]{3,1,0,2:T(8,128)} %pad_maximum_fusion), calls=%async_computation | async-start | bytes 4718592 | tf_op jit(solution)/shard_map/all_to_all | solution.py:858
  (224 other events, 2296.8 us)
Sparse Core Ops, SparseCore 0:
  401.0 99.3 all-reduce.5
  503.8 187.6 all-reduce.7

commit v4 on v3

--- a/solution.py
+++ b/solution.py
@@ -67,7 +67,7 @@
     return center * inverse, inverse
 
 
-def assemble(parts, length, sources, order, rows, extra, after=()):
+def assemble(parts, length, sources, order, rows, extra, after=(), near=()):
     count = len(parts)
     cols = parts[0].shape[0]
     half, total, width = count // 2, rows * count, cols * count
@@ -104,6 +104,7 @@
         scratch=(pltpu.VMEM((width, deep), BF16), pltpu.VMEM((deep, width), BF16)),
         limit=10,
         after=after,
+        near=near,
     )
     return (mine, other), small
 
@@ -157,8 +158,8 @@
     return run(body, [shape, shape], (*scalars, *arrays), scalars=len(scalars), flops=rows * width)
 
 
-def project(info, source, gain, bias, wq, bq, wk, wv, bv, rows, after=()):
-    cols, width = wq.shape
+def project(info, source, gain, bias, weight, shift, rows, after=()):
+    cols, width = weight.shape[0] // 3, weight.shape[1]
     heads = cols // HD
     scalars, arrays = source.operands((0, 1))
     count, total = len(arrays), rows
@@ -169,8 +170,7 @@
         info_ref, flags = refs[0], refs[1 : 1 + len(scalars)]
         refs = refs[1 + len(scalars) :]
         read = source.reader((0, 1), flags, refs[:count])
-        (g_ref, b_ref, wq_ref, bq_ref, wk_ref, wv_ref, bv_ref,
-         x_ref, n_ref, q_ref, k_ref, v_ref) = refs[count:]
+        g_ref, b_ref, w_ref, s_ref, x_ref, n_ref, *outs = refs[count:]
         for index in (0, 1):
             for at in range(0, half, step):
                 value = read(index, at, step)
@@ -180,29 +180,26 @@
                 n_ref[index * half + at : index * half + at + step, :] = (
                     unit * g_ref[...] + b_ref[...]
                 ).astype(BF16)
-        normed = n_ref[...]
         row = lax.broadcasted_iota(jnp.int32, (total, LANES - HD), 0)
         lane = lax.broadcasted_iota(jnp.int32, (total, LANES - HD), 1)
         pad_start = info_ref[0]
         padded = (row >= pad_start) & (row < pad_start + info_ref[1])
         ones = jnp.where(lane == 0, 1.0, 0.0).astype(BF16)
         mask = jnp.where((lane == 0) & padded, FAR, 0.0).astype(BF16)
-
-        def spread(value, out, extra):
+        normed = n_ref[...]
+        for i, (out, extra) in enumerate(zip(outs, (ones, mask, ones))):
+            here = slice(i * cols, (i + 1) * cols)
+            value = (mm_nt(normed, w_ref[here, :]) + s_ref[:, here]).astype(BF16)
             for h in range(heads):
                 out[:, h * LANES : (h + 1) * LANES] = jnp.concatenate(
                     [value[:, h * HD : (h + 1) * HD], extra], axis=1
                 )
 
-        spread((mm_nt(normed, wq_ref[...]) + bq_ref[...]).astype(BF16), q_ref, ones)
-        spread(mm_nt(normed, wk_ref[...]).astype(BF16), k_ref, mask)
-        spread((mm_nt(normed, wv_ref[...]) + bv_ref[...]).astype(BF16), v_ref, ones)
-
     wide = ((total, heads * LANES), BF16)
     return run(
         body,
         [((half, width), BF16), ((total, width), BF16), wide, wide, wide],
-        (info, *scalars, *arrays, gain, bias, wq, bq, wk, wv, bv),
+        (info, *scalars, *arrays, gain, bias, weight, shift),
         scalars=1 + len(scalars),
         flops=6 * total * width * cols,
         after=after,
@@ -213,7 +210,7 @@
     total, wide = q.shape
     heads = wide // LANES
     half = total // 2
-    step = half // 2
+    step = half
 
     def body(q_ref, k_ref, v_ref, w_ref, z_ref, o_ref, l_ref):
         for at in range(0, half, step):
@@ -277,7 +274,7 @@
 def mlp(n2, w_up, b_up, w_down, out_type, save):
     half, width = n2.shape
     hidden = w_up.shape[0]
-    step = half // 2
+    step = half
 
     def body(n_ref, wu_ref, bu_ref, wd_ref, z_ref, *saved):
         for at in range(0, half, step):
@@ -311,12 +308,9 @@
         s_ref, wu_ref, wd_ref, g_ref, z_ref, d_ref = refs[len(scalars) + count :]
         for at in range(0, half, step):
             g_ref[at : at + step, :] = read(which, at, step)
-        for at in range(0, half, half // 2):
-            here = slice(at, at + half // 2)
-            grad = mm_nt(g_ref[here, :], wd_ref[...]) * s_ref[here, :].astype(F32)
-            grad = grad.astype(BF16)
-            d_ref[here, :] = grad
-            z_ref[here, :] = mm(grad, wu_ref[...]).astype(out_type)
+        grad = (mm_nt(g_ref[...], wd_ref[...]) * s_ref[...].astype(F32)).astype(BF16)
+        d_ref[...] = grad
+        z_ref[...] = mm(grad, wu_ref[...]).astype(out_type)
 
     return run(
         body,
@@ -374,10 +368,10 @@
     half = dm.shape[0]
     total, wide = q.shape
     heads = wide // LANES
-    step = total // 3
+    step = total
 
     def body(dm_ref, do_ref, w_ref, q_ref, k_ref, v_ref, lm_ref, lo_ref,
-             dq_ref, dk_ref, dv_ref, up_ref, log_ref, p_ref, w_ref2):
+             d_ref, up_ref, log_ref, p_ref, w_ref2):
         for index, ref in enumerate((dm_ref, do_ref)):
             here = slice(index * half, (index + 1) * half)
             grad = mm_nt(ref[...], w_ref[...]).astype(BF16)
@@ -414,14 +408,11 @@
             dqs.append((dq_t * SCALE).T.astype(BF16)[:, :HD])
             dks.append(jnp.concatenate(dk_h, axis=0))
             dvs.append(jnp.concatenate(dv_h, axis=0))
-        dq_ref[...] = jnp.concatenate(dqs, axis=1)
-        dk_ref[...] = jnp.concatenate(dks, axis=1)
-        dv_ref[...] = jnp.concatenate(dvs, axis=1)
-
-    out = ((total, heads * HD), BF16)
+        d_ref[...] = jnp.concatenate([*dqs, *dks, *dvs], axis=1)
+
     return run(
         body,
-        [out, out, out],
+        [((total, 3 * heads * HD), BF16)],
         (dm, do, wout, q, k, v, lm, lo),
         flops=10 * total * total * LANES * heads + 2 * total * heads * HD * dm.shape[1],
         scratch=(
@@ -431,34 +422,30 @@
             pltpu.VMEM((total, total), F32),
         ),
         limit=12,
-    )
-
-
-def project_back(first_row, dq, dk, dv, wq, wk, wv, out_type):
-    total, cols = dq.shape
+    )[0]
+
+
+def project_back(first_row, grad, weight, out_type):
+    total = grad.shape[0]
     half = total // 2
-    width = wq.shape[1]
-
-    def body(dq_ref, dk_ref, dv_ref, wq_ref, wk_ref, wv_ref, z_ref):
-        here = slice(first_row, first_row + half)
-        z_ref[...] = (
-            mm(dq_ref[here, :], wq_ref[...])
-            + mm(dk_ref[here, :], wk_ref[...])
-            + mm(dv_ref[here, :], wv_ref[...])
-        ).astype(out_type)
+    cols, width = weight.shape
+
+    def body(d_ref, w_ref, z_ref):
+        z_ref[...] = mm(d_ref[first_row : first_row + half, :], w_ref[...]).astype(out_type)
 
     return run(
-        body, [((half, width), out_type)], (dq, dk, dv, wq, wk, wv), flops=6 * half * cols * width
+        body, [((half, width), out_type)], (grad, weight), flops=2 * half * cols * width
     )[0]
 
 
 def start_back(xm, dh, own, arrived, gain, after=()):
     rows, width = own.shape
+    part = rows // pieces_of(rows)
     count = len(arrived)
 
     def body(x_ref, dh_ref, own_ref, *refs):
         got = refs[:count]
-        gain_ref, d_ref, low_ref, sums_ref = refs[count:]
+        gain_ref, d_ref, sums_ref, *low_refs = refs[count:]
         def step(i, sums):
             here = pl.ds(pl.multiple_of(i * STEP, 16), STEP)
             grad = own_ref[here, :]
@@ -470,7 +457,6 @@
             second = jnp.mean(scaled * unit, 1, keepdims=True)
             total = dh_ref[here, :] + inverse * (scaled - first - unit * second)
             d_ref[here, :] = total
-            low_ref[here, :] = total.astype(BF16)
             return tuple(
                 a + jnp.sum(t, 0, keepdims=True) for a, t in zip(sums, (grad * unit, grad))
             )
@@ -478,35 +464,42 @@
         sums = lax.fori_loop(0, rows // STEP, step, (jnp.zeros((1, width), F32),) * 2)
         for i in range(2):
             sums_ref[i : i + 1, :] = sums[i]
-
-    return run(
-        body,
-        [((rows, width), F32), ((rows, width), BF16), ((8, width), F32)],
+        for i, ref in enumerate(low_refs):
+            ref[...] = d_ref[i * part : (i + 1) * part, :].astype(BF16)
+
+    d, sums, *low = run(
+        body,
+        [((rows, width), F32), ((8, width), F32)]
+        + [((part, width), BF16)] * (rows // part),
         (xm, dh, own, *arrived, gain),
         flops=30 * rows * width,
         after=after,
     )
+    return d, low, sums
 
 
 def finish_rows(hidden, total, arrived, out_bias, after=()):
     rows, width = total[0].shape
+    part = rows // pieces_of(rows)
 
     def body(h_ref, total_ref, *refs):
-        bias_ref, y_ref, low_ref = refs[len(arrived) :]
+        bias_ref, y_ref, *low_refs = refs[len(arrived) :]
         value = total_ref[...]
         for ref in refs[: len(arrived)]:
             value = value + ref[...].astype(F32)
         value = h_ref[0:rows, :] + value + bias_ref[...]
         y_ref[...] = value
-        low_ref[...] = value.astype(BF16)
-
-    return run(
-        body,
-        [((rows, width), F32), ((rows, width), BF16)],
+        for i, ref in enumerate(low_refs):
+            ref[...] = value[i * part : (i + 1) * part, :].astype(BF16)
+
+    y, *low = run(
+        body,
+        [((rows, width), F32)] + [((part, width), BF16)] * (rows // part),
         (hidden, total[0], *arrived, out_bias),
         flops=4 * rows * width,
         after=after,
     )
+    return y, low
 
 
 def outer(pairs, low, high, after=()):
@@ -568,14 +561,15 @@
     return mine, [core_swap(b) for b in mine]
 
 
-def hand_over(block, step, chips):
-    size = lax.axis_size("tensor")
-    source, target = (0, size) if step > 0 else (size, 0)
-    mine = []
-    for p in range(chips):
-        pairs = [(source + (i + 2 * p) % size, target + i) for i in range(size)]
-        mine.append(lax.ppermute(block, ("section", "tensor"), pairs))
-    return [mine, [core_swap(b) for b in mine]]
+def hand_over(pieces, chips, after=()):
+    if after:
+        pieces = hold(pieces, after)
+    spread = [spread_block(piece, chips) for piece in pieces]
+    return [[spread[j][i][p] for p in range(chips) for j in range(len(pieces))] for i in (0, 1)]
+
+
+def pieces_of(rows):
+    return 2 if rows % 32 == 0 and rows >= 128 else 1
 
 
 def sum_blocks(mine, other, chips):
@@ -592,6 +586,11 @@
     return (own, *sends), [chip_shift(send, p) for p, send in enumerate(sends, 1)]
 
 
+def to_section(value, step):
+    pairs = [(0, 1)] if step > 0 else [(1, 0)]
+    return lax.ppermute(value, "section", pairs)
+
+
 class Turns:
     def __init__(self):
         self.last, self.first = (), ()
@@ -606,8 +605,7 @@
 def forward(source, w, info, chips, rows, save, turns):
     source = source()
     xm, normed, q, k, v = project(
-        info, source, w["gain"][0], w["bias"][0], w["wq"], w["bq"], w["wk"], w["wv"], w["bv"],
-        rows, turns.take(),
+        info, source, w["gain"][0], w["bias"][0], w["qkv"], w["qkv_shift"], rows, turns.take(),
     )
     turns.first = (q,)
     half = rows // 2
@@ -638,8 +636,8 @@
     turns.end(*total)
     yield
     _, low = finish_rows(hidden, total, arrived, w["out_bias"][1], turns.take())
-    turns.end(low)
-    return hand_over(low, 1, chips)
+    turns.end(low[0])
+    return [to_section(piece, 1) for piece in low]
 
 
 def backward(source, saved, w, chips, turns, pass_on):
@@ -660,18 +658,18 @@
     )
     dho = core_swap(dhm)
     q, k, v = saved["q"], saved["k"], saved["v"]
-    dq, dk, dv = attend_back(dhm, dho, w["wout"], q, k, v, *saved["l"])
+    dqkv = attend_back(dhm, dho, w["wout"], q, k, v, *saved["l"])
     half = gm.shape[0]
-    d_other = core_swap(project_back(half, dq, dk, dv, w["wq"], w["wk"], w["wv"], BF16))
-    d_mine = project_back(0, dq, dk, dv, w["wq"], w["wk"], w["wv"], F32)
+    d_other = core_swap(project_back(half, dqkv, w["qkv"], BF16))
+    d_mine = project_back(0, dqkv, w["qkv"], F32)
     total, arrived = sum_blocks(d_mine, d_other, chips)
     turns.end(*total)
-    work.update(dh=(dhm, dho), dq=dq, dk=dk, dv=dv)
+    work.update(dh=(dhm, dho), dqkv=dqkv)
     yield work
     dx, low, sums_one = start_back(saved["x"], dh, total[0], arrived, w["gain"][0], turns.take())
-    turns.end(low)
+    turns.end(low[0])
     work.update(sums=(sums_one, sums_two))
-    return dx, hand_over(low, -1, chips) if pass_on else None, work
+    return dx, [to_section(piece, -1) for piece in low] if pass_on else None, work
 
 
 def step_all(steps):
@@ -705,12 +703,6 @@
         out_specs=pl.BlockSpec((step, 1, width), lambda i: (i, 0, 0)),
         compiler_params=pltpu.CompilerParams(vmem_limit_bytes=8 * 2**20),
     )(value)
-
-
-def dp_sum(pieces):
-    if lax.axis_size("dp") == 4:
-        return line_sum(pieces)
-    return [lax.psum(piece, "dp") for piece in pieces]
 
 
 def per_device(inputs, norm_gain, norm_bias, w_query, b_query, w_key, w_value, b_value, w_out,
@@ -740,6 +732,7 @@
     middle_part = lax.reduce_precision(small - high, 8, 7)
     thirds = jnp.concatenate([high, middle_part, small - high - middle_part], axis=0)
     features = inputs[0].reshape(images_all, length, cols).transpose(0, 2, 1)
+    qkv = jnp.concatenate([w_query[0].T, w_key[0].T, w_value[0].T], axis=0)
     spread = []
     for n in range(images_all):
         block = features[n]
@@ -752,7 +745,8 @@
         spread.append(mine + other)
         if n == 0:
             halves, (small,) = assemble(
-                spread[0], length, sources, order, rows, small.shape[0]
+                spread[0], length, sources, order, rows, small.shape[0],
+                near=(qkv,),
             )
             full = {0: halves}
     turns = Turns()
@@ -765,13 +759,13 @@
     w = dict(
         gain=(small[0:1], small[1:2]), bias=(small[2:3], small[3:4]),
         out_bias=(small[4:5], small[5:6]),
-        wq=w_query[0].T, bq=b_query, wk=w_key[0].T, wv=w_value[0].T, bv=b_value,
+        qkv=qkv, qkv_shift=jnp.concatenate([b_query, jnp.zeros_like(b_query), b_value], axis=1),
         wout=w_out[0], w_up=w_up[0].T, b_up=b_up, w_down=w_down[0],
     )
     span = range(images_all)
 
-    def widen(n, blocks, chosen):
-        return Source(full[n], blocks, chosen)
+    def widen(n, pieces, chosen):
+        return Source(full[n], hand_over(pieces, chips), chosen)
 
     *_, lows = step_all(
         [
@@ -816,8 +810,7 @@
         turns.take(),
     )
     rest = [outer([(saves[n]["o"][i], works[n]["dh"][i]) for n in span for i in both], 0, heads)]
-    for left in ("dq", "dk", "dv"):
-        rest.append(outer([(works[n][left], saves[n]["normed"]) for n in span], 0, heads))
+    rest.append(outer([(works[n]["dqkv"], saves[n]["normed"]) for n in span], 0, 3 * heads))
     done = next(steps)
     works = [d[2] for d in done]
     ends = [jnp.where(first, done[n][0], results[n]) for n in span]
@@ -840,8 +833,7 @@
     vector = jnp.concatenate(
         [
             wide.reshape(-1),
-            total_of([works[n]["dq"] for n in span]),
-            total_of([works[n]["dv"] for n in span]),
+            total_of([works[n]["dqkv"] for n in span]),
             total_of([works[n]["du"][i] for n in span for i in both]),
         ]
     )
@@ -849,7 +841,8 @@
     lines = -(-count // (16 * width)) * 16
     vector = jnp.pad(vector, (0, lines * width - count)).reshape(lines, width).astype(BF16)
     rest = hold([g_up, *rest, vector], (g_down,))
-    g_up, g_out, g_query, g_key, g_value, vector = lax.psum(rest, "dp")
+    g_up, g_out, g_qkv, vector = lax.psum(rest, "dp")
+    g_query, g_key, g_value = (g_qkv[i * heads : (i + 1) * heads] for i in range(3))
     vector = vector.astype(F32).reshape(-1)
     wide = vector[: 6 * cols].reshape(6, cols)
     narrow = vector[6 * cols : count]
@@ -860,9 +853,9 @@
     ends = ends.reshape(1, micro, images, length, cols)
     return (
         ends, wide[None, 0:2], wide[None, 2:4], g_query.T[None].astype(F32), narrow[None, :heads], g_key.T[None].astype(F32),
-        g_value.T[None].astype(F32), narrow[None, heads : 2 * heads], g_out[None].astype(F32), wide[None, 4:6],
+        g_value.T[None].astype(F32), narrow[None, 2 * heads : 3 * heads], g_out[None].astype(F32), wide[None, 4:6],
         finish(g_up).transpose(1, 2, 0),
-        narrow[None, 2 * heads :], finish(g_down).transpose(1, 0, 2),
+        narrow[None, 3 * heads :], finish(g_down).transpose(1, 0, 2),
     )
 
 

time: 720 us -> 690 us (0.958)
  Pallas kernels: 240 us -> 207 us
  starting transfers between devices: 51.9 us -> 66.8 us
  waiting for transfers between devices: 286 us -> 277 us
    pallas_call x82 -> x80, Pallas kernels: 231 us -> 198 us  [run(): pl.pallas_call(kernel, out_shape=[jax.ShapeDtypeStruct(shape, dtype) for...]
    ppermute x8, waiting for transfers between devices: 58.2 us -> 30.6 us  [to_section(): return lax.ppermute(value, 'section', pairs)]
    ppermute x18 -> x26, waiting for transfers between devices: 84.4 us -> 105 us  [chip_shift(): lax.ppermute(value, 'tensor', [(i, (i + 2 * shift) % size) for i in range...]
    ppermute x18 -> x26, starting transfers between devices: 23.9 us -> 37.8 us  [chip_shift(): lax.ppermute(value, 'tensor', [(i, (i + 2 * shift) % size) for i in range...]
    unnamed x367 -> x329, local copies, waits for them, and re-layouts: 49 us -> 45.5 us
  transfers between devices with their start and end apart: 65 -> 81, of which waited for: 32 -> 34; matrix products, arithmetic and copies ran while one was open for 4% -> 4% of each run, Pallas kernels for 28% -> 25%
where the time goes in v4:
time: 690 us; the launch traced here: 680 us
  waiting for transfers between devices  277 us (40%)
  Pallas kernels  207 us (30%)
  starting transfers between devices  66.8 us (10%)
  local copies, waits for them, and re-layouts  64.9 us (9%)
  blocking collectives  34.7 us (5%)
  between operations  16.9 us (2%)
  other arithmetic  12.7 us (2%)
    pallas_call x80, Pallas kernels, run(): pl.pallas_call(kernel, out_shape=[jax.ShapeDtypeStruct(shape, dtype) for...  198 us
    psum x1, waiting for transfers between devices, per_device(): g_up, g_out, g_qkv, vector = lax.psum(rest, 'dp')  117 us
    ppermute x26, waiting for transfers between devices, chip_shift(): lax.ppermute(value, 'tensor', [(i, (i + 2 * shift) % size) for i in range...  105 us
    unnamed x329, local copies, waits for them, and re-layouts  45.5 us
    ppermute x26, starting transfers between devices, chip_shift(): lax.ppermute(value, 'tensor', [(i, (i + 2 * shift) % size) for i in range...  37.8 us
    ppermute x8, waiting for transfers between devices, to_section(): return lax.ppermute(value, 'section', pairs)  30.6 us
    psum x1, blocking collectives, per_device(): g_up, g_out, g_qkv, vector = lax.psum(rest, 'dp')  22.9 us
    ppermute x8, starting transfers between devices, to_section(): return lax.ppermute(value, 'section', pairs)  17.2 us
  transfers between devices with their start and end apart: 81, of which 34 were waited for; matrix products, arithmetic and copies ran while one was open for 4% of the time, Pallas kernels for 25%

profile of v4, /device:TPU:0, one launch (start us, length us, event | category | flops | bytes accessed | tf_op | source)
XLA Modules:
  0.0 679.9 jit_solution(13404725819678930338)
XLA Ops:
  14.5 10.5 %collective-permute-done.refs_3_ = bf16[288,792]{1,0:T(8,128)(2,1)S(1)} collective-permute-done((bf16[288,792]{1,0:T(8,128)(2,1)S(1)}, bf16[288,792]{1,0:T(8,128)(2,1)S(1)}, u32[]{:S(2)}, u32[]{:S(2)}) %collective-permute-start) | collective-permute-done | bytes 456224 | tf_op jit(solution)/shard_map/ppermute | solution.py:552
  34.6 5.3 shard_map.229
  50.3 5.5 shard_map.235
  62.4 6.9 %collective-permute-done.4.refs_2_ = bf16[384,1152]{1,0:T(8,128)(2,1)S(1)} collective-permute-done((bf16[384,1152]{1,0:T(8,128)(2,1)S(1)}, bf16[384,1152]{1,0:T(8,128)(2,1)S(1)}, u32[]{:S(2)}, u32[]{:S(2)}) %collective-permute-start.4) | collective-permute-done | bytes 884768 | tf_op jit(solution)/shard_map/ppermute | solution.py:552
  80.2 13.6 %collective-permute-done.12.refs_2_ = bf16[384,1152]{1,0:T(8,128)(2,1)S(1)} collective-permute-done((bf16[384,1152]{1,0:T(8,128)(2,1)S(1)}, bf16[384,1152]{1,0:T(8,128)(2,1)S(1)}, u32[]{:S(2)}, u32[]{:S(2)}) %collective-permute-start.12) | collective-permute-done | bytes 884768 | tf_op jit(solution)/shard_map/ppermute | solution.py:552
  143.5 5.7 shard_map.249
  172.9 7.2 %collective-permute-done.25.refs_2_ = bf16[384,1152]{1,0:T(8,128)(2,1)S(1)} collective-permute-done((bf16[384,1152]{1,0:T(8,128)(2,1)S(1)}, bf16[384,1152]{1,0:T(8,128)(2,1)S(1)}, u32[]{:S(2)}, u32[]{:S(2)}) %collective-permute-start.25) | collective-permute-done | bytes 884768 | tf_op jit(solution)/shard_map/ppermute | solution.py:552
  189.4 9.2 %collective-permute-done.36.refs_2_ = bf16[384,1152]{1,0:T(8,128)(2,1)S(1)} collective-permute-done((bf16[384,1152]{1,0:T(8,128)(2,1)S(1)}, bf16[384,1152]{1,0:T(8,128)(2,1)S(1)}, u32[]{:S(2)}, u32[]{:S(2)}) %collective-permute-start.36) | collective-permute-done | bytes 884768 | tf_op jit(solution)/shard_map/ppermute | solution.py:552
  223.8 13.3 %collective-permute-done.39.refs_3_ = bf16[384,1152]{1,0:T(8,128)(2,1)S(1)} collective-permute-done((bf16[384,1152]{1,0:T(8,128)(2,1)S(1)}, bf16[384,1152]{1,0:T(8,128)(2,1)S(1)}, u32[]{:S(2)}, u32[]{:S(2)}) %collective-permute-start.39) | collective-permute-done | bytes 884768 | tf_op jit(solution)/shard_map/ppermute | solution.py:552
  242.9 7.2 %shard_map.270.refs_0_ = bf16[768,864]{1,0:T(8,128)(2,1)S(1)} custom-call(bf16[384,1152]{1,0:T(8,128)(2,1)S(1)} %get-tuple-element.191.refs_0_, bf16[384,1152]{1,0:T(8,128)(2,1)S(1)} %collective-permute-done.41.refs_1_, bf16[288,1152]{1,0:T(8,128)(2,1)S(1)} %bitcast.91, bf16[768,512]{1,0:T(8,128)(2,1)S(1)} %copy-done.116, bf16[768,512]{1,0:T(8,128)(2,1)S(1)} %copy-done.119, ...), custom_call_target="tpu_custom_call" | custom-call | flops 49413095424 | bytes 6144000 | tf_op jit(solution)/shard_map/pallas_call | solution.py:36
  253.9 8.6 %collective-permute-done.44.refs_3_ = bf16[384,1152]{1,0:T(8,128)(2,1)S(1)} collective-permute-done((bf16[384,1152]{1,0:T(8,128)(2,1)S(1)}, bf16[384,1152]{1,0:T(8,128)(2,1)S(1)}, u32[]{:S(2)}, u32[]{:S(2)}) %collective-permute-start.44) | collective-permute-done | bytes 884768 | tf_op jit(solution)/shard_map/ppermute | solution.py:552
  268.4 7.2 %shard_map.275.refs_0_ = bf16[768,864]{1,0:T(8,128)(2,1)S(1)} custom-call(bf16[384,1152]{1,0:T(8,128)(2,1)S(1)} %get-tuple-element.198.refs_0_, bf16[384,1152]{1,0:T(8,128)(2,1)S(1)} %collective-permute-done.45.refs_1_, bf16[288,1152]{1,0:T(8,128)(2,1)S(1)} %bitcast.92, bf16[768,512]{1,0:T(8,128)(2,1)S(1)} %copy-done.125, bf16[768,512]{1,0:T(8,128)(2,1)S(1)} %copy-done.128, ...), custom_call_target="tpu_custom_call" | custom-call | flops 49413095424 | bytes 6144000 | tf_op jit(solution)/shard_map/pallas_call | solution.py:36
  285.8 6.0 collective-permute-done.48.refs_3_
  311.7 6.7 collective-permute-done.59.refs_3_
  335.4 7.2 %shard_map.287.refs_4_ = bf16[1076,1152]{1,0:T(8,128)(2,1)} custom-call(bf16[384,1076]{1,0:T(8,128)(2,1)S(1)} %get-tuple-element.216.refs_0_, bf16[384,1152]{1,0:T(8,128)(2,1)S(1)} %get-tuple-element.205.refs_0_.refs_1_, bf16[384,1076]{1,0:T(8,128)(2,1)S(1)} %get-tuple-element.217.refs_2_, bf16[384,1152]{1,0:T(8,128)(2,1)S(1)} %get-tuple-element.208.refs_0_.refs_3_, ...), custom_call_target="tpu_custom_call" | custom-call | flops 53310652416 | bytes 9323520 | tf_op jit(solution)/shard_map/pallas_call | solution.py:36
  378.9 8.6 %shard_map.291.refs_0_ = bf16[768,864]{1,0:T(8,128)(2,1)S(1)} custom-call(bf16[384,1152]{1,0:T(8,128)(2,1)} %get-tuple-element.222.refs_0_.refs_1_, bf16[384,1152]{1,0:T(8,128)(2,1)} %collective-permute-done.67.refs_1_.refs_3_, bf16[288,1152]{1,0:T(8,128)(2,1)S(1)} %bitcast.93, bf16[768,512]{1,0:T(8,128)(2,1)S(1)} %copy-done.117, ...), custom_call_target="tpu_custom_call" | custom-call | flops 49413095424 | bytes 6144000 | tf_op jit(solution)/shard_map/pallas_call | solution.py:36
  402.1 7.2 %shard_map.296.refs_0_.refs_2_ = bf16[768,864]{1,0:T(8,128)(2,1)S(1)} custom-call(bf16[384,1152]{1,0:T(8,128)(2,1)S(1)} %get-tuple-element.226.refs_0_.refs_5_, bf16[384,1152]{1,0:T(8,128)(2,1)S(1)} %collective-permute-done.71.refs_1_.refs_7_, bf16[288,1152]{1,0:T(8,128)(2,1)S(1)} %bitcast.94, bf16[768,512]{1,0:T(8,128)(2,1)S(1)} %copy-done.126, ...), custom_call_target="tpu_custom_call" | custom-call | flops 49413095424 | bytes 6144000 | tf_op jit(solution)/shard_map/pallas_call | solution.py:36
  422.7 5.7 shard_map.306.refs_0_
  442.2 11.9 %psum.42 = bf16[6,1152]{1,0:T(8,128)(2,1)S(1)} all-reduce(f32[6,1152]{1,0:T(8,128)S(1)} %add.99), channel_id=1, replica_groups=mesh['section'=2,'tensor'=4,'dp'=4] {'tensor'}, use_global_device_ids=true, to_apply=%region_0.1 | all-reduce | flops 6912 | bytes 41472 | tf_op jit(solution)/shard_map/psum | solution.py:831
  456.4 16.1 %all-reduce.6.cloned.1.call-done.refs_4_.value_ref = bf16[1076,1152]{1,0:T(8,128)(2,1)} async-done(((bf16[1076,1152]{1,0:T(8,128)(2,1)}), bf16[1076,1152]{1,0:T(8,128)(2,1)}) %all-reduce.6.cloned.1.call-update) | async-done | bytes 2479120 | tf_op jit(solution)/shard_map/psum | solution.py:801
  479.1 10.4 %collective-permute-done.74.refs_2_ = bf16[192,1152]{1,0:T(8,128)(2,1)S(1)} collective-permute-done((bf16[192,1152]{1,0:T(8,128)(2,1)S(1)}, bf16[192,1152]{1,0:T(8,128)(2,1)S(1)}, u32[]{:S(2)}, u32[]{:S(2)}) %collective-permute-start.74) | collective-permute-done | bytes 442400 | tf_op jit(solution)/shard_map/ppermute | solution.py:552
  490.3 7.8 %collective-permute-done.77.refs_2_ = bf16[192,1152]{1,0:T(8,128)(2,1)S(1)} collective-permute-done((bf16[192,1152]{1,0:T(8,128)(2,1)S(1)}, bf16[192,1152]{1,0:T(8,128)(2,1)S(1)}, u32[]{:S(2)}, u32[]{:S(2)}) %collective-permute-start.77) | collective-permute-done | bytes 442400 | tf_op jit(solution)/shard_map/ppermute | solution.py:552
  511.8 22.9 %psum.44 = bf16[16,1152]{1,0:T(8,128)(2,1)S(1)} all-reduce(bf16[16,1152]{1,0:T(8,128)(2,1)S(1)} %copy-done.158), channel_id=1, replica_groups=mesh['section'=2,'tensor'=4,'dp'=4] {'dp'}, use_global_device_ids=true, to_apply=%region_8.9 | all-reduce | flops 18432 | bytes 73728 | tf_op jit(solution)/shard_map/psum | solution.py:844
  546.1 116.6 %all-reduce.8.cloned.1.call-done = (bf16[864,1152]{1,0:T(8,128)(2,1)}, bf16[1,288,1152]{2,1,0:T(8,128)(2,1)}, bf16[1076,1152]{1,0:T(8,128)(2,1)}) async-done(((bf16[864,1152]{1,0:T(8,128)(2,1)}, bf16[1,288,1152]{2,1,0:T(8,128)(2,1)}, bf16[1076,1152]{1,0:T(8,128)(2,1)}), (bf16[864,1152]{1,0:T(8,128)(2,1)}, bf16[1,288,1152]{2,1,0:T(8,128)(2,1)}, bf16[1076,1152]{1,0:T(8,128)(2,1)})) %all-reduce.8.cloned.1.call-update) | async-done | bytes 5133328 | tf_op jit(solution)/shard_map/psum | solution.py:844
  (609 shorter events, 336.0 us)
Async XLA Ops:
  10.2 14.8 %collective-permute-start = (bf16[288,792]{1,0:T(8,128)(2,1)S(1)}, bf16[288,792]{1,0:T(8,128)(2,1)S(1)}, u32[]{:S(2)}, u32[]{:S(2)}) collective-permute-start(bf16[288,792]{1,0:T(8,128)(2,1)S(1)} %fusion.1.refs_2_), channel_id=1, source_target_pairs={{0,8},{4,12},{8,0},{12,4},{1,9},{5,13},{9,1},{13,5},{2,10},{6,14},... | collective-permute-start | bytes 1368584 | tf_op jit(solution)/shard_map/ppermute | solution.py:552
  13.2 13.6 %collective-permute-start.1 = (bf16[288,792]{1,0:T(8,128)(2,1)S(1)}, bf16[288,792]{1,0:T(8,128)(2,1)}, u32[]{:S(2)}, u32[]{:S(2)}) collective-permute-start(bf16[288,792]{1,0:T(8,128)(2,1)S(1)} %fusion.1.refs_2_), channel_id=1, source_target_pairs={{0,4},{4,0},{8,12},{12,8},{1,5},{5,1},{9,13},{13,9},{2,6},{6,2},{1... | collective-permute-start | bytes 1368584 | tf_op jit(solution)/shard_map/ppermute | solution.py:547
  31.1 17.9 %collective-permute-start.6 = (bf16[288,729]{1,0:T(8,128)(2,1)}, bf16[288,729]{1,0:T(8,128)(2,1)S(1)}, u32[]{:S(2)}, u32[]{:S(2)}) collective-permute-start(bf16[288,729]{1,0:T(8,128)(2,1)} %shard_map.233.refs_2_), channel_id=1, source_target_pairs={{0,4},{4,0},{8,12},{12,8},{1,5},{5,1},{9,13},{13,9},{2,6},{6,2},{1... | collective-permute-start | bytes 1259720 | tf_op jit(solution)/shard_map/ppermute | solution.py:547
  47.2 22.1 %collective-permute-start.4 = (bf16[384,1152]{1,0:T(8,128)(2,1)S(1)}, bf16[384,1152]{1,0:T(8,128)(2,1)S(1)}, u32[]{:S(2)}, u32[]{:S(2)}) collective-permute-start(bf16[384,1152]{1,0:T(8,128)(2,1)S(1)} %shard_map.232.refs_6_.refs_7_.refs_1_), channel_id=1, source_target_pairs={{0,8},{4,12},{8,0},{12,4},{1,9},{5,13},{9,1},{13,5},{2,10},{6,14},... | collective-permute-start | bytes 2654216 | tf_op jit(solution)/shard_map/ppermute | solution.py:552
  71.7 22.1 %collective-permute-start.12 = (bf16[384,1152]{1,0:T(8,128)(2,1)S(1)}, bf16[384,1152]{1,0:T(8,128)(2,1)S(1)}, u32[]{:S(2)}, u32[]{:S(2)}) collective-permute-start(bf16[384,1152]{1,0:T(8,128)(2,1)S(1)} %shard_map.238.refs_6_.refs_1_), channel_id=1, source_target_pairs={{0,8},{4,12},{8,0},{12,4},{1,9},{5,13},{9,1},{13,5},{2,10},{6,14},... | collective-permute-start | bytes 2654216 | tf_op jit(solution)/shard_map/ppermute | solution.py:552
  104.2 19.6 %collective-permute-start.23 = (bf16[192,1152]{1,0:T(8,128)(2,1)S(1)}, bf16[192,1152]{1,0:T(8,128)(2,1)S(1)}, u32[]{:S(2)}, u32[]{:S(2)}) collective-permute-start(bf16[192,1152]{1,0:T(8,128)(2,1)S(1)} %get-tuple-element.160.refs_5_), channel_id=1, source_target_pairs={{0,8},{4,12},{8,0},{12,4},{1,9},{5,13},{9,1},{13,5},{2,10},{6,14},... | collective-permute-start | bytes 1327112 | tf_op jit(solution)/shard_map/ppermute | solution.py:552
  123.8 16.6 %collective-permute-start.19 = (bf16[96,1152]{1,0:T(8,128)(2,1)}, bf16[96,1152]{1,0:T(8,128)(2,1)}, u32[]{:S(2)}, u32[]{:S(2)}) collective-permute-start(bf16[96,1152]{1,0:T(8,128)(2,1)} %collective-permute-done.15.refs_3_), channel_id=1, source_target_pairs={{0,4},{4,0},{8,12},{12,8},{1,5},{5,1},{9,13},{13,9},{2,6},{6,2},{1... | collective-permute-start | bytes 663560 | tf_op jit(solution)/shard_map/ppermute | solution.py:547
  135.5 18.2 %collective-permute-start.29 = (bf16[96,1152]{1,0:T(8,128)(2,1)S(1)}, bf16[96,1152]{1,0:T(8,128)(2,1)S(1)}, u32[]{:S(2)}, u32[]{:S(2)}) collective-permute-start(bf16[96,1152]{1,0:T(8,128)(2,1)S(1)} %collective-permute-done.27.refs_4_), channel_id=1, source_target_pairs={{0,8},{4,12},{8,0},{12,4},{1,9},{5,13},{9,1},{13,5},{2,10},{6,14},... | collective-permute-start | bytes 663560 | tf_op jit(solution)/shard_map/ppermute | solution.py:552
  139.9 14.3 %collective-permute-start.28 = (bf16[96,1152]{1,0:T(8,128)(2,1)S(1)}, bf16[96,1152]{1,0:T(8,128)(2,1)S(1)}, u32[]{:S(2)}, u32[]{:S(2)}) collective-permute-start(bf16[96,1152]{1,0:T(8,128)(2,1)S(1)} %collective-permute-done.26.refs_3_), channel_id=1, source_target_pairs={{0,8},{4,12},{8,0},{12,4},{1,9},{5,13},{9,1},{13,5},{2,10},{6,14},... | collective-permute-start | bytes 663560 | tf_op jit(solution)/shard_map/ppermute | solution.py:552
  157.6 22.5 %collective-permute-start.25 = (bf16[384,1152]{1,0:T(8,128)(2,1)S(1)}, bf16[384,1152]{1,0:T(8,128)(2,1)S(1)}, u32[]{:S(2)}, u32[]{:S(2)}) collective-permute-start(bf16[384,1152]{1,0:T(8,128)(2,1)S(1)} %shard_map.252.refs_16_.refs_1_), channel_id=1, source_target_pairs={{0,8},{4,12},{8,0},{12,4},{1,9},{5,13},{9,1},{13,5},{2,10},{6,14},... | collective-permute-start | bytes 2654216 | tf_op jit(solution)/shard_map/ppermute | solution.py:552
  171.8 26.8 %collective-permute-start.36 = (bf16[384,1152]{1,0:T(8,128)(2,1)S(1)}, bf16[384,1152]{1,0:T(8,128)(2,1)S(1)}, u32[]{:S(2)}, u32[]{:S(2)}) collective-permute-start(bf16[384,1152]{1,0:T(8,128)(2,1)S(1)} %shard_map.256.refs_6_.refs_1_), channel_id=1, source_target_pairs={{0,8},{4,12},{8,0},{12,4},{1,9},{5,13},{9,1},{13,5},{2,10},{6,14},... | collective-permute-start | bytes 2654216 | tf_op jit(solution)/shard_map/ppermute | solution.py:552
  215.5 21.6 %collective-permute-start.39 = (bf16[384,1152]{1,0:T(8,128)(2,1)S(1)}, bf16[384,1152]{1,0:T(8,128)(2,1)S(1)}, u32[]{:S(2)}, u32[]{:S(2)}) collective-permute-start(bf16[384,1152]{1,0:T(8,128)(2,1)S(1)} %shard_map.265.refs_4_.refs_2_), channel_id=1, source_target_pairs={{0,8},{4,12},{8,0},{12,4},{1,9},{5,13},{9,1},{13,5},{2,10},{6,14},... | collective-permute-start | bytes 2654216 | tf_op jit(solution)/shard_map/ppermute | solution.py:552
  240.4 22.1 %collective-permute-start.44 = (bf16[384,1152]{1,0:T(8,128)(2,1)S(1)}, bf16[384,1152]{1,0:T(8,128)(2,1)S(1)}, u32[]{:S(2)}, u32[]{:S(2)}) collective-permute-start(bf16[384,1152]{1,0:T(8,128)(2,1)S(1)} %shard_map.268.refs_5_.refs_2_), channel_id=1, source_target_pairs={{0,8},{4,12},{8,0},{12,4},{1,9},{5,13},{9,1},{13,5},{2,10},{6,14},... | collective-permute-start | bytes 2654216 | tf_op jit(solution)/shard_map/ppermute | solution.py:552
  266.0 13.5 %collective-permute-start.43 = (bf16[192,1152]{1,0:T(8,128)(2,1)S(1)}, bf16[192,1152]{1,0:T(8,128)(2,1)S(1)}, u32[]{:S(2)}, u32[]{:S(2)}) collective-permute-start(bf16[192,1152]{1,0:T(8,128)(2,1)S(1)} %get-tuple-element.195.refs_6_), channel_id=1, source_target_pairs={{0,8},{4,12},{8,0},{12,4},{1,9},{5,13},{9,1},{13,5},{2,10},{6,14},... | collective-permute-start | bytes 1327112 | tf_op jit(solution)/shard_map/ppermute | solution.py:552
  284.3 21.9 %collective-permute-start.55 = (bf16[192,1152]{1,0:T(8,128)(2,1)S(1)}, bf16[192,1152]{1,0:T(8,128)(2,1)S(1)}, u32[]{:S(2)}, u32[]{:S(2)}) collective-permute-start(bf16[192,1152]{1,0:T(8,128)(2,1)S(1)} %get-tuple-element.202.refs_6_), channel_id=1, source_target_pairs={{0,8},{4,12},{8,0},{12,4},{1,9},{5,13},{9,1},{13,5},{2,10},{6,14},... | collective-permute-start | bytes 1327112 | tf_op jit(solution)/shard_map/ppermute | solution.py:552
  297.4 14.1 %collective-permute-start.51 = (bf16[96,1152]{1,0:T(8,128)(2,1)S(1)}, bf16[96,1152]{1,0:T(8,128)(2,1)S(1)}, u32[]{:S(2)}, u32[]{:S(2)}) collective-permute-start(bf16[96,1152]{1,0:T(8,128)(2,1)S(1)} %collective-permute-done.47.refs_2_), channel_id=1, source_target_pairs={{0,4},{4,0},{8,12},{12,8},{1,5},{5,1},{9,13},{13,9},{2,6},{6,2},{1... | collective-permute-start | bytes 663560 | tf_op jit(solution)/shard_map/ppermute | solution.py:547
  333.8 29.7 %collective-permute-start.57 = (bf16[384,1152]{1,0:T(8,128)(2,1)S(1)}, bf16[384,1152]{1,0:T(8,128)(2,1)}, u32[]{:S(2)}, u32[]{:S(2)}) collective-permute-start(bf16[384,1152]{1,0:T(8,128)(2,1)S(1)} %shard_map.284.refs_8_.refs_2_), channel_id=1, source_target_pairs={{0,8},{4,12},{8,0},{12,4},{1,9},{5,13},{9,1},{13,5},{2,10},{6,14},... | collective-permute-start | bytes 2654216 | tf_op jit(solution)/shard_map/ppermute | solution.py:552
  353.0 119.5 %all-reduce.6.cloned.1.call-start = ((), (), s32[]{:S(2)}) async-start(), calls=%async_computation.1 | async-start | bytes 4976640 | tf_op jit(solution)/shard_map/psum | solution.py:801
  372.6 290.1 %all-reduce.8.cloned.1.call-start = ((), (), s32[]{:S(2)}) async-start(), calls=%async_computation.2 | async-start | bytes 10285056 | tf_op jit(solution)/shard_map/psum | solution.py:844
  374.3 21.8 %collective-permute-start.70 = (bf16[384,1152]{1,0:T(8,128)(2,1)S(1)}, bf16[384,1152]{1,0:T(8,128)(2,1)S(1)}, u32[]{:S(2)}, u32[]{:S(2)}) collective-permute-start(bf16[384,1152]{1,0:T(8,128)(2,1)S(1)} %shard_map.289.refs_5_.refs_2_), channel_id=1, source_target_pairs={{0,8},{4,12},{8,0},{12,4},{1,9},{5,13},{9,1},{13,5},{2,10},{6,14},... | collective-permute-start | bytes 2654216 | tf_op jit(solution)/shard_map/ppermute | solution.py:552
  400.2 28.3 %collective-permute-start.69 = (bf16[192,1152]{1,0:T(8,128)(2,1)}, bf16[192,1152]{1,0:T(8,128)(2,1)}, u32[]{:S(2)}, u32[]{:S(2)}) collective-permute-start(bf16[192,1152]{1,0:T(8,128)(2,1)} %get-tuple-element.224.refs_6_), channel_id=1, source_target_pairs={{0,8},{4,12},{8,0},{12,4},{1,9},{5,13},{9,1},{13,5},{2,10},{6,14},... | collective-permute-start | bytes 1327112 | tf_op jit(solution)/shard_map/ppermute | solution.py:552
  421.5 14.2 %collective-permute-start.75 = (bf16[192,1152]{1,0:T(8,128)(2,1)}, bf16[192,1152]{1,0:T(8,128)(2,1)}, u32[]{:S(2)}, u32[]{:S(2)}) collective-permute-start(bf16[192,1152]{1,0:T(8,128)(2,1)} %get-tuple-element.228.refs_6_.refs_9_), channel_id=1, source_target_pairs={{0,8},{4,12},{8,0},{12,4},{1,9},{5,13},{9,1},{13,5},{2,10},{6,14},... | collective-permute-start | bytes 1327112 | tf_op jit(solution)/shard_map/ppermute | solution.py:552
  478.1 20.1 %collective-permute-start.77 = (bf16[192,1152]{1,0:T(8,128)(2,1)S(1)}, bf16[192,1152]{1,0:T(8,128)(2,1)S(1)}, u32[]{:S(2)}, u32[]{:S(2)}) collective-permute-start(bf16[192,1152]{1,0:T(8,128)(2,1)S(1)} %get-tuple-element.241), channel_id=1, source_target_pairs={{0,8},{4,12},{8,0},{12,4},{1,9},{5,13},{9,1},{13,5},{2,10},{6,14},... | collective-permute-start | bytes 1327112 | tf_op jit(solution)/shard_map/ppermute | solution.py:552
  502.5 34.9 %all-to-all-start = ((f32[2,192,4,288]{3,1,0,2:T(8,128)}), f32[2,192,4,288]{3,1,0,2:T(8,128)}, u32[]{:S(2)}, u32[]{:S(2)}) async-start(f32[2,192,4,288]{3,1,0,2:T(8,128)} %pad_maximum_fusion), calls=%async_computation | async-start | bytes 4718592 | tf_op jit(solution)/shard_map/all_to_all | solution.py:851
  (221 other events, 2508.5 us)
Sparse Core Ops, SparseCore 0:
  372.7 99.7 all-reduce.5
  475.7 186.9 all-reduce.7

commit v5 on v4

--- a/solution.py
+++ b/solution.py
@@ -158,7 +158,7 @@
     return run(body, [shape, shape], (*scalars, *arrays), scalars=len(scalars), flops=rows * width)
 
 
-def project(info, source, gain, bias, weight, shift, rows, after=()):
+def project(info, source, gain, bias, weight, shift, rows, save, after=()):
     cols, width = weight.shape[0] // 3, weight.shape[1]
     heads = cols // HD
     scalars, arrays = source.operands((0, 1))
@@ -170,7 +170,7 @@
         info_ref, flags = refs[0], refs[1 : 1 + len(scalars)]
         refs = refs[1 + len(scalars) :]
         read = source.reader((0, 1), flags, refs[:count])
-        g_ref, b_ref, w_ref, s_ref, x_ref, n_ref, *outs = refs[count:]
+        g_ref, b_ref, w_ref, s_ref, x_ref, *outs, n_ref = refs[count:]
         for index in (0, 1):
             for at in range(0, half, step):
                 value = read(index, at, step)
@@ -187,7 +187,7 @@
         ones = jnp.where(lane == 0, 1.0, 0.0).astype(BF16)
         mask = jnp.where((lane == 0) & padded, FAR, 0.0).astype(BF16)
         normed = n_ref[...]
-        for i, (out, extra) in enumerate(zip(outs, (ones, mask, ones))):
+        for i, (out, extra) in enumerate(zip(outs[:3], (ones, mask, ones))):
             here = slice(i * cols, (i + 1) * cols)
             value = (mm_nt(normed, w_ref[here, :]) + s_ref[:, here]).astype(BF16)
             for h in range(heads):
@@ -198,21 +198,23 @@
     wide = ((total, heads * LANES), BF16)
     return run(
         body,
-        [((half, width), BF16), ((total, width), BF16), wide, wide, wide],
+        [((half, width), BF16), wide, wide, wide] + ([((total, width), BF16)] if save else []),
         (info, *scalars, *arrays, gain, bias, weight, shift),
         scalars=1 + len(scalars),
         flops=6 * total * width * cols,
+        scratch=() if save else (pltpu.VMEM((total, width), BF16),),
+        limit=LIMIT if save else LIMIT + 2,
         after=after,
     )
 
 
-def attend(first_row, q, k, v, wout, out_type):
+def attend(first_row, q, k, v, wout, out_type, save):
     total, wide = q.shape
     heads = wide // LANES
     half = total // 2
     step = half
 
-    def body(q_ref, k_ref, v_ref, w_ref, z_ref, o_ref, l_ref):
+    def body(q_ref, k_ref, v_ref, w_ref, z_ref, *saved):
         for at in range(0, half, step):
             outs, logs = [], []
             for h in range(heads):
@@ -225,14 +227,17 @@
                 outs.append((mixed / sums).astype(BF16)[:, :HD])
                 logs.append(highest * (SCALE * LOG2E) + jnp.log(sums) * LOG2E)
             mixed = jnp.concatenate(outs, axis=1)
-            o_ref[at : at + step, :] = mixed
             z_ref[at : at + step, :] = mm(mixed, w_ref[...]).astype(out_type)
+            if not save:
+                continue
+            saved[0][at : at + step, :] = mixed
             logs = jnp.concatenate(logs + [jnp.zeros((step, LANES - heads), F32)], axis=1)
-            l_ref[:, at : at + step] = logs.T[:8, :]
+            saved[1][:, at : at + step] = logs.T[:8, :]
 
     return run(
         body,
-        [((half, wout.shape[1]), out_type), ((half, heads * HD), BF16), ((8, half), F32)],
+        [((half, wout.shape[1]), out_type)]
+        + ([((half, heads * HD), BF16), ((8, half), F32)] if save else []),
         (q, k, v, wout),
         flops=4 * half * total * LANES * heads + 2 * half * heads * HD * wout.shape[1],
     )
@@ -296,27 +301,20 @@
     return run(body, outs, (n2, w_up, b_up, w_down), flops=4 * half * width * hidden)
 
 
-def mlp_back(which, source, slope, w_up, w_down, out_type, after=()):
+def mlp_back(g, slope, w_up, w_down, out_type, save, after=()):
     half, hidden = slope.shape
     width = w_up.shape[1]
-    scalars, arrays = source.operands((which,))
-    count = len(arrays)
-    step = half // 2 if source.blocks is None else source.blocks[0][0].shape[0]
-
-    def body(*refs):
-        read = source.reader((which,), refs[: len(scalars)], refs[len(scalars) :][:count])
-        s_ref, wu_ref, wd_ref, g_ref, z_ref, d_ref = refs[len(scalars) + count :]
-        for at in range(0, half, step):
-            g_ref[at : at + step, :] = read(which, at, step)
+
+    def body(g_ref, s_ref, wu_ref, wd_ref, z_ref, *saved):
         grad = (mm_nt(g_ref[...], wd_ref[...]) * s_ref[...].astype(F32)).astype(BF16)
-        d_ref[...] = grad
+        if save:
+            saved[0][...] = grad
         z_ref[...] = mm(grad, wu_ref[...]).astype(out_type)
 
     return run(
         body,
-        [((half, width), BF16), ((half, width), out_type), ((half, hidden), BF16)],
-        (*scalars, *arrays, slope, w_up, w_down),
-        scalars=len(scalars),
+        [((half, width), out_type)] + ([((half, hidden), BF16)] if save else []),
+        (g, slope, w_up, w_down),
         flops=4 * half * width * hidden,
         after=after,
     )
@@ -604,14 +602,15 @@
 
 def forward(source, w, info, chips, rows, save, turns):
     source = source()
-    xm, normed, q, k, v = project(
-        info, source, w["gain"][0], w["bias"][0], w["qkv"], w["qkv_shift"], rows, turns.take(),
+    xm, q, k, v, *kept = project(
+        info, source, w["gain"][0], w["bias"][0], w["qkv"], w["qkv_shift"], rows, save,
+        turns.take(),
     )
     turns.first = (q,)
     half = rows // 2
-    z_other, o_other, l_other = attend(half, q, k, v, w["wout"], BF16)
+    z_other, *kept_other = attend(half, q, k, v, w["wout"], BF16, save)
     z_other = core_swap(z_other)
-    z_mine, o_mine, l_mine = attend(0, q, k, v, w["wout"], F32)
+    z_mine, *kept_mine = attend(0, q, k, v, w["wout"], F32, save)
     own = add(z_mine, z_other)
     turns.end(own)
     arrived = share_half(own, chips)
@@ -627,7 +626,8 @@
     saved = None
     if save:
         saved = dict(
-            x=xm, normed=normed, q=q, k=k, v=v, o=(o_mine, o_other), l=(l_mine, l_other),
+            x=xm, normed=kept[0], q=q, k=k, v=v,
+            o=(kept_mine[0], kept_other[0]), l=(kept_mine[1], kept_other[1]),
             h=hidden, n2=(n2m, n2o), m=(mine[1], other[1]), slope=(mine[2], other[2]),
         )
         turns.end(mine[2], other[2])
@@ -641,17 +641,17 @@
 
 
 def backward(source, saved, w, chips, turns, pass_on):
-    source = source()
-    go, z_other, du_other = mlp_back(
-        1, source, saved["slope"][1], w["w_up"], w["w_down"], BF16, turns.take()
-    )
-    turns.first = (go,)
+    gm, go = source().halves
+    save = not pass_on
+    z_other, *du_other = mlp_back(
+        go, saved["slope"][1], w["w_up"], w["w_down"], BF16, save, turns.take()
+    )
     z_other = core_swap(z_other)
-    gm, z_mine, du_mine = mlp_back(0, source, saved["slope"][0], w["w_up"], w["w_down"], F32)
+    z_mine, *du_mine = mlp_back(gm, saved["slope"][0], w["w_up"], w["w_down"], F32, save)
     own = add(z_mine, z_other)
     turns.end(own)
     arrived = share_half(own, chips)
-    work = dict(g=(gm, go), du=(du_mine, du_other))
+    work = dict(du=(*du_mine, *du_other))
     yield work
     dh, dhm, sums_two = middle_back(
         gm, saved["h"], own, arrived, w["gain"][1], turns.take()

time: 690 us -> 692 us (level)
  waiting for transfers between devices: 277 us -> 284 us
    ppermute x26, waiting for transfers between devices: 105 us -> 112 us  [chip_shift(): lax.ppermute(value, 'tensor', [(i, (i + 2 * shift) % size) for i in range...]
    unnamed x329 -> x327, local copies, waits for them, and re-layouts: 45.5 us -> 44.4 us
  transfers between devices with their start and end apart: 81 -> 81, of which waited for: 34 -> 34; matrix products, arithmetic and copies ran while one was open for 4% -> 4% of each run, Pallas kernels for 25% -> 24%
where the time goes in v5:
time: 692 us; the launch traced here: 681 us
  waiting for transfers between devices  284 us (41%)
  Pallas kernels  202 us (29%)
  starting transfers between devices  67.5 us (10%)
  local copies, waits for them, and re-layouts  63.9 us (9%)
  blocking collectives  34.7 us (5%)
  between operations  17.1 us (2%)
  other arithmetic  12.7 us (2%)
    pallas_call x80, Pallas kernels, run(): pl.pallas_call(kernel, out_shape=[jax.ShapeDtypeStruct(shape, dtype) for...  192 us
    psum x1, waiting for transfers between devices, per_device(): g_up, g_out, g_qkv, vector = lax.psum(rest, 'dp')  117 us
    ppermute x26, waiting for transfers between devices, chip_shift(): lax.ppermute(value, 'tensor', [(i, (i + 2 * shift) % size) for i in range...  112 us
    unnamed x327, local copies, waits for them, and re-layouts  44.4 us
    ppermute x26, starting transfers between devices, chip_shift(): lax.ppermute(value, 'tensor', [(i, (i + 2 * shift) % size) for i in range...  38.2 us
    ppermute x8, waiting for transfers between devices, to_section(): return lax.ppermute(value, 'section', pairs)  30.5 us
    psum x1, blocking collectives, per_device(): g_up, g_out, g_qkv, vector = lax.psum(rest, 'dp')  22.8 us
    ppermute x8, starting transfers between devices, to_section(): return lax.ppermute(value, 'section', pairs)  17.2 us
  transfers between devices with their start and end apart: 81, of which 34 were waited for; matrix products, arithmetic and copies ran while one was open for 4% of the time, Pallas kernels for 24%

profile of v5, /device:TPU:0, one launch (start us, length us, event | category | flops | bytes accessed | tf_op | source)
XLA Modules:
  0.0 681.4 jit_solution(13185285891831201362)
XLA Ops:
  14.5 10.5 %collective-permute-done.refs_3_ = bf16[288,792]{1,0:T(8,128)(2,1)S(1)} collective-permute-done((bf16[288,792]{1,0:T(8,128)(2,1)S(1)}, bf16[288,792]{1,0:T(8,128)(2,1)S(1)}, u32[]{:S(2)}, u32[]{:S(2)}) %collective-permute-start) | collective-permute-done | bytes 456224 | tf_op jit(solution)/shard_map/ppermute | solution.py:550
  49.9 4.9 shard_map.235
  60.6 8.2 %collective-permute-done.4.refs_2_ = bf16[384,1152]{1,0:T(8,128)(2,1)S(1)} collective-permute-done((bf16[384,1152]{1,0:T(8,128)(2,1)S(1)}, bf16[384,1152]{1,0:T(8,128)(2,1)S(1)}, u32[]{:S(2)}, u32[]{:S(2)}) %collective-permute-start.4) | collective-permute-done | bytes 884768 | tf_op jit(solution)/shard_map/ppermute | solution.py:550
  79.7 13.6 %collective-permute-done.12.refs_2_ = bf16[384,1152]{1,0:T(8,128)(2,1)S(1)} collective-permute-done((bf16[384,1152]{1,0:T(8,128)(2,1)S(1)}, bf16[384,1152]{1,0:T(8,128)(2,1)S(1)}, u32[]{:S(2)}, u32[]{:S(2)}) %collective-permute-start.12) | collective-permute-done | bytes 884768 | tf_op jit(solution)/shard_map/ppermute | solution.py:550
  143.1 5.6 shard_map.249
  158.5 5.0 shard_map.253
  171.1 8.2 %collective-permute-done.25.refs_2_ = bf16[384,1152]{1,0:T(8,128)(2,1)S(1)} collective-permute-done((bf16[384,1152]{1,0:T(8,128)(2,1)S(1)}, bf16[384,1152]{1,0:T(8,128)(2,1)S(1)}, u32[]{:S(2)}, u32[]{:S(2)}) %collective-permute-start.25) | collective-permute-done | bytes 884768 | tf_op jit(solution)/shard_map/ppermute | solution.py:550
  188.8 9.1 %collective-permute-done.36.refs_2_ = bf16[384,1152]{1,0:T(8,128)(2,1)S(1)} collective-permute-done((bf16[384,1152]{1,0:T(8,128)(2,1)S(1)}, bf16[384,1152]{1,0:T(8,128)(2,1)S(1)}, u32[]{:S(2)}, u32[]{:S(2)}) %collective-permute-start.36) | collective-permute-done | bytes 884768 | tf_op jit(solution)/shard_map/ppermute | solution.py:550
  223.1 16.9 %collective-permute-done.39.refs_3_ = bf16[384,1152]{1,0:T(8,128)(2,1)S(1)} collective-permute-done((bf16[384,1152]{1,0:T(8,128)(2,1)S(1)}, bf16[384,1152]{1,0:T(8,128)(2,1)S(1)}, u32[]{:S(2)}, u32[]{:S(2)}) %collective-permute-start.39) | collective-permute-done | bytes 884768 | tf_op jit(solution)/shard_map/ppermute | solution.py:550
  245.8 7.2 %shard_map.270.refs_0_ = bf16[768,864]{1,0:T(8,128)(2,1)S(1)} custom-call(bf16[384,1152]{1,0:T(8,128)(2,1)S(1)} %get-tuple-element.170.refs_0_, bf16[384,1152]{1,0:T(8,128)(2,1)S(1)} %collective-permute-done.41.refs_1_, bf16[288,1152]{1,0:T(8,128)(2,1)S(1)} %bitcast.91, bf16[768,512]{1,0:T(8,128)(2,1)S(1)} %copy-done.115, bf16[768,512]{1,0:T(8,128)(2,1)S(1)} %copy-done.118, ...), custom_call_target="tpu_custom_call" | custom-call | flops 49413095424 | bytes 6144000 | tf_op jit(solution)/shard_map/pallas_call | solution.py:36
  256.9 8.6 %collective-permute-done.44.refs_3_ = bf16[384,1152]{1,0:T(8,128)(2,1)S(1)} collective-permute-done((bf16[384,1152]{1,0:T(8,128)(2,1)S(1)}, bf16[384,1152]{1,0:T(8,128)(2,1)S(1)}, u32[]{:S(2)}, u32[]{:S(2)}) %collective-permute-start.44) | collective-permute-done | bytes 884768 | tf_op jit(solution)/shard_map/ppermute | solution.py:550
  271.4 7.2 %shard_map.275.refs_0_ = bf16[768,864]{1,0:T(8,128)(2,1)S(1)} custom-call(bf16[384,1152]{1,0:T(8,128)(2,1)S(1)} %get-tuple-element.176.refs_0_, bf16[384,1152]{1,0:T(8,128)(2,1)S(1)} %collective-permute-done.45.refs_1_, bf16[288,1152]{1,0:T(8,128)(2,1)S(1)} %bitcast.92, bf16[768,512]{1,0:T(8,128)(2,1)S(1)} %copy-done.124, bf16[768,512]{1,0:T(8,128)(2,1)S(1)} %copy-done.127, ...), custom_call_target="tpu_custom_call" | custom-call | flops 49413095424 | bytes 6144000 | tf_op jit(solution)/shard_map/pallas_call | solution.py:36
  288.8 6.0 collective-permute-done.48.refs_3_
  314.6 6.8 collective-permute-done.59.refs_3_
  337.8 7.2 %shard_map.287.refs_4_ = bf16[1076,1152]{1,0:T(8,128)(2,1)} custom-call(bf16[384,1076]{1,0:T(8,128)(2,1)S(1)} %get-tuple-element.193.refs_0_, bf16[384,1152]{1,0:T(8,128)(2,1)S(1)} %get-tuple-element.183.refs_0_.refs_1_, bf16[384,1076]{1,0:T(8,128)(2,1)S(1)} %get-tuple-element.194.refs_2_, bf16[384,1152]{1,0:T(8,128)(2,1)S(1)} %get-tuple-element.185.refs_0_.refs_3_, ...), custom_call_target="tpu_custom_call" | custom-call | flops 53310652416 | bytes 9323520 | tf_op jit(solution)/shard_map/pallas_call | solution.py:36
  380.4 8.6 %shard_map.291.refs_0_ = bf16[768,864]{1,0:T(8,128)(2,1)S(1)} custom-call(bf16[384,1152]{1,0:T(8,128)(2,1)} %get-tuple-element.199.refs_0_.refs_1_, bf16[384,1152]{1,0:T(8,128)(2,1)} %collective-permute-done.67.refs_1_.refs_3_, bf16[288,1152]{1,0:T(8,128)(2,1)S(1)} %bitcast.93, bf16[768,512]{1,0:T(8,128)(2,1)S(1)} %copy-done.116, ...), custom_call_target="tpu_custom_call" | custom-call | flops 49413095424 | bytes 6144000 | tf_op jit(solution)/shard_map/pallas_call | solution.py:36
  403.6 7.2 %shard_map.296.refs_0_.refs_2_ = bf16[768,864]{1,0:T(8,128)(2,1)S(1)} custom-call(bf16[384,1152]{1,0:T(8,128)(2,1)S(1)} %get-tuple-element.202.refs_0_.refs_5_, bf16[384,1152]{1,0:T(8,128)(2,1)S(1)} %collective-permute-done.71.refs_1_.refs_7_, bf16[288,1152]{1,0:T(8,128)(2,1)S(1)} %bitcast.94, bf16[768,512]{1,0:T(8,128)(2,1)S(1)} %copy-done.125, ...), custom_call_target="tpu_custom_call" | custom-call | flops 49413095424 | bytes 6144000 | tf_op jit(solution)/shard_map/pallas_call | solution.py:36
  424.2 5.7 shard_map.306.refs_0_
  443.7 11.9 %psum.42 = bf16[6,1152]{1,0:T(8,128)(2,1)S(1)} all-reduce(f32[6,1152]{1,0:T(8,128)S(1)} %add.99), channel_id=1, replica_groups=mesh['section'=2,'tensor'=4,'dp'=4] {'tensor'}, use_global_device_ids=true, to_apply=%region_0.1 | all-reduce | flops 6912 | bytes 41472 | tf_op jit(solution)/shard_map/psum | solution.py:831
  457.9 16.2 %all-reduce.6.cloned.1.call-done.refs_4_.value_ref = bf16[1076,1152]{1,0:T(8,128)(2,1)} async-done(((bf16[1076,1152]{1,0:T(8,128)(2,1)}), bf16[1076,1152]{1,0:T(8,128)(2,1)}) %all-reduce.6.cloned.1.call-update) | async-done | bytes 2479120 | tf_op jit(solution)/shard_map/psum | solution.py:801
  480.6 10.4 %collective-permute-done.74.refs_2_ = bf16[192,1152]{1,0:T(8,128)(2,1)S(1)} collective-permute-done((bf16[192,1152]{1,0:T(8,128)(2,1)S(1)}, bf16[192,1152]{1,0:T(8,128)(2,1)S(1)}, u32[]{:S(2)}, u32[]{:S(2)}) %collective-permute-start.74) | collective-permute-done | bytes 442400 | tf_op jit(solution)/shard_map/ppermute | solution.py:550
  491.8 7.8 %collective-permute-done.77.refs_2_ = bf16[192,1152]{1,0:T(8,128)(2,1)S(1)} collective-permute-done((bf16[192,1152]{1,0:T(8,128)(2,1)S(1)}, bf16[192,1152]{1,0:T(8,128)(2,1)S(1)}, u32[]{:S(2)}, u32[]{:S(2)}) %collective-permute-start.77) | collective-permute-done | bytes 442400 | tf_op jit(solution)/shard_map/ppermute | solution.py:550
  513.4 22.8 %psum.44 = bf16[16,1152]{1,0:T(8,128)(2,1)S(1)} all-reduce(bf16[16,1152]{1,0:T(8,128)(2,1)S(1)} %copy-done.157), channel_id=1, replica_groups=mesh['section'=2,'tensor'=4,'dp'=4] {'dp'}, use_global_device_ids=true, to_apply=%region_8.9 | all-reduce | flops 18432 | bytes 73728 | tf_op jit(solution)/shard_map/psum | solution.py:844
  547.6 116.6 %all-reduce.8.cloned.1.call-done = (bf16[864,1152]{1,0:T(8,128)(2,1)}, bf16[1,288,1152]{2,1,0:T(8,128)(2,1)}, bf16[1076,1152]{1,0:T(8,128)(2,1)}) async-done(((bf16[864,1152]{1,0:T(8,128)(2,1)}, bf16[1,288,1152]{2,1,0:T(8,128)(2,1)}, bf16[1076,1152]{1,0:T(8,128)(2,1)}), (bf16[864,1152]{1,0:T(8,128)(2,1)}, bf16[1,288,1152]{2,1,0:T(8,128)(2,1)}, bf16[1076,1152]{1,0:T(8,128)(2,1)})) %all-reduce.8.cloned.1.call-update) | async-done | bytes 5133328 | tf_op jit(solution)/shard_map/psum | solution.py:844
  (607 shorter events, 332.3 us)
Async XLA Ops:
  10.2 14.8 %collective-permute-start = (bf16[288,792]{1,0:T(8,128)(2,1)S(1)}, bf16[288,792]{1,0:T(8,128)(2,1)S(1)}, u32[]{:S(2)}, u32[]{:S(2)}) collective-permute-start(bf16[288,792]{1,0:T(8,128)(2,1)S(1)} %fusion.1.refs_2_), channel_id=1, source_target_pairs={{0,8},{4,12},{8,0},{12,4},{1,9},{5,13},{9,1},{13,5},{2,10},{6,14},... | collective-permute-start | bytes 1368584 | tf_op jit(solution)/shard_map/ppermute | solution.py:550
  13.2 13.6 %collective-permute-start.1 = (bf16[288,792]{1,0:T(8,128)(2,1)S(1)}, bf16[288,792]{1,0:T(8,128)(2,1)}, u32[]{:S(2)}, u32[]{:S(2)}) collective-permute-start(bf16[288,792]{1,0:T(8,128)(2,1)S(1)} %fusion.1.refs_2_), channel_id=1, source_target_pairs={{0,4},{4,0},{8,12},{12,8},{1,5},{5,1},{9,13},{13,9},{2,6},{6,2},{1... | collective-permute-start | bytes 1368584 | tf_op jit(solution)/shard_map/ppermute | solution.py:545
  31.1 17.4 %collective-permute-start.6 = (bf16[288,729]{1,0:T(8,128)(2,1)}, bf16[288,729]{1,0:T(8,128)(2,1)S(1)}, u32[]{:S(2)}, u32[]{:S(2)}) collective-permute-start(bf16[288,729]{1,0:T(8,128)(2,1)} %shard_map.233.refs_2_), channel_id=1, source_target_pairs={{0,4},{4,0},{8,12},{12,8},{1,5},{5,1},{9,13},{13,9},{2,6},{6,2},{1... | collective-permute-start | bytes 1259720 | tf_op jit(solution)/shard_map/ppermute | solution.py:545
  46.7 22.1 %collective-permute-start.4 = (bf16[384,1152]{1,0:T(8,128)(2,1)S(1)}, bf16[384,1152]{1,0:T(8,128)(2,1)S(1)}, u32[]{:S(2)}, u32[]{:S(2)}) collective-permute-start(bf16[384,1152]{1,0:T(8,128)(2,1)S(1)} %shard_map.232.refs_6_.refs_7_.refs_1_), channel_id=1, source_target_pairs={{0,8},{4,12},{8,0},{12,4},{1,9},{5,13},{9,1},{13,5},{2,10},{6,14},... | collective-permute-start | bytes 2654216 | tf_op jit(solution)/shard_map/ppermute | solution.py:550
  71.3 22.1 %collective-permute-start.12 = (bf16[384,1152]{1,0:T(8,128)(2,1)S(1)}, bf16[384,1152]{1,0:T(8,128)(2,1)S(1)}, u32[]{:S(2)}, u32[]{:S(2)}) collective-permute-start(bf16[384,1152]{1,0:T(8,128)(2,1)S(1)} %shard_map.238.refs_6_.refs_1_), channel_id=1, source_target_pairs={{0,8},{4,12},{8,0},{12,4},{1,9},{5,13},{9,1},{13,5},{2,10},{6,14},... | collective-permute-start | bytes 2654216 | tf_op jit(solution)/shard_map/ppermute | solution.py:550
  103.8 19.6 %collective-permute-start.23 = (bf16[192,1152]{1,0:T(8,128)(2,1)S(1)}, bf16[192,1152]{1,0:T(8,128)(2,1)S(1)}, u32[]{:S(2)}, u32[]{:S(2)}) collective-permute-start(bf16[192,1152]{1,0:T(8,128)(2,1)S(1)} %get-tuple-element.144.refs_5_), channel_id=1, source_target_pairs={{0,8},{4,12},{8,0},{12,4},{1,9},{5,13},{9,1},{13,5},{2,10},{6,14},... | collective-permute-start | bytes 1327112 | tf_op jit(solution)/shard_map/ppermute | solution.py:550
  123.4 16.6 %collective-permute-start.19 = (bf16[96,1152]{1,0:T(8,128)(2,1)}, bf16[96,1152]{1,0:T(8,128)(2,1)}, u32[]{:S(2)}, u32[]{:S(2)}) collective-permute-start(bf16[96,1152]{1,0:T(8,128)(2,1)} %collective-permute-done.15.refs_3_), channel_id=1, source_target_pairs={{0,4},{4,0},{8,12},{12,8},{1,5},{5,1},{9,13},{13,9},{2,6},{6,2},{1... | collective-permute-start | bytes 663560 | tf_op jit(solution)/shard_map/ppermute | solution.py:545
  135.1 17.5 %collective-permute-start.29 = (bf16[96,1152]{1,0:T(8,128)(2,1)S(1)}, bf16[96,1152]{1,0:T(8,128)(2,1)S(1)}, u32[]{:S(2)}, u32[]{:S(2)}) collective-permute-start(bf16[96,1152]{1,0:T(8,128)(2,1)S(1)} %collective-permute-done.27.refs_4_), channel_id=1, source_target_pairs={{0,8},{4,12},{8,0},{12,4},{1,9},{5,13},{9,1},{13,5},{2,10},{6,14},... | collective-permute-start | bytes 663560 | tf_op jit(solution)/shard_map/ppermute | solution.py:550
  139.5 13.7 %collective-permute-start.28 = (bf16[96,1152]{1,0:T(8,128)(2,1)S(1)}, bf16[96,1152]{1,0:T(8,128)(2,1)S(1)}, u32[]{:S(2)}, u32[]{:S(2)}) collective-permute-start(bf16[96,1152]{1,0:T(8,128)(2,1)S(1)} %collective-permute-done.26.refs_3_), channel_id=1, source_target_pairs={{0,8},{4,12},{8,0},{12,4},{1,9},{5,13},{9,1},{13,5},{2,10},{6,14},... | collective-permute-start | bytes 663560 | tf_op jit(solution)/shard_map/ppermute | solution.py:550
  156.8 22.5 %collective-permute-start.25 = (bf16[384,1152]{1,0:T(8,128)(2,1)S(1)}, bf16[384,1152]{1,0:T(8,128)(2,1)S(1)}, u32[]{:S(2)}, u32[]{:S(2)}) collective-permute-start(bf16[384,1152]{1,0:T(8,128)(2,1)S(1)} %shard_map.252.refs_16_.refs_1_), channel_id=1, source_target_pairs={{0,8},{4,12},{8,0},{12,4},{1,9},{5,13},{9,1},{13,5},{2,10},{6,14},... | collective-permute-start | bytes 2654216 | tf_op jit(solution)/shard_map/ppermute | solution.py:550
  169.8 28.0 %collective-permute-start.36 = (bf16[384,1152]{1,0:T(8,128)(2,1)S(1)}, bf16[384,1152]{1,0:T(8,128)(2,1)S(1)}, u32[]{:S(2)}, u32[]{:S(2)}) collective-permute-start(bf16[384,1152]{1,0:T(8,128)(2,1)S(1)} %shard_map.256.refs_6_.refs_1_), channel_id=1, source_target_pairs={{0,8},{4,12},{8,0},{12,4},{1,9},{5,13},{9,1},{13,5},{2,10},{6,14},... | collective-permute-start | bytes 2654216 | tf_op jit(solution)/shard_map/ppermute | solution.py:550
  218.4 21.6 %collective-permute-start.39 = (bf16[384,1152]{1,0:T(8,128)(2,1)S(1)}, bf16[384,1152]{1,0:T(8,128)(2,1)S(1)}, u32[]{:S(2)}, u32[]{:S(2)}) collective-permute-start(bf16[384,1152]{1,0:T(8,128)(2,1)S(1)} %shard_map.265.refs_4_.refs_2_), channel_id=1, source_target_pairs={{0,8},{4,12},{8,0},{12,4},{1,9},{5,13},{9,1},{13,5},{2,10},{6,14},... | collective-permute-start | bytes 2654216 | tf_op jit(solution)/shard_map/ppermute | solution.py:550
  243.3 22.1 %collective-permute-start.44 = (bf16[384,1152]{1,0:T(8,128)(2,1)S(1)}, bf16[384,1152]{1,0:T(8,128)(2,1)S(1)}, u32[]{:S(2)}, u32[]{:S(2)}) collective-permute-start(bf16[384,1152]{1,0:T(8,128)(2,1)S(1)} %shard_map.268.refs_5_.refs_2_), channel_id=1, source_target_pairs={{0,8},{4,12},{8,0},{12,4},{1,9},{5,13},{9,1},{13,5},{2,10},{6,14},... | collective-permute-start | bytes 2654216 | tf_op jit(solution)/shard_map/ppermute | solution.py:550
  268.9 13.5 %collective-permute-start.43 = (bf16[192,1152]{1,0:T(8,128)(2,1)S(1)}, bf16[192,1152]{1,0:T(8,128)(2,1)S(1)}, u32[]{:S(2)}, u32[]{:S(2)}) collective-permute-start(bf16[192,1152]{1,0:T(8,128)(2,1)S(1)} %get-tuple-element.174.refs_6_), channel_id=1, source_target_pairs={{0,8},{4,12},{8,0},{12,4},{1,9},{5,13},{9,1},{13,5},{2,10},{6,14},... | collective-permute-start | bytes 1327112 | tf_op jit(solution)/shard_map/ppermute | solution.py:550
  287.2 21.9 %collective-permute-start.55 = (bf16[192,1152]{1,0:T(8,128)(2,1)S(1)}, bf16[192,1152]{1,0:T(8,128)(2,1)S(1)}, u32[]{:S(2)}, u32[]{:S(2)}) collective-permute-start(bf16[192,1152]{1,0:T(8,128)(2,1)S(1)} %get-tuple-element.180.refs_6_), channel_id=1, source_target_pairs={{0,8},{4,12},{8,0},{12,4},{1,9},{5,13},{9,1},{13,5},{2,10},{6,14},... | collective-permute-start | bytes 1327112 | tf_op jit(solution)/shard_map/ppermute | solution.py:550
  300.3 14.0 %collective-permute-start.51 = (bf16[96,1152]{1,0:T(8,128)(2,1)S(1)}, bf16[96,1152]{1,0:T(8,128)(2,1)S(1)}, u32[]{:S(2)}, u32[]{:S(2)}) collective-permute-start(bf16[96,1152]{1,0:T(8,128)(2,1)S(1)} %collective-permute-done.47.refs_2_), channel_id=1, source_target_pairs={{0,4},{4,0},{8,12},{12,8},{1,5},{5,1},{9,13},{13,9},{2,6},{6,2},{1... | collective-permute-start | bytes 663560 | tf_op jit(solution)/shard_map/ppermute | solution.py:545
  336.3 28.7 %collective-permute-start.57 = (bf16[384,1152]{1,0:T(8,128)(2,1)S(1)}, bf16[384,1152]{1,0:T(8,128)(2,1)}, u32[]{:S(2)}, u32[]{:S(2)}) collective-permute-start(bf16[384,1152]{1,0:T(8,128)(2,1)S(1)} %shard_map.284.refs_8_.refs_2_), channel_id=1, source_target_pairs={{0,8},{4,12},{8,0},{12,4},{1,9},{5,13},{9,1},{13,5},{2,10},{6,14},... | collective-permute-start | bytes 2654216 | tf_op jit(solution)/shard_map/ppermute | solution.py:550
  355.2 118.9 %all-reduce.6.cloned.1.call-start = ((), (), s32[]{:S(2)}) async-start(), calls=%async_computation.1 | async-start | bytes 4976640 | tf_op jit(solution)/shard_map/psum | solution.py:801
  374.1 290.1 %all-reduce.8.cloned.1.call-start = ((), (), s32[]{:S(2)}) async-start(), calls=%async_computation.2 | async-start | bytes 10285056 | tf_op jit(solution)/shard_map/psum | solution.py:844
  375.8 21.8 %collective-permute-start.70 = (bf16[384,1152]{1,0:T(8,128)(2,1)S(1)}, bf16[384,1152]{1,0:T(8,128)(2,1)S(1)}, u32[]{:S(2)}, u32[]{:S(2)}) collective-permute-start(bf16[384,1152]{1,0:T(8,128)(2,1)S(1)} %shard_map.289.refs_5_.refs_2_), channel_id=1, source_target_pairs={{0,8},{4,12},{8,0},{12,4},{1,9},{5,13},{9,1},{13,5},{2,10},{6,14},... | collective-permute-start | bytes 2654216 | tf_op jit(solution)/shard_map/ppermute | solution.py:550
  401.7 28.2 %collective-permute-start.69 = (bf16[192,1152]{1,0:T(8,128)(2,1)}, bf16[192,1152]{1,0:T(8,128)(2,1)}, u32[]{:S(2)}, u32[]{:S(2)}) collective-permute-start(bf16[192,1152]{1,0:T(8,128)(2,1)} %get-tuple-element.201.refs_6_), channel_id=1, source_target_pairs={{0,8},{4,12},{8,0},{12,4},{1,9},{5,13},{9,1},{13,5},{2,10},{6,14},... | collective-permute-start | bytes 1327112 | tf_op jit(solution)/shard_map/ppermute | solution.py:550
  423.0 14.2 %collective-permute-start.75 = (bf16[192,1152]{1,0:T(8,128)(2,1)}, bf16[192,1152]{1,0:T(8,128)(2,1)}, u32[]{:S(2)}, u32[]{:S(2)}) collective-permute-start(bf16[192,1152]{1,0:T(8,128)(2,1)} %get-tuple-element.204.refs_6_.refs_9_), channel_id=1, source_target_pairs={{0,8},{4,12},{8,0},{12,4},{1,9},{5,13},{9,1},{13,5},{2,10},{6,14},... | collective-permute-start | bytes 1327112 | tf_op jit(solution)/shard_map/ppermute | solution.py:550
  479.6 20.1 %collective-permute-start.77 = (bf16[192,1152]{1,0:T(8,128)(2,1)S(1)}, bf16[192,1152]{1,0:T(8,128)(2,1)S(1)}, u32[]{:S(2)}, u32[]{:S(2)}) collective-permute-start(bf16[192,1152]{1,0:T(8,128)(2,1)S(1)} %get-tuple-element.217), channel_id=1, source_target_pairs={{0,8},{4,12},{8,0},{12,4},{1,9},{5,13},{9,1},{13,5},{2,10},{6,14},... | collective-permute-start | bytes 1327112 | tf_op jit(solution)/shard_map/ppermute | solution.py:550
  504.0 34.8 %all-to-all-start = ((f32[2,192,4,288]{3,1,0,2:T(8,128)}), f32[2,192,4,288]{3,1,0,2:T(8,128)}, u32[]{:S(2)}, u32[]{:S(2)}) async-start(f32[2,192,4,288]{3,1,0,2:T(8,128)} %pad_maximum_fusion), calls=%async_computation | async-start | bytes 4718592 | tf_op jit(solution)/shard_map/all_to_all | solution.py:851
  (220 other events, 2656.3 us)
Sparse Core Ops, SparseCore 0:
  374.3 99.7 all-reduce.5
  477.2 186.9 all-reduce.7

commit v6 on v5

--- a/solution.py
+++ b/solution.py
@@ -158,8 +158,8 @@
     return run(body, [shape, shape], (*scalars, *arrays), scalars=len(scalars), flops=rows * width)
 
 
-def project(info, source, gain, bias, weight, shift, rows, save, after=()):
-    cols, width = weight.shape[0] // 3, weight.shape[1]
+def project(info, source, gain, bias, weights, shift, rows, save, after=()):
+    cols, width = weights[0].shape
     heads = cols // HD
     scalars, arrays = source.operands((0, 1))
     count, total = len(arrays), rows
@@ -170,7 +170,8 @@
         info_ref, flags = refs[0], refs[1 : 1 + len(scalars)]
         refs = refs[1 + len(scalars) :]
         read = source.reader((0, 1), flags, refs[:count])
-        g_ref, b_ref, w_ref, s_ref, x_ref, *outs, n_ref = refs[count:]
+        g_ref, b_ref, *w_refs = refs[count : count + 5]
+        s_ref, x_ref, *outs, n_ref = refs[count + 5 :]
         for index in (0, 1):
             for at in range(0, half, step):
                 value = read(index, at, step)
@@ -189,7 +190,7 @@
         normed = n_ref[...]
         for i, (out, extra) in enumerate(zip(outs[:3], (ones, mask, ones))):
             here = slice(i * cols, (i + 1) * cols)
-            value = (mm_nt(normed, w_ref[here, :]) + s_ref[:, here]).astype(BF16)
+            value = (mm_nt(normed, w_refs[i][...]) + s_ref[:, here]).astype(BF16)
             for h in range(heads):
                 out[:, h * LANES : (h + 1) * LANES] = jnp.concatenate(
                     [value[:, h * HD : (h + 1) * HD], extra], axis=1
@@ -199,7 +200,7 @@
     return run(
         body,
         [((half, width), BF16), wide, wide, wide] + ([((total, width), BF16)] if save else []),
-        (info, *scalars, *arrays, gain, bias, weight, shift),
+        (info, *scalars, *arrays, gain, bias, *weights, shift),
         scalars=1 + len(scalars),
         flops=6 * total * width * cols,
         scratch=() if save else (pltpu.VMEM((total, width), BF16),),
@@ -603,7 +604,7 @@
 def forward(source, w, info, chips, rows, save, turns):
     source = source()
     xm, q, k, v, *kept = project(
-        info, source, w["gain"][0], w["bias"][0], w["qkv"], w["qkv_shift"], rows, save,
+        info, source, w["gain"][0], w["bias"][0], w["three"], w["qkv_shift"], rows, save,
         turns.take(),
     )
     turns.first = (q,)
@@ -690,7 +691,7 @@
 
 def finish(value):
     rows, width = value.shape
-    step = 128
+    step = 272
 
     def body(value_ref, out_ref):
         out_ref[...] = value_ref[...].astype(F32).reshape(step, 1, width)
@@ -701,7 +702,7 @@
         grid=(pl.cdiv(rows, step),),
         in_specs=[pl.BlockSpec((step, width), lambda i: (i, 0))],
         out_specs=pl.BlockSpec((step, 1, width), lambda i: (i, 0, 0)),
-        compiler_params=pltpu.CompilerParams(vmem_limit_bytes=8 * 2**20),
+        compiler_params=pltpu.CompilerParams(vmem_limit_bytes=12 * 2**20),
     )(value)
 
 
@@ -732,7 +733,8 @@
     middle_part = lax.reduce_precision(small - high, 8, 7)
     thirds = jnp.concatenate([high, middle_part, small - high - middle_part], axis=0)
     features = inputs[0].reshape(images_all, length, cols).transpose(0, 2, 1)
-    qkv = jnp.concatenate([w_query[0].T, w_key[0].T, w_value[0].T], axis=0)
+    three = (w_query[0].T, w_key[0].T, w_value[0].T)
+    qkv = jnp.concatenate(three, axis=0)
     spread = []
     for n in range(images_all):
         block = features[n]
@@ -746,7 +748,7 @@
         if n == 0:
             halves, (small,) = assemble(
                 spread[0], length, sources, order, rows, small.shape[0],
-                near=(qkv,),
+                near=three,
             )
             full = {0: halves}
     turns = Turns()
@@ -759,7 +761,7 @@
     w = dict(
         gain=(small[0:1], small[1:2]), bias=(small[2:3], small[3:4]),
         out_bias=(small[4:5], small[5:6]),
-        qkv=qkv, qkv_shift=jnp.concatenate([b_query, jnp.zeros_like(b_query), b_value], axis=1),
+        three=three, qkv=qkv, qkv_shift=jnp.concatenate([b_query, jnp.zeros_like(b_query), b_value], axis=1),
         wout=w_out[0], w_up=w_up[0].T, b_up=b_up, w_down=w_down[0],
     )
     span = range(images_all)

time: 692 us -> 690 us (level)
    unnamed x327 -> x337, local copies, waits for them, and re-layouts: 44.4 us -> 43.3 us
  transfers between devices with their start and end apart: 81 -> 81, of which waited for: 34 -> 35; matrix products, arithmetic and copies ran while one was open for 4% -> 4% of each run, Pallas kernels for 24% -> 24%
where the time goes in v6:
time: 690 us; the launch traced here: 679 us
  waiting for transfers between devices  290 us (42%)
  Pallas kernels  198 us (29%)
  starting transfers between devices  67.6 us (10%)
  local copies, waits for them, and re-layouts  62.7 us (9%)
  blocking collectives  32 us (5%)
  between operations  17.3 us (3%)
  other arithmetic  12.1 us (2%)
    pallas_call x80, Pallas kernels, run(): pl.pallas_call(kernel, out_shape=[jax.ShapeDtypeStruct(shape, dtype) for...  192 us
    psum x1, waiting for transfers between devices, per_device(): g_up, g_out, g_qkv, vector = lax.psum(rest, 'dp')  118 us
    ppermute x26, waiting for transfers between devices, chip_shift(): lax.ppermute(value, 'tensor', [(i, (i + 2 * shift) % size) for i in range...  114 us
    unnamed x337, local copies, waits for them, and re-layouts  43.3 us
    ppermute x26, starting transfers between devices, chip_shift(): lax.ppermute(value, 'tensor', [(i, (i + 2 * shift) % size) for i in range...  38.1 us
    ppermute x8, waiting for transfers between devices, to_section(): return lax.ppermute(value, 'section', pairs)  30.6 us
    psum x1, blocking collectives, per_device(): g_up, g_out, g_qkv, vector = lax.psum(rest, 'dp')  20.1 us
    ppermute x8, starting transfers between devices, to_section(): return lax.ppermute(value, 'section', pairs)  17.2 us
  transfers between devices with their start and end apart: 81, of which 35 were waited for; matrix products, arithmetic and copies ran while one was open for 4% of the time, Pallas kernels for 24%

profile of v6, /device:TPU:0, one launch (start us, length us, event | category | flops | bytes accessed | tf_op | source)
XLA Modules:
  0.0 679.2 jit_solution(9601432753234688738)
XLA Ops:
  13.4 11.7 %collective-permute-done.refs_3_ = bf16[288,792]{1,0:T(8,128)(2,1)S(1)} collective-permute-done((bf16[288,792]{1,0:T(8,128)(2,1)S(1)}, bf16[288,792]{1,0:T(8,128)(2,1)S(1)}, u32[]{:S(2)}, u32[]{:S(2)}) %collective-permute-start) | collective-permute-done | bytes 456224 | tf_op jit(solution)/shard_map/ppermute | solution.py:551
  50.6 4.9 shard_map.235
  61.2 8.3 %collective-permute-done.4.refs_2_ = bf16[384,1152]{1,0:T(8,128)(2,1)S(1)} collective-permute-done((bf16[384,1152]{1,0:T(8,128)(2,1)S(1)}, bf16[384,1152]{1,0:T(8,128)(2,1)S(1)}, u32[]{:S(2)}, u32[]{:S(2)}) %collective-permute-start.4) | collective-permute-done | bytes 884768 | tf_op jit(solution)/shard_map/ppermute | solution.py:551
  80.4 13.6 %collective-permute-done.12.refs_2_ = bf16[384,1152]{1,0:T(8,128)(2,1)S(1)} collective-permute-done((bf16[384,1152]{1,0:T(8,128)(2,1)S(1)}, bf16[384,1152]{1,0:T(8,128)(2,1)S(1)}, u32[]{:S(2)}, u32[]{:S(2)}) %collective-permute-start.12) | collective-permute-done | bytes 884768 | tf_op jit(solution)/shard_map/ppermute | solution.py:551
  143.8 5.6 shard_map.249
  158.3 5.0 shard_map.253
  170.9 8.3 %collective-permute-done.25.refs_2_ = bf16[384,1152]{1,0:T(8,128)(2,1)S(1)} collective-permute-done((bf16[384,1152]{1,0:T(8,128)(2,1)S(1)}, bf16[384,1152]{1,0:T(8,128)(2,1)S(1)}, u32[]{:S(2)}, u32[]{:S(2)}) %collective-permute-start.25) | collective-permute-done | bytes 884768 | tf_op jit(solution)/shard_map/ppermute | solution.py:551
  188.6 9.2 %collective-permute-done.36.refs_2_ = bf16[384,1152]{1,0:T(8,128)(2,1)S(1)} collective-permute-done((bf16[384,1152]{1,0:T(8,128)(2,1)S(1)}, bf16[384,1152]{1,0:T(8,128)(2,1)S(1)}, u32[]{:S(2)}, u32[]{:S(2)}) %collective-permute-start.36) | collective-permute-done | bytes 884768 | tf_op jit(solution)/shard_map/ppermute | solution.py:551
  222.1 17.0 %collective-permute-done.39.refs_3_ = bf16[384,1152]{1,0:T(8,128)(2,1)S(1)} collective-permute-done((bf16[384,1152]{1,0:T(8,128)(2,1)S(1)}, bf16[384,1152]{1,0:T(8,128)(2,1)S(1)}, u32[]{:S(2)}, u32[]{:S(2)}) %collective-permute-start.39) | collective-permute-done | bytes 884768 | tf_op jit(solution)/shard_map/ppermute | solution.py:551
  244.9 7.2 %shard_map.270.refs_0_ = bf16[768,864]{1,0:T(8,128)(2,1)S(1)} custom-call(bf16[384,1152]{1,0:T(8,128)(2,1)S(1)} %get-tuple-element.170.refs_0_, bf16[384,1152]{1,0:T(8,128)(2,1)S(1)} %collective-permute-done.41.refs_1_, bf16[288,1152]{1,0:T(8,128)(2,1)S(1)} %bitcast.109, bf16[768,512]{1,0:T(8,128)(2,1)S(1)} %copy-done.121, bf16[768,512]{1,0:T(8,128)(2,1)S(1)} %copy-done.124, ...), custom_call_target="tpu_custom_call" | custom-call | flops 49413095424 | bytes 6144000 | tf_op jit(solution)/shard_map/pallas_call | solution.py:36
  255.9 8.8 %collective-permute-done.44.refs_3_ = bf16[384,1152]{1,0:T(8,128)(2,1)S(1)} collective-permute-done((bf16[384,1152]{1,0:T(8,128)(2,1)S(1)}, bf16[384,1152]{1,0:T(8,128)(2,1)S(1)}, u32[]{:S(2)}, u32[]{:S(2)}) %collective-permute-start.44) | collective-permute-done | bytes 884768 | tf_op jit(solution)/shard_map/ppermute | solution.py:551
  270.7 7.2 %shard_map.275.refs_0_ = bf16[768,864]{1,0:T(8,128)(2,1)S(1)} custom-call(bf16[384,1152]{1,0:T(8,128)(2,1)S(1)} %get-tuple-element.176.refs_0_, bf16[384,1152]{1,0:T(8,128)(2,1)S(1)} %collective-permute-done.45.refs_1_, bf16[288,1152]{1,0:T(8,128)(2,1)S(1)} %bitcast.110, bf16[768,512]{1,0:T(8,128)(2,1)S(1)} %copy-done.130, bf16[768,512]{1,0:T(8,128)(2,1)S(1)} %copy-done.133, ...), custom_call_target="tpu_custom_call" | custom-call | flops 49413095424 | bytes 6144000 | tf_op jit(solution)/shard_map/pallas_call | solution.py:36
  288.1 6.0 collective-permute-done.48.refs_3_
  314.0 6.8 collective-permute-done.59.refs_3_
  337.1 7.2 %shard_map.287.refs_4_ = bf16[1076,1152]{1,0:T(8,128)(2,1)} custom-call(bf16[384,1076]{1,0:T(8,128)(2,1)S(1)} %get-tuple-element.193.refs_0_, bf16[384,1152]{1,0:T(8,128)(2,1)S(1)} %get-tuple-element.183.refs_0_.refs_1_, bf16[384,1076]{1,0:T(8,128)(2,1)S(1)} %get-tuple-element.194.refs_2_, bf16[384,1152]{1,0:T(8,128)(2,1)S(1)} %get-tuple-element.185.refs_0_.refs_3_, ...), custom_call_target="tpu_custom_call" | custom-call | flops 53310652416 | bytes 9323520 | tf_op jit(solution)/shard_map/pallas_call | solution.py:36
  379.8 8.6 %shard_map.291.refs_0_ = bf16[768,864]{1,0:T(8,128)(2,1)S(1)} custom-call(bf16[384,1152]{1,0:T(8,128)(2,1)} %get-tuple-element.199.refs_0_.refs_1_, bf16[384,1152]{1,0:T(8,128)(2,1)} %collective-permute-done.67.refs_1_.refs_3_, bf16[288,1152]{1,0:T(8,128)(2,1)S(1)} %bitcast.111, bf16[768,512]{1,0:T(8,128)(2,1)S(1)} %copy-done.122, ...), custom_call_target="tpu_custom_call" | custom-call | flops 49413095424 | bytes 6144000 | tf_op jit(solution)/shard_map/pallas_call | solution.py:36
  403.0 7.2 %shard_map.296.refs_0_.refs_2_ = bf16[768,864]{1,0:T(8,128)(2,1)S(1)} custom-call(bf16[384,1152]{1,0:T(8,128)(2,1)S(1)} %get-tuple-element.202.refs_0_.refs_5_, bf16[384,1152]{1,0:T(8,128)(2,1)S(1)} %collective-permute-done.71.refs_1_.refs_7_, bf16[288,1152]{1,0:T(8,128)(2,1)S(1)} %bitcast.112, bf16[768,512]{1,0:T(8,128)(2,1)S(1)} %copy-done.131, ...), custom_call_target="tpu_custom_call" | custom-call | flops 49413095424 | bytes 6144000 | tf_op jit(solution)/shard_map/pallas_call | solution.py:36
  423.6 5.7 shard_map.306.refs_0_
  443.1 11.8 %psum.42 = bf16[6,1152]{1,0:T(8,128)(2,1)S(1)} all-reduce(f32[6,1152]{1,0:T(8,128)S(1)} %add.99), channel_id=1, replica_groups=mesh['section'=2,'tensor'=4,'dp'=4] {'tensor'}, use_global_device_ids=true, to_apply=%region_0.1 | all-reduce | flops 6912 | bytes 41472 | tf_op jit(solution)/shard_map/psum | solution.py:833
  457.2 16.2 %all-reduce.6.cloned.1.call-done.refs_4_.value_ref = bf16[1076,1152]{1,0:T(8,128)(2,1)} async-done(((bf16[1076,1152]{1,0:T(8,128)(2,1)}), bf16[1076,1152]{1,0:T(8,128)(2,1)}) %all-reduce.6.cloned.1.call-update) | async-done | bytes 2479120 | tf_op jit(solution)/shard_map/psum | solution.py:803
  479.9 10.3 %collective-permute-done.74.refs_2_ = bf16[192,1152]{1,0:T(8,128)(2,1)S(1)} collective-permute-done((bf16[192,1152]{1,0:T(8,128)(2,1)S(1)}, bf16[192,1152]{1,0:T(8,128)(2,1)S(1)}, u32[]{:S(2)}, u32[]{:S(2)}) %collective-permute-start.74) | collective-permute-done | bytes 442400 | tf_op jit(solution)/shard_map/ppermute | solution.py:551
  491.1 7.8 %collective-permute-done.77.refs_2_ = bf16[192,1152]{1,0:T(8,128)(2,1)S(1)} collective-permute-done((bf16[192,1152]{1,0:T(8,128)(2,1)S(1)}, bf16[192,1152]{1,0:T(8,128)(2,1)S(1)}, u32[]{:S(2)}, u32[]{:S(2)}) %collective-permute-start.77) | collective-permute-done | bytes 442400 | tf_op jit(solution)/shard_map/ppermute | solution.py:551
  511.0 20.1 %psum.44 = bf16[16,1152]{1,0:T(8,128)(2,1)S(1)} all-reduce(bf16[16,1152]{1,0:T(8,128)(2,1)S(1)} %copy-done.163), channel_id=1, replica_groups=mesh['section'=2,'tensor'=4,'dp'=4] {'dp'}, use_global_device_ids=true, to_apply=%region_8.9 | all-reduce | flops 18432 | bytes 73728 | tf_op jit(solution)/shard_map/psum | solution.py:846
  545.3 118.3 %all-reduce.8.cloned.1.call-done = (bf16[864,1152]{1,0:T(8,128)(2,1)}, bf16[1,288,1152]{2,1,0:T(8,128)(2,1)}, bf16[1076,1152]{1,0:T(8,128)(2,1)}) async-done(((bf16[864,1152]{1,0:T(8,128)(2,1)}, bf16[1,288,1152]{2,1,0:T(8,128)(2,1)}, bf16[1076,1152]{1,0:T(8,128)(2,1)}), (bf16[864,1152]{1,0:T(8,128)(2,1)}, bf16[1,288,1152]{2,1,0:T(8,128)(2,1)}, bf16[1076,1152]{1,0:T(8,128)(2,1)})) %all-reduce.8.cloned.1.call-update) | async-done | bytes 5133328 | tf_op jit(solution)/shard_map/psum | solution.py:846
  (617 shorter events, 329.1 us)
Async XLA Ops:
  10.4 14.8 %collective-permute-start = (bf16[288,792]{1,0:T(8,128)(2,1)S(1)}, bf16[288,792]{1,0:T(8,128)(2,1)S(1)}, u32[]{:S(2)}, u32[]{:S(2)}) collective-permute-start(bf16[288,792]{1,0:T(8,128)(2,1)S(1)} %fusion.1.refs_2_), channel_id=1, source_target_pairs={{0,8},{4,12},{8,0},{12,4},{1,9},{5,13},{9,1},{13,5},{2,10},{6,14},... | collective-permute-start | bytes 1368584 | tf_op jit(solution)/shard_map/ppermute | solution.py:551
  13.4 13.9 %collective-permute-start.1 = (bf16[288,792]{1,0:T(8,128)(2,1)S(1)}, bf16[288,792]{1,0:T(8,128)(2,1)S(1)}, u32[]{:S(2)}, u32[]{:S(2)}) collective-permute-start(bf16[288,792]{1,0:T(8,128)(2,1)S(1)} %fusion.1.refs_2_), channel_id=1, source_target_pairs={{0,4},{4,0},{8,12},{12,8},{1,5},{5,1},{9,13},{13,9},{2,6},{6,2},{1... | collective-permute-start | bytes 1368584 | tf_op jit(solution)/shard_map/ppermute | solution.py:546
  31.8 17.4 %collective-permute-start.6 = (bf16[288,729]{1,0:T(8,128)(2,1)}, bf16[288,729]{1,0:T(8,128)(2,1)S(1)}, u32[]{:S(2)}, u32[]{:S(2)}) collective-permute-start(bf16[288,729]{1,0:T(8,128)(2,1)} %shard_map.233.refs_2_), channel_id=1, source_target_pairs={{0,4},{4,0},{8,12},{12,8},{1,5},{5,1},{9,13},{13,9},{2,6},{6,2},{1... | collective-permute-start | bytes 1259720 | tf_op jit(solution)/shard_map/ppermute | solution.py:546
  47.4 22.1 %collective-permute-start.4 = (bf16[384,1152]{1,0:T(8,128)(2,1)S(1)}, bf16[384,1152]{1,0:T(8,128)(2,1)S(1)}, u32[]{:S(2)}, u32[]{:S(2)}) collective-permute-start(bf16[384,1152]{1,0:T(8,128)(2,1)S(1)} %shard_map.232.refs_6_.refs_9_.refs_1_), channel_id=1, source_target_pairs={{0,8},{4,12},{8,0},{12,4},{1,9},{5,13},{9,1},{13,5},{2,10},{6,14},... | collective-permute-start | bytes 2654216 | tf_op jit(solution)/shard_map/ppermute | solution.py:551
  71.9 22.1 %collective-permute-start.12 = (bf16[384,1152]{1,0:T(8,128)(2,1)S(1)}, bf16[384,1152]{1,0:T(8,128)(2,1)S(1)}, u32[]{:S(2)}, u32[]{:S(2)}) collective-permute-start(bf16[384,1152]{1,0:T(8,128)(2,1)S(1)} %shard_map.238.refs_6_.refs_1_), channel_id=1, source_target_pairs={{0,8},{4,12},{8,0},{12,4},{1,9},{5,13},{9,1},{13,5},{2,10},{6,14},... | collective-permute-start | bytes 2654216 | tf_op jit(solution)/shard_map/ppermute | solution.py:551
  104.5 19.6 %collective-permute-start.23 = (bf16[192,1152]{1,0:T(8,128)(2,1)S(1)}, bf16[192,1152]{1,0:T(8,128)(2,1)S(1)}, u32[]{:S(2)}, u32[]{:S(2)}) collective-permute-start(bf16[192,1152]{1,0:T(8,128)(2,1)S(1)} %get-tuple-element.144.refs_5_), channel_id=1, source_target_pairs={{0,8},{4,12},{8,0},{12,4},{1,9},{5,13},{9,1},{13,5},{2,10},{6,14},... | collective-permute-start | bytes 1327112 | tf_op jit(solution)/shard_map/ppermute | solution.py:551
  124.1 16.6 %collective-permute-start.19 = (bf16[96,1152]{1,0:T(8,128)(2,1)}, bf16[96,1152]{1,0:T(8,128)(2,1)}, u32[]{:S(2)}, u32[]{:S(2)}) collective-permute-start(bf16[96,1152]{1,0:T(8,128)(2,1)} %collective-permute-done.15.refs_3_), channel_id=1, source_target_pairs={{0,4},{4,0},{8,12},{12,8},{1,5},{5,1},{9,13},{13,9},{2,6},{6,2},{1... | collective-permute-start | bytes 663560 | tf_op jit(solution)/shard_map/ppermute | solution.py:546
  135.8 17.0 %collective-permute-start.29 = (bf16[96,1152]{1,0:T(8,128)(2,1)S(1)}, bf16[96,1152]{1,0:T(8,128)(2,1)S(1)}, u32[]{:S(2)}, u32[]{:S(2)}) collective-permute-start(bf16[96,1152]{1,0:T(8,128)(2,1)S(1)} %collective-permute-done.27.refs_4_), channel_id=1, source_target_pairs={{0,8},{4,12},{8,0},{12,4},{1,9},{5,13},{9,1},{13,5},{2,10},{6,14},... | collective-permute-start | bytes 663560 | tf_op jit(solution)/shard_map/ppermute | solution.py:551
  156.8 22.5 %collective-permute-start.25 = (bf16[384,1152]{1,0:T(8,128)(2,1)S(1)}, bf16[384,1152]{1,0:T(8,128)(2,1)S(1)}, u32[]{:S(2)}, u32[]{:S(2)}) collective-permute-start(bf16[384,1152]{1,0:T(8,128)(2,1)S(1)} %shard_map.252.refs_18_.refs_1_), channel_id=1, source_target_pairs={{0,8},{4,12},{8,0},{12,4},{1,9},{5,13},{9,1},{13,5},{2,10},{6,14},... | collective-permute-start | bytes 2654216 | tf_op jit(solution)/shard_map/ppermute | solution.py:551
  169.9 27.9 %collective-permute-start.36 = (bf16[384,1152]{1,0:T(8,128)(2,1)S(1)}, bf16[384,1152]{1,0:T(8,128)(2,1)S(1)}, u32[]{:S(2)}, u32[]{:S(2)}) collective-permute-start(bf16[384,1152]{1,0:T(8,128)(2,1)S(1)} %shard_map.256.refs_6_.refs_1_), channel_id=1, source_target_pairs={{0,8},{4,12},{8,0},{12,4},{1,9},{5,13},{9,1},{13,5},{2,10},{6,14},... | collective-permute-start | bytes 2654216 | tf_op jit(solution)/shard_map/ppermute | solution.py:551
  217.4 21.6 %collective-permute-start.39 = (bf16[384,1152]{1,0:T(8,128)(2,1)S(1)}, bf16[384,1152]{1,0:T(8,128)(2,1)S(1)}, u32[]{:S(2)}, u32[]{:S(2)}) collective-permute-start(bf16[384,1152]{1,0:T(8,128)(2,1)S(1)} %shard_map.265.refs_4_.refs_2_), channel_id=1, source_target_pairs={{0,8},{4,12},{8,0},{12,4},{1,9},{5,13},{9,1},{13,5},{2,10},{6,14},... | collective-permute-start | bytes 2654216 | tf_op jit(solution)/shard_map/ppermute | solution.py:551
  242.6 22.1 %collective-permute-start.44 = (bf16[384,1152]{1,0:T(8,128)(2,1)S(1)}, bf16[384,1152]{1,0:T(8,128)(2,1)S(1)}, u32[]{:S(2)}, u32[]{:S(2)}) collective-permute-start(bf16[384,1152]{1,0:T(8,128)(2,1)S(1)} %shard_map.268.refs_5_.refs_2_), channel_id=1, source_target_pairs={{0,8},{4,12},{8,0},{12,4},{1,9},{5,13},{9,1},{13,5},{2,10},{6,14},... | collective-permute-start | bytes 2654216 | tf_op jit(solution)/shard_map/ppermute | solution.py:551
  268.2 13.5 %collective-permute-start.43 = (bf16[192,1152]{1,0:T(8,128)(2,1)S(1)}, bf16[192,1152]{1,0:T(8,128)(2,1)S(1)}, u32[]{:S(2)}, u32[]{:S(2)}) collective-permute-start(bf16[192,1152]{1,0:T(8,128)(2,1)S(1)} %get-tuple-element.174.refs_6_), channel_id=1, source_target_pairs={{0,8},{4,12},{8,0},{12,4},{1,9},{5,13},{9,1},{13,5},{2,10},{6,14},... | collective-permute-start | bytes 1327112 | tf_op jit(solution)/shard_map/ppermute | solution.py:551
  286.6 21.9 %collective-permute-start.55 = (bf16[192,1152]{1,0:T(8,128)(2,1)S(1)}, bf16[192,1152]{1,0:T(8,128)(2,1)S(1)}, u32[]{:S(2)}, u32[]{:S(2)}) collective-permute-start(bf16[192,1152]{1,0:T(8,128)(2,1)S(1)} %get-tuple-element.180.refs_6_), channel_id=1, source_target_pairs={{0,8},{4,12},{8,0},{12,4},{1,9},{5,13},{9,1},{13,5},{2,10},{6,14},... | collective-permute-start | bytes 1327112 | tf_op jit(solution)/shard_map/ppermute | solution.py:551
  299.7 14.0 %collective-permute-start.51 = (bf16[96,1152]{1,0:T(8,128)(2,1)S(1)}, bf16[96,1152]{1,0:T(8,128)(2,1)S(1)}, u32[]{:S(2)}, u32[]{:S(2)}) collective-permute-start(bf16[96,1152]{1,0:T(8,128)(2,1)S(1)} %collective-permute-done.47.refs_2_), channel_id=1, source_target_pairs={{0,4},{4,0},{8,12},{12,8},{1,5},{5,1},{9,13},{13,9},{2,6},{6,2},{1... | collective-permute-start | bytes 663560 | tf_op jit(solution)/shard_map/ppermute | solution.py:546
  312.0 13.2 %collective-permute-start.58 = (bf16[96,1152]{1,0:T(8,128)(2,1)S(1)}, bf16[96,1152]{1,0:T(8,128)(2,1)S(1)}, u32[]{:S(2)}, u32[]{:S(2)}) collective-permute-start(bf16[96,1152]{1,0:T(8,128)(2,1)S(1)} %get-tuple-element.187.refs_4_), channel_id=1, source_target_pairs={{16,0},{17,1},{18,2},{19,3},{20,4},{21,5},{22,6},{23,7},{24,8},{25... | collective-permute-start | bytes 663560 | tf_op jit(solution)/shard_map/ppermute | solution.py:590
  335.5 28.9 %collective-permute-start.57 = (bf16[384,1152]{1,0:T(8,128)(2,1)S(1)}, bf16[384,1152]{1,0:T(8,128)(2,1)}, u32[]{:S(2)}, u32[]{:S(2)}) collective-permute-start(bf16[384,1152]{1,0:T(8,128)(2,1)S(1)} %shard_map.284.refs_8_.refs_2_), channel_id=1, source_target_pairs={{0,8},{4,12},{8,0},{12,4},{1,9},{5,13},{9,1},{13,5},{2,10},{6,14},... | collective-permute-start | bytes 2654216 | tf_op jit(solution)/shard_map/ppermute | solution.py:551
  354.5 118.9 %all-reduce.6.cloned.1.call-start = ((), (), s32[]{:S(2)}) async-start(), calls=%async_computation.1 | async-start | bytes 4976640 | tf_op jit(solution)/shard_map/psum | solution.py:803
  373.5 290.1 %all-reduce.8.cloned.1.call-start = ((), (), s32[]{:S(2)}) async-start(), calls=%async_computation.2 | async-start | bytes 10285056 | tf_op jit(solution)/shard_map/psum | solution.py:846
  375.2 21.8 %collective-permute-start.70 = (bf16[384,1152]{1,0:T(8,128)(2,1)S(1)}, bf16[384,1152]{1,0:T(8,128)(2,1)S(1)}, u32[]{:S(2)}, u32[]{:S(2)}) collective-permute-start(bf16[384,1152]{1,0:T(8,128)(2,1)S(1)} %shard_map.289.refs_5_.refs_2_), channel_id=1, source_target_pairs={{0,8},{4,12},{8,0},{12,4},{1,9},{5,13},{9,1},{13,5},{2,10},{6,14},... | collective-permute-start | bytes 2654216 | tf_op jit(solution)/shard_map/ppermute | solution.py:551
  401.1 28.2 %collective-permute-start.69 = (bf16[192,1152]{1,0:T(8,128)(2,1)}, bf16[192,1152]{1,0:T(8,128)(2,1)}, u32[]{:S(2)}, u32[]{:S(2)}) collective-permute-start(bf16[192,1152]{1,0:T(8,128)(2,1)} %get-tuple-element.201.refs_6_), channel_id=1, source_target_pairs={{0,8},{4,12},{8,0},{12,4},{1,9},{5,13},{9,1},{13,5},{2,10},{6,14},... | collective-permute-start | bytes 1327112 | tf_op jit(solution)/shard_map/ppermute | solution.py:551
  422.4 14.2 %collective-permute-start.75 = (bf16[192,1152]{1,0:T(8,128)(2,1)}, bf16[192,1152]{1,0:T(8,128)(2,1)}, u32[]{:S(2)}, u32[]{:S(2)}) collective-permute-start(bf16[192,1152]{1,0:T(8,128)(2,1)} %get-tuple-element.204.refs_6_.refs_9_), channel_id=1, source_target_pairs={{0,8},{4,12},{8,0},{12,4},{1,9},{5,13},{9,1},{13,5},{2,10},{6,14},... | collective-permute-start | bytes 1327112 | tf_op jit(solution)/shard_map/ppermute | solution.py:551
  478.8 20.1 %collective-permute-start.77 = (bf16[192,1152]{1,0:T(8,128)(2,1)S(1)}, bf16[192,1152]{1,0:T(8,128)(2,1)S(1)}, u32[]{:S(2)}, u32[]{:S(2)}) collective-permute-start(bf16[192,1152]{1,0:T(8,128)(2,1)S(1)} %get-tuple-element.217), channel_id=1, source_target_pairs={{0,8},{4,12},{8,0},{12,4},{1,9},{5,13},{9,1},{13,5},{2,10},{6,14},... | collective-permute-start | bytes 1327112 | tf_op jit(solution)/shard_map/ppermute | solution.py:551
  503.3 33.2 %all-to-all-start = ((f32[2,192,4,288]{3,1,0,2:T(8,128)}), f32[2,192,4,288]{3,1,0,2:T(8,128)}, u32[]{:S(2)}, u32[]{:S(2)}) async-start(f32[2,192,4,288]{3,1,0,2:T(8,128)} %pad_maximum_fusion), calls=%async_computation | async-start | bytes 4718592 | tf_op jit(solution)/shard_map/all_to_all | solution.py:853
  (225 other events, 2380.5 us)
Sparse Core Ops, SparseCore 0:
  373.6 99.7 all-reduce.5
  476.5 186.9 all-reduce.7
